TPU v7x, 32 devices: a whole 2x2x4 slice. The times are simulated.
32 devices in a mesh: dp: 4 (over y, x), seq: 8 (over z, core).
Axes of the slice: x: 2, y: 2, z: 4, core: 2. Of those that a mesh axis runs over, the one named last changes fastest.
Arguments:
- tokens: bfloat16 [8, 1024, 2048], P('dp', 'seq'), may hold values from -6 to 6
- lengths: int32 [8], P('dp'), may hold values from 256 to 1024, as said below
- gains: bfloat16 [2, 2048], P(None, ('dp', 'seq')), may hold values from 0.5 to 1.5
- w_query: bfloat16 [2048, 1024], P(('dp', 'seq')), may hold values from -0.125 to 0.125
- w_keyval: bfloat16 [2048, 512], P(('dp', 'seq')), may hold values from -0.125 to 0.125
- w_attn_out: bfloat16 [1024, 2048], P(('dp', 'seq')), may hold values from -0.5 to 0.5
- w_in: bfloat16 [2048, 6656], P(('dp', 'seq')), may hold values from -0.125 to 0.125
- w_dt: bfloat16 [2048, 48], P(('dp', 'seq')), may hold values from -0.125 to 0.125
- conv_params: bfloat16 [5, 3584], P(None, ('dp', 'seq')), may hold values from -0.5 to 0.5
- head_params: float32 [3, 48], replicated, may hold values from -11 to 1.5, as said below
- w_mamba_out: bfloat16 [3072, 2048], P(('dp', 'seq')), may hold values from -0.013671875 to 0.013671875
- w_gate_up: bfloat16 [2048, 8192], P(('dp', 'seq')), may hold values from -0.125 to 0.125
- w_down: bfloat16 [4096, 2048], P(('dp', 'seq')), may hold values from -0.09375 to 0.09375
- cotangent: bfloat16 [8, 1024, 2048], P('dp', 'seq'), may hold values from -6 to 6
Outputs:
- mixed: bfloat16 [8, 1024, 2048], P('dp', 'seq')
- grad_tokens: bfloat16 [8, 1024, 2048], P('dp', 'seq')
- grad_gains: float32 [2, 2048], P(None, ('dp', 'seq'))
- grad_query: float32 [2048, 1024], P(('dp', 'seq'))
- grad_keyval: float32 [2048, 512], P(('dp', 'seq'))
- grad_attn_out: float32 [1024, 2048], P(('dp', 'seq'))
- grad_in: float32 [2048, 6656], P(('dp', 'seq'))
- grad_dt: float32 [2048, 48], P(('dp', 'seq'))
- grad_conv: float32 [5, 3584], P(None, ('dp', 'seq'))
- grad_head: float32 [2, 48], replicated
- grad_skip: float32 [48], replicated
- grad_mamba_out: float32 [3072, 2048], P(('dp', 'seq'))
- grad_gate_up: float32 [2048, 8192], P(('dp', 'seq'))
- grad_down: float32 [4096, 2048], P(('dp', 'seq'))
Inputs may be any that keep to these rules, and one draw needn't show every extreme that they name: `lengths`: of the 2 sequences of each index of dp, one, drawn from the seed, has all 1024 positions valid. `head_params`: row 0 is the time-step bias, row 1 the logarithm of each head's decay rate, row 2 the skip coefficient.
All inputs are finite; a program needn't handle non-finite values.
Results may differ from a plain program's by a relative error of at most 0.015.
Values may be sent and summed in bfloat16 or wider, within the bound.
No kernel may reach another device: no remote copies, remote signals or barrier semaphores. Data moves between devices by JAX's collectives and lax.ppermute only.
A program may use at most 640 MiB of HBM per device.

v0:
```python
import math

import jax
import jax.numpy as jnp
from jax import lax
from jax.sharding import PartitionSpec as P

HQ = 8
KV = 2
HD = 128
MH = 48
MP = 64
NS = 256
KW = 4


epsilon = 1e-05
rope_base = 100000000000.0
neg_big = -1e30
highest = lax.Precision.HIGHEST


def passed_along(block, axis, distance):
    devices = range(lax.axis_size(axis))
    route = [(i - distance, i) for i in devices if i - distance in devices]
    return lax.ppermute(block, axis, route)


def entering(array, axis, combine, identity, reverse):
    peers, here = (lax.axis_size(axis), lax.axis_index(axis))
    everything = jax.tree.map(
        lambda part, kind: lax.all_gather(part.astype(kind), axis),
        array,
        (jnp.bfloat16, jnp.bfloat16),
    )
    start = jax.tree.map(
        lambda part, zero: jnp.broadcast_to(jnp.asarray(zero, part.dtype), part.shape),
        array,
        identity,
    )

    def lap(k, before):
        at = peers - 1 - k if reverse else k
        reached = at > here if reverse else at < here
        new = combine(
            before, jax.tree.map(lambda part, own: part[at].astype(own.dtype), everything, array)
        )
        return jax.tree.map(lambda a, b: jnp.where(reached, a, b), new, before)

    return lax.fori_loop(0, peers, lap, start)


def rms_norm(values, gain):
    return values * lax.rsqrt(jnp.mean(values * values, -1, keepdims=True) + epsilon) * gain


def rope_tables(positions, head_size):
    half = head_size // 2
    freq = jnp.exp(jnp.arange(half, dtype=jnp.float32) * (-2.0 * math.log(rope_base) / head_size))
    angle = positions.astype(jnp.float32)[:, None] * freq[None, :]
    return (
        jnp.concatenate([jnp.cos(angle), jnp.cos(angle)], -1),
        jnp.concatenate([jnp.sin(angle), jnp.sin(angle)], -1),
    )


def rotate(values, cosine, sine):
    half = values.shape[-1] // 2
    turned = jnp.concatenate([-values[..., half:], values[..., :half]], -1)
    return values * cosine + turned * sine


def rotate_back(grads, cosine, sine):
    half = grads.shape[-1] // 2
    scaled = grads * sine
    return grads * cosine + jnp.concatenate([scaled[..., half:], -scaled[..., :half]], -1)


def conv_apply(extended, conv_params):
    width = conv_params.shape[0] - 1
    count = extended.shape[-2] - width + 1
    total = conv_params[width]
    for offset in range(width):
        total = total + conv_params[offset] * lax.slice_in_dim(
            extended, offset, offset + count, axis=extended.ndim - 2
        )
    return jax.nn.silu(total)


def ssd_span(inner_x, bmat, cmat, step, decay_log, state):
    cum = jnp.cumsum(decay_log, axis=0)
    index = jnp.arange(cum.shape[0])
    lower = index[:, None] >= index[None, :]
    diff = cum.T[:, :, None] - cum.T[:, None, :]
    decay = jnp.exp(jnp.where(lower[None], diff, neg_big))
    inner = jnp.dot(cmat, bmat.T, precision=highest)
    mixing = decay * inner[None] * step.T[:, None, :]
    intra = jnp.einsum("hts,shp->thp", mixing, inner_x, precision=highest)
    carried = jnp.einsum("tn,hpn->thp", cmat, state, precision=highest) * jnp.exp(cum)[:, :, None]
    tail = jnp.exp(cum[-1][None, :] - cum) * step
    new_state = jnp.exp(cum[-1])[:, None, None] * state + jnp.einsum(
        "sh,shp,sn->hpn", tail, inner_x, bmat, precision=highest
    )
    return (intra + carried, new_state)


def mamba_core(cvals, dt_raw, head_params, state):
    heads, head_size, nstate = state.shape
    inner = heads * head_size
    count = cvals.shape[0]
    inner_x = cvals[:, :inner].reshape(count, heads, head_size)
    bmat = cvals[:, inner : inner + nstate]
    cmat = cvals[:, inner + nstate :]
    step = jax.nn.softplus(dt_raw + head_params[0])
    decay_log = -jnp.exp(head_params[1]) * step
    mixed, new_state = ssd_span(inner_x, bmat, cmat, step, decay_log, state)
    out = mixed + head_params[2][None, :, None] * inner_x
    return (out.reshape(count, inner), new_state)


def dot_first(left, right):
    return lax.dot_general(
        left, right, (((0,), (0,)), ((), ())), preferred_element_type=jnp.float32
    )


def dot_last(left, right):
    return lax.dot_general(
        left, right, (((1,), (1,)), ((), ())), preferred_element_type=jnp.float32
    )


def chain_combine(earlier, later):
    return (earlier[0] * later[0], later[1] + later[0][:, :, None, None] * earlier[1])


def attend_block(qblock, keys, values, qpos, length, scale):
    scores = dot_last(qblock, keys) * scale
    kpos = jnp.arange(keys.shape[0], dtype=jnp.int32)
    allowed = (kpos[None, :] <= qpos[:, None]) & (kpos[None, :] < length)
    scores = jnp.where(allowed, scores, neg_big)
    top = jnp.max(scores, -1, keepdims=True)
    expo = jnp.exp(scores - top)
    total = jnp.sum(expo, -1, keepdims=True)
    prob = (expo / total).astype(jnp.bfloat16)
    out = jnp.dot(prob, values, preferred_element_type=jnp.float32)
    return (out, (top + jnp.log(total))[:, 0])


def attend_fore(qrows, qpos, keys, values, length, scale, block):
    count = qrows.shape[0] // block

    def one_block(inputs):
        return attend_block(inputs[0], keys, values, inputs[1], length, scale)

    outs, logs = lax.map(one_block, (qrows.reshape(count, block, -1), qpos.reshape(count, block)))
    return (outs.reshape(qrows.shape[0], -1), logs.reshape(-1))


def attend_back(qrows, qpos, keys, values, length, grad_out, log_total, scale, block):
    count = qrows.shape[0] // block
    kpos = jnp.arange(keys.shape[0], dtype=jnp.int32)

    def one_block(carry, inputs):
        grad_keys, grad_values = carry
        qblock, pblock, gblock, lblock = inputs
        scores = dot_last(qblock, keys) * scale
        allowed = (kpos[None, :] <= pblock[:, None]) & (kpos[None, :] < length)
        scores = jnp.where(allowed, scores, neg_big)
        prob = jnp.exp(scores - lblock[:, None])
        grad_prob = dot_last(gblock, values)
        centre = jnp.sum(prob * grad_prob, -1, keepdims=True)
        grad_score = (prob * (grad_prob - centre)).astype(jnp.bfloat16)
        grad_query = jnp.dot(grad_score, keys, preferred_element_type=jnp.float32) * scale
        grad_keys = grad_keys + dot_first(grad_score, qblock) * scale
        grad_values = grad_values + dot_first(prob.astype(jnp.bfloat16), gblock)
        return ((grad_keys, grad_values), grad_query)

    zero_keys = jnp.zeros(keys.shape, jnp.float32)
    inputs = (
        qrows.reshape(count, block, -1),
        qpos.reshape(count, block),
        grad_out.reshape(count, block, -1),
        log_total.reshape(count, block),
    )
    (grad_keys, grad_values), grad_query = lax.scan(one_block, (zero_keys, zero_keys), inputs)
    return (grad_query.reshape(qrows.shape[0], -1), grad_keys, grad_values)


def body(
    tokens,
    lengths,
    gains,
    w_query,
    w_keyval,
    w_attn_out,
    w_in,
    w_dt,
    conv_params,
    head_params,
    w_mamba_out,
    w_gate_up,
    w_down,
    cotangent,
):
    seq_count, rows_seq, width = tokens.shape
    total_rows = seq_count * rows_seq
    groups = HQ // KV
    seq_len = rows_seq * lax.axis_size("seq")
    inner = MH * MP
    scale = 1.0 / math.sqrt(HD)
    block = math.gcd(512, groups * rows_seq)
    shards = (
        gains,
        w_query,
        w_keyval,
        w_attn_out,
        w_in,
        w_dt,
        conv_params,
        w_mamba_out,
        w_gate_up,
        w_down,
    )
    fore = (
        lax.all_gather(shards[0], ("dp", "seq"), axis=1, tiled=True),
        lax.all_gather(shards[1], ("dp", "seq"), axis=0, tiled=True),
        lax.all_gather(shards[2], ("dp", "seq"), axis=0, tiled=True),
        lax.all_gather(shards[3], ("dp", "seq"), axis=0, tiled=True),
        lax.all_gather(shards[4], ("dp", "seq"), axis=0, tiled=True),
        lax.all_gather(shards[5], ("dp", "seq"), axis=0, tiled=True),
        lax.all_gather(shards[6], ("dp", "seq"), axis=1, tiled=True),
        lax.all_gather(shards[7], ("dp", "seq"), axis=0, tiled=True),
        lax.all_gather(shards[8], ("dp", "seq"), axis=0, tiled=True),
        lax.all_gather(shards[9], ("dp", "seq"), axis=0, tiled=True),
    )
    positions = lax.axis_index("seq") * rows_seq + jnp.arange(rows_seq, dtype=jnp.int32)
    valid = (positions[None, :] < lengths[:, None]).astype(jnp.float32)
    valid_rows = valid.reshape(total_rows, 1)
    cosine, sine = rope_tables(positions, HD)
    cos_heads = cosine[:, None, :]
    sin_heads = sine[:, None, :]
    qpos_rows = jnp.tile(positions, groups)
    token_f = tokens.astype(jnp.float32).reshape(total_rows, width)
    gain_all = fore[0].astype(jnp.float32)
    norm1_b = rms_norm(token_f, gain_all[0]).astype(jnp.bfloat16)
    q_raw = jnp.dot(norm1_b, fore[1], preferred_element_type=jnp.float32).reshape(
        seq_count, rows_seq, HQ, HD
    )
    query_rot = rotate(q_raw, cos_heads, sin_heads).astype(jnp.bfloat16)
    kv_raw = jnp.dot(norm1_b, fore[2], preferred_element_type=jnp.float32).reshape(
        seq_count, rows_seq, 2, KV, HD
    )
    keys_rot = rotate(kv_raw[:, :, 0], cos_heads, sin_heads)
    kv_local = (
        jnp.stack([keys_rot, kv_raw[:, :, 1]], 2)
        .astype(jnp.bfloat16)
        .reshape(seq_count, rows_seq, 2 * KV * HD)
    )
    kv_fore = lax.all_gather(kv_local, "seq", axis=1, tiled=True)
    query_group = (
        query_rot.reshape(seq_count, rows_seq, KV, groups, HD)
        .transpose(0, 2, 3, 1, 4)
        .reshape(seq_count, KV, groups * rows_seq, HD)
    )

    def split_keys(gathered):
        parts = gathered.reshape(seq_count, seq_len, 2, KV, HD).transpose(0, 2, 3, 1, 4)
        return (parts[:, 0], parts[:, 1])

    keys_all, values_all = split_keys(kv_fore)
    fore_heads = jax.vmap(
        lambda qrows, keys, values, length: attend_fore(
            qrows, qpos_rows, keys, values, length, scale, block
        ),
        in_axes=(0, 0, 0, None),
    )
    attn_group, log_total = lax.map(
        lambda item: fore_heads(*item), (query_group, keys_all, values_all, lengths)
    )
    attn_rows = (
        attn_group.astype(jnp.bfloat16)
        .reshape(seq_count, KV, groups, rows_seq, HD)
        .transpose(0, 3, 1, 2, 4)
        .reshape(total_rows, HQ * HD)
    )
    attn_part = jnp.dot(attn_rows, fore[3], preferred_element_type=jnp.float32)
    proj = jnp.dot(norm1_b, fore[4], preferred_element_type=jnp.float32)
    gate_z = proj[:, :inner]
    xbc = proj[:, inner:].reshape(seq_count, rows_seq, -1)
    dt_raw = jnp.dot(norm1_b, fore[5], preferred_element_type=jnp.float32).reshape(
        seq_count, rows_seq, MH
    )
    rim = xbc[:, rows_seq - (KW - 1) :, :]
    before = passed_along(rim.astype(jnp.bfloat16), "seq", 1).astype(rim.dtype)
    extended = jnp.concatenate([before, xbc], 1)
    conv_f = fore[6].astype(jnp.float32)
    cvals = conv_apply(extended, conv_f)
    step_all = jax.nn.softplus(dt_raw + head_params[0])
    cum_all = jnp.cumsum(-jnp.exp(head_params[1]) * step_all, axis=1)
    decay = jnp.exp(cum_all[:, -1, :])
    core_batch = jax.vmap(mamba_core, in_axes=(0, 0, None, 0))
    zero_state = jnp.zeros((seq_count, MH, MP, NS), jnp.float32)
    y_zero, state_local = core_batch(cvals, dt_raw, head_params, zero_state)
    identity = (jnp.ones((seq_count, MH), jnp.float32), zero_state)
    _, state_in = entering((decay, state_local), "seq", chain_combine, identity, False)
    cmat = cvals[:, :, inner + NS :]
    carried = (
        jnp.einsum("stn,shpn->sthp", cmat, state_in, precision=highest)
        * jnp.exp(cum_all)[..., None]
    )
    ssm_out = (y_zero + carried.reshape(seq_count, rows_seq, inner)).reshape(total_rows, inner)
    silu_z = jax.nn.silu(gate_z)
    gated = (ssm_out * silu_z).astype(jnp.bfloat16)
    mamba_part = jnp.dot(gated, fore[7], preferred_element_type=jnp.float32)
    hidden = token_f + valid_rows * (attn_part + mamba_part)
    norm2_f, norm2_pull = jax.vjp(rms_norm, hidden, gain_all[1])
    norm2_b = norm2_f.astype(jnp.bfloat16)
    gate_up = jnp.dot(norm2_b, fore[8], preferred_element_type=jnp.float32)
    ffn_width = gate_up.shape[1] // 2
    gate = gate_up[:, :ffn_width]
    upper = gate_up[:, ffn_width:]
    act = (jax.nn.silu(gate) * upper).astype(jnp.bfloat16)
    ffn_part = jnp.dot(act, fore[9], preferred_element_type=jnp.float32)
    mixed = (
        (hidden + valid_rows * ffn_part).astype(jnp.bfloat16).reshape(seq_count, rows_seq, width)
    )
    back = (
        lax.all_gather(shards[0], ("dp", "seq"), axis=1, tiled=True),
        lax.all_gather(shards[1], ("dp", "seq"), axis=0, tiled=True),
        lax.all_gather(shards[2], ("dp", "seq"), axis=0, tiled=True),
        lax.all_gather(shards[3], ("dp", "seq"), axis=0, tiled=True),
        lax.all_gather(shards[4], ("dp", "seq"), axis=0, tiled=True),
        lax.all_gather(shards[5], ("dp", "seq"), axis=0, tiled=True),
        lax.all_gather(shards[6], ("dp", "seq"), axis=1, tiled=True),
        lax.all_gather(shards[7], ("dp", "seq"), axis=0, tiled=True),
        lax.all_gather(shards[8], ("dp", "seq"), axis=0, tiled=True),
        lax.all_gather(shards[9], ("dp", "seq"), axis=0, tiled=True),
    )
    kv_back = lax.all_gather(kv_local, "seq", axis=1, tiled=True)
    cot = cotangent.astype(jnp.float32).reshape(total_rows, width)
    grad_ffn = (valid_rows * cot).astype(jnp.bfloat16)
    grad_act = dot_last(grad_ffn, back[9])
    grad_down = dot_first(act, grad_ffn)
    sig_gate = jax.nn.sigmoid(gate)
    grad_gate = grad_act * upper * (sig_gate * (1.0 + gate * (1.0 - sig_gate)))
    grad_upper = grad_act * gate * sig_gate
    grad_gu = jnp.concatenate([grad_gate, grad_upper], 1).astype(jnp.bfloat16)
    grad_gate_up = dot_first(norm2_b, grad_gu)
    grad_norm2 = dot_last(grad_gu, back[8])
    grad_hidden_norm, grad_gain2 = norm2_pull(grad_norm2)
    grad_hidden = cot + grad_hidden_norm
    ffn_shards = (
        lax.psum_scatter(grad_gate_up, ("dp", "seq"), scatter_dimension=0, tiled=True),
        lax.psum_scatter(grad_down, ("dp", "seq"), scatter_dimension=0, tiled=True),
    )
    grad_mix = (valid_rows * grad_hidden).astype(jnp.bfloat16)
    grad_attn_out = dot_first(attn_rows, grad_mix)
    grad_o = dot_last(grad_mix, back[3]).astype(jnp.bfloat16)
    grad_mamba_out = dot_first(gated, grad_mix)
    grad_gated = dot_last(grad_mix, back[7])
    sig_z = jax.nn.sigmoid(gate_z)
    grad_y = grad_gated * silu_z
    grad_z = grad_gated * ssm_out * (sig_z * (1.0 + gate_z * (1.0 - sig_z)))
    grad_y3 = grad_y.reshape(seq_count, rows_seq, inner)
    local_term = jnp.einsum(
        "sth,sthp,stn->shpn",
        jnp.exp(cum_all),
        grad_y3.reshape(seq_count, rows_seq, MH, MP),
        cmat,
        precision=highest,
    )
    _, later = entering((decay, local_term), "seq", chain_combine, identity, True)
    _, core_pull = jax.vjp(core_batch, cvals, dt_raw, head_params, state_in)
    grad_cvals, grad_dt_raw, grad_head_local, _ = core_pull((grad_y3, later))
    _, conv_pull = jax.vjp(conv_apply, extended, conv_f)
    grad_ext, grad_conv = conv_pull(grad_cvals)
    from_next = passed_along(grad_ext[:, : KW - 1, :].astype(jnp.bfloat16), "seq", -1).astype(
        jnp.float32
    )
    grad_xbc = grad_ext[:, KW - 1 :, :]
    grad_xbc = grad_xbc.at[:, rows_seq - (KW - 1) :, :].add(from_next)
    grad_proj = jnp.concatenate([grad_z, grad_xbc.reshape(total_rows, -1)], 1).astype(jnp.bfloat16)
    grad_dt_b = grad_dt_raw.reshape(total_rows, MH).astype(jnp.bfloat16)
    keys_back, values_back = split_keys(kv_back)
    grad_o_group = (
        grad_o.reshape(seq_count, rows_seq, KV, groups, HD)
        .transpose(0, 2, 3, 1, 4)
        .reshape(seq_count, KV, groups * rows_seq, HD)
    )
    back_heads = jax.vmap(
        lambda qrows, keys, values, length, gout, logs: attend_back(
            qrows, qpos_rows, keys, values, length, gout, logs, scale, block
        ),
        in_axes=(0, 0, 0, None, 0, 0),
    )
    grad_q_group, grad_keys, grad_values = lax.map(
        lambda item: back_heads(*item),
        (query_group, keys_back, values_back, lengths, grad_o_group, log_total),
    )
    grad_q = (
        grad_q_group.reshape(seq_count, KV, groups, rows_seq, HD)
        .transpose(0, 3, 1, 2, 4)
        .reshape(seq_count, rows_seq, HQ, HD)
    )
    grad_q_b = (
        rotate_back(grad_q, cos_heads, sin_heads).astype(jnp.bfloat16).reshape(total_rows, HQ * HD)
    )
    grad_kv_full = (
        jnp.stack([grad_keys, grad_values], 1)
        .transpose(0, 3, 1, 2, 4)
        .reshape(seq_count, seq_len, 2 * KV * HD)
    )
    grad_kv_local = (
        lax.psum_scatter(grad_kv_full.astype(jnp.bfloat16), "seq", scatter_dimension=1, tiled=True)
        .astype(jnp.float32)
        .reshape(seq_count, rows_seq, 2, KV, HD)
    )
    grad_k = rotate_back(grad_kv_local[:, :, 0], cos_heads, sin_heads)
    grad_kv_b = (
        jnp.stack([grad_k, grad_kv_local[:, :, 1]], 2)
        .astype(jnp.bfloat16)
        .reshape(total_rows, 2 * KV * HD)
    )
    grad_query = dot_first(norm1_b, grad_q_b)
    grad_keyval = dot_first(norm1_b, grad_kv_b)
    grad_in = dot_first(norm1_b, grad_proj)
    grad_dt = dot_first(norm1_b, grad_dt_b)
    grad_norm1 = (
        dot_last(grad_q_b, back[1])
        + dot_last(grad_kv_b, back[2])
        + dot_last(grad_proj, back[4])
        + dot_last(grad_dt_b, back[5])
    )
    _, norm1_pull = jax.vjp(rms_norm, token_f, gain_all[0])
    grad_token_norm, grad_gain1 = norm1_pull(grad_norm1)
    grad_tokens = (
        (grad_hidden + grad_token_norm).astype(jnp.bfloat16).reshape(seq_count, rows_seq, width)
    )
    grad_gains = jnp.stack([grad_gain1, grad_gain2])
    mixer_shards = (
        lax.psum_scatter(grad_gains, ("dp", "seq"), scatter_dimension=1, tiled=True),
        lax.psum_scatter(grad_query, ("dp", "seq"), scatter_dimension=0, tiled=True),
        lax.psum_scatter(grad_keyval, ("dp", "seq"), scatter_dimension=0, tiled=True),
        lax.psum_scatter(grad_attn_out, ("dp", "seq"), scatter_dimension=0, tiled=True),
        lax.psum_scatter(grad_in, ("dp", "seq"), scatter_dimension=0, tiled=True),
        lax.psum_scatter(grad_dt, ("dp", "seq"), scatter_dimension=0, tiled=True),
        lax.psum_scatter(grad_conv, ("dp", "seq"), scatter_dimension=1, tiled=True),
        lax.psum_scatter(grad_mamba_out, ("dp", "seq"), scatter_dimension=0, tiled=True),
    )
    owned = (
        mixer_shards[0],
        mixer_shards[1],
        mixer_shards[2],
        mixer_shards[3],
        mixer_shards[4],
        mixer_shards[5],
        mixer_shards[6],
        mixer_shards[7],
        ffn_shards[0],
        ffn_shards[1],
    )
    head_total = lax.psum(grad_head_local, ("dp", "seq"))
    return (
        mixed,
        grad_tokens,
        owned[0],
        owned[1],
        owned[2],
        owned[3],
        owned[4],
        owned[5],
        owned[6],
        head_total[:2],
        head_total[2],
        owned[7],
        owned[8],
        owned[9],
    )


def solution(mesh):
    return jax.shard_map(
        body,
        mesh=mesh,
        in_specs=(
            P("dp", "seq", None),
            P("dp"),
            P(None, ("dp", "seq")),
            P(("dp", "seq"), None),
            P(("dp", "seq"), None),
            P(("dp", "seq"), None),
            P(("dp", "seq"), None),
            P(("dp", "seq"), None),
            P(None, ("dp", "seq")),
            P(),
            P(("dp", "seq"), None),
            P(("dp", "seq"), None),
            P(("dp", "seq"), None),
            P("dp", "seq", None),
        ),
        out_specs=(
            P("dp", "seq", None),
            P("dp", "seq", None),
            P(None, ("dp", "seq")),
            P(("dp", "seq"), None),
            P(("dp", "seq"), None),
            P(("dp", "seq"), None),
            P(("dp", "seq"), None),
            P(("dp", "seq"), None),
            P(None, ("dp", "seq")),
            P(),
            P(),
            P(("dp", "seq"), None),
            P(("dp", "seq"), None),
            P(("dp", "seq"), None),
        ),
        check_vma=False,
    )
```

profile of v0, /device:TPU:0, one launch (start us, length us, event | category | flops | bytes accessed | tf_op | source)
XLA Modules:
  0.0 4267.3 jit_solution(5535126166074606269)
XLA Ops:
  8.7 43.2 %all-gather.3 = bf16[32,64,2]{1,2,0:T(2,128)(2,1)S(1)} all-gather(bf16[1,64,2]{1,2,0:T(2,128)(2,1)} %bitcast.550), channel_id=1, replica_groups=mesh['dp'=4,'seq'=8] {'dp','seq'}, dimensions={0}, use_global_device_ids=true | all-gather | bytes 8448 | tf_op jit(solution)/shard_map/all_gather | solution.py:226
  55.5 14.7 all-gather.19.cloned.1.call-done
  75.5 40.4 all-gather.4
  116.0 40.9 all-gather.5
  161.7 77.7 %all-gather.25.cloned.1.call-done = bf16[2048,6656]{1,0:T(8,128)(2,1)} async-done(((bf16[64,6656]{1,0:T(8,128)(2,1)}), bf16[2048,6656]{1,0:T(8,128)(2,1)}) %all-gather.25.cloned.1.call-update) | async-done | bytes 27262992 | tf_op jit(solution)/shard_map/all_gather | solution.py:230
  288.6 14.4 all-gather.1
  315.6 19.2 all-gather.17.cloned.1.call-done
  349.1 15.8 while.74
  385.1 169.7 %all-gather.33.cloned.1.call-done = bf16[16,48,64,256]{3,2,1,0:T(8,128)(2,1)} async-done(((bf16[2,48,64,256]{3,2,1,0:T(8,128)(2,1)}), bf16[16,48,64,256]{3,2,1,0:T(8,128)(2,1)}) %all-gather.33.cloned.1.call-update) | async-done | bytes 25165840 | tf_op jit(solution)/shard_map/all_gather | solution.py:32
  554.8 64.4 %while.76 = (s32[]{:T(128)}, f32[2,48,64,256]{3,2,1,0:T(8,128)}, s32[]{:T(128)}, bf16[8,2,48,64,256]{4,3,2,1,0:T(8,128)(2,1)}, bf16[8,2,48]{2,1,0:T(2,128)(2,1)S(1)}) while((s32[]{:T(128)}, f32[2,48,64,256]{3,2,1,0:T(8,128)}, s32[]{:T(128)}, bf16[8,2,48,64,256]{4,3,2,1,0:T(8,128)(2,1)}, ...), condition=%wide.region_7.8_spmd.clone.clone, body=%wide.region_6.7_spmd.clone.sunk.clone | while | flops 7864420 | bytes 15729697 | solution.py:50
  664.0 51.3 %all-gather.23.cloned.1.call-done = bf16[1024,2048]{1,0:T(8,128)(2,1)} async-done(((bf16[32,2048]{1,0:T(8,128)(2,1)}), bf16[1024,2048]{1,0:T(8,128)(2,1)}) %all-gather.23.cloned.1.call-update) | async-done | bytes 4194320 | tf_op jit(solution)/shard_map/all_gather | solution.py:229
  719.9 191.8 %all-gather.29.cloned.1.call-done = bf16[2048,8192]{1,0:T(8,128)(2,1)} async-done(((bf16[64,8192]{1,0:T(8,128)(2,1)}), bf16[2048,8192]{1,0:T(8,128)(2,1)}) %all-gather.29.cloned.1.call-update) | async-done | bytes 33554448 | tf_op jit(solution)/shard_map/all_gather | solution.py:234
  911.7 17.7 fusion.207
  929.4 98.5 %all-gather.31.cloned.1.call-done = bf16[4096,2048]{1,0:T(8,128)(2,1)} async-done(((bf16[128,2048]{1,0:T(8,128)(2,1)}), bf16[4096,2048]{1,0:T(8,128)(2,1)}) %all-gather.31.cloned.1.call-update) | async-done | bytes 16777232 | tf_op jit(solution)/shard_map/all_gather | solution.py:235
  1040.8 16.8 multiply_reduce_fusion.10
  1062.7 29.7 while.75
  1143.1 17.3 fusion.70
  1188.2 168.2 %all-gather.35.cloned.1.call-done = bf16[16,48,64,256]{3,2,1,0:T(8,128)(2,1)} async-done(((bf16[2,48,64,256]{3,2,1,0:T(8,128)(2,1)}), bf16[16,48,64,256]{3,2,1,0:T(8,128)(2,1)}) %all-gather.35.cloned.1.call-update) | async-done | bytes 25165840 | tf_op jit(solution)/shard_map/all_gather | solution.py:32
  1356.4 68.3 %while.77 = (s32[]{:T(128)}, f32[2,48,64,256]{3,2,1,0:T(8,128)}, s32[]{:T(128)}, bf16[8,2,48,64,256]{4,3,2,1,0:T(8,128)(2,1)}, bf16[8,2,48]{2,1,0:T(2,128)(2,1)}) while((s32[]{:T(128)}, f32[2,48,64,256]{3,2,1,0:T(8,128)}, s32[]{:T(128)}, bf16[8,2,48,64,256]{4,3,2,1,0:T(8,128)(2,1)}, ...), condition=%wide.region_16.17_spmd.clone.clone, body=%wide.region_15.16_spmd.clone.sunk.clone | while | flops 7864424 | bytes 15729743 | solution.py:50
  1539.9 14.9 fusion.221
  1555.5 27.1 fusion.106
  1583.8 21.0 fusion.119
  1619.0 41.3 psum.7
  1667.8 110.9 %reduce-scatter.40.cloned.1.call-done = f32[112,5]{1,0:T(8,128)} async-done(((f32[3584,5]{1,0:T(8,128)}), f32[112,5]{1,0:T(8,128)}) %reduce-scatter.40.cloned.1.call-update) | async-done | bytes 2256
  1780.1 131.8 %reduce-scatter.38.cloned.1.call-done = f32[64,48]{1,0:T(8,128)} async-done(((f32[2048,48]{1,0:T(8,128)}), f32[64,48]{1,0:T(8,128)}) %reduce-scatter.38.cloned.1.call-update) | async-done | bytes 12304
  1913.4 140.2 %reduce-scatter.22.cloned.1.call-done = f32[64,512]{1,0:T(8,128)} async-done(((f32[2048,512]{1,0:T(8,128)}), f32[64,512]{1,0:T(8,128)}) %reduce-scatter.22.cloned.1.call-update) | async-done | bytes 131088 | tf_op jit(solution)/shard_map/reduce_scatter | solution.py:444
  2053.7 151.5 %reduce-scatter.20.cloned.1.call-done = f32[64,1024]{1,0:T(8,128)} async-done(((f32[2048,1024]{1,0:T(8,128)}), f32[64,1024]{1,0:T(8,128)}) %reduce-scatter.20.cloned.1.call-update) | async-done | bytes 262160 | tf_op jit(solution)/shard_map/reduce_scatter | solution.py:443
  2205.1 153.6 %reduce-scatter.24.cloned.1.call-done = f32[32,2048]{1,0:T(8,128)} async-done(((f32[1024,2048]{1,0:T(8,128)}), f32[32,2048]{1,0:T(8,128)}) %reduce-scatter.24.cloned.1.call-update) | async-done | bytes 262160 | tf_op jit(solution)/shard_map/reduce_scatter | solution.py:445
  2358.7 250.7 %reduce-scatter.28.cloned.1.call-done = f32[96,2048]{1,0:T(8,128)} async-done(((f32[3072,2048]{1,0:T(8,128)}), f32[96,2048]{1,0:T(8,128)}) %reduce-scatter.28.cloned.1.call-update) | async-done | bytes 786448 | tf_op jit(solution)/shard_map/reduce_scatter | solution.py:449
  2609.4 363.6 %reduce-scatter.32.cloned.1.call-done = f32[128,2048]{1,0:T(8,128)} async-done(((f32[4096,2048]{1,0:T(8,128)}), f32[128,2048]{1,0:T(8,128)}) %reduce-scatter.32.cloned.1.call-update) | async-done | bytes 1048592 | tf_op jit(solution)/shard_map/reduce_scatter | solution.py:355
  2973.0 708.7 %reduce-scatter.30.cloned.1.call-done = f32[64,8192]{1,0:T(8,128)} async-done(((f32[2048,8192]{1,0:T(8,128)}), f32[64,8192]{1,0:T(8,128)}) %reduce-scatter.30.cloned.1.call-update) | async-done | bytes 2097168 | tf_op jit(solution)/shard_map/reduce_scatter | solution.py:354
  3681.8 578.5 %reduce-scatter.26.cloned.1.call-done = f32[64,6656]{1,0:T(8,128)} async-done(((f32[2048,6656]{1,0:T(8,128)}), f32[64,6656]{1,0:T(8,128)}) %reduce-scatter.26.cloned.1.call-update) | async-done | bytes 1703952 | tf_op jit(solution)/shard_map/reduce_scatter | solution.py:446
  (570 shorter events, 574.9 us)
Async XLA Ops:
  7.2 63.0 %all-gather.19.cloned.1.call-start = ((), (), s32[]{:S(2)}) async-start(), calls=%async_computation.12 | async-start | bytes 2162688 | tf_op jit(solution)/shard_map/all_gather | solution.py:228
  7.9 231.5 %all-gather.25.cloned.1.call-start = ((), (), s32[]{:S(2)}) async-start(), calls=%async_computation.15 | async-start | bytes 28114944 | tf_op jit(solution)/shard_map/all_gather | solution.py:230
  8.7 299.4 %all-gather.21.cloned.1.call-start = ((), (), s32[]{:S(2)}) async-start(), calls=%async_computation.13 | async-start | bytes 2359296 | tf_op jit(solution)/shard_map/all_gather | solution.py:260
  52.3 293.8 %copy-start.42 = (f32[128,128]{0,1:T(8,128)}, f32[128,128]{0,1:T(8,128)S(1)}, u32[]{:S(2)}) copy-start(f32[128,128]{0,1:T(8,128)S(1)} %get-tuple-element.728) | copy-start | bytes 196612
  52.3 293.8 %copy-start.52 = (f32[128,128]{0,1:T(8,128)}, f32[128,128]{0,1:T(8,128)S(1)}, u32[]{:S(2)}) copy-start(f32[128,128]{0,1:T(8,128)S(1)} %get-tuple-element.729) | copy-start | bytes 196612
  53.9 1003.7 %copy-start.59 = (f32[1,2048]{1,0:T(1,128)}, f32[1,2048]{1,0:T(1,128)S(1)}, u32[]{:S(2)}) copy-start(f32[1,2048]{1,0:T(1,128)S(1)} %get-tuple-element.715) | copy-start | bytes 24580
  74.9 260.0 %all-gather.17.cloned.1.call-start = ((), (), s32[]{:S(2)}) async-start(), calls=%async_computation.11 | async-start | bytes 4325376 | tf_op jit(solution)/shard_map/all_gather | solution.py:227
  75.4 479.4 %all-gather.33.cloned.1.call-start = ((), (), s32[]{:S(2)}) async-start(), calls=%async_computation.26 | async-start | bytes 28311552 | tf_op jit(solution)/shard_map/all_gather | solution.py:32
  159.3 128.6 %copy-start.31 = (f32[2,128,48]{2,1,0:T(8,128)}, f32[2,128,48]{2,1,0:T(8,128)S(1)}, u32[]{:S(2)}) copy-start(f32[2,128,48]{2,1,0:T(8,128)S(1)} %reduce_window_sum.26) | copy-start | bytes 147460
  256.7 3.2 collective-permute-start
  274.6 353.5 %copy-start.1 = (f32[2,128,3072]{1,2,0:T(8,128)}, f32[2,128,3072]{1,2,0:T(8,128)S(1)}, u32[]{:S(2)}) copy-start(f32[2,128,3072]{1,2,0:T(8,128)S(1)} %copy.284) | copy-start | bytes 9437188
  282.4 371.7 %all-gather.27.cloned.1.call-start = ((), (), s32[]{:S(2)}) async-start(), calls=%async_computation.16 | async-start | bytes 12976128 | tf_op jit(solution)/shard_map/all_gather | solution.py:233
  283.0 432.3 %all-gather.23.cloned.1.call-start = ((), (), s32[]{:S(2)}) async-start(), calls=%async_computation.14 | async-start | bytes 4325376 | tf_op jit(solution)/shard_map/all_gather | solution.py:229
  283.7 628.0 %all-gather.29.cloned.1.call-start = ((), (), s32[]{:S(2)}) async-start(), calls=%async_computation.17 | async-start | bytes 34603008 | tf_op jit(solution)/shard_map/all_gather | solution.py:234
  284.5 743.4 %all-gather.31.cloned.1.call-start = ((), (), s32[]{:S(2)}) async-start(), calls=%async_computation.18 | async-start | bytes 17301504 | tf_op jit(solution)/shard_map/all_gather | solution.py:235
  285.2 897.8 %reduce-scatter.34.cloned.1.call-start = ((), (), s32[]{:S(2)}) async-start(), calls=%async_computation.28 | async-start | bytes 2359296
  304.0 324.1 %copy-start.61 = (f32[2,128,48]{1,2,0:T(8,128)}, f32[2,128,48]{1,2,0:T(8,128)S(1)}, u32[]{:S(2)}) copy-start(f32[2,128,48]{1,2,0:T(8,128)S(1)} %copy.292) | copy-start | bytes 147460
  305.6 752.0 %copy-start.108 = (f32[256]{0:T(256)}, f32[256]{0:T(256)S(1)}, u32[]{:S(2)}) copy-start(f32[256]{0:T(256)S(1)} %fusion.195) | copy-start | bytes 3076
  719.9 337.8 %copy-start.15 = (f32[256,2048]{1,0:T(8,128)}, f32[256,2048]{1,0:T(8,128)S(1)}, u32[]{:S(2)}) copy-start(f32[256,2048]{1,0:T(8,128)S(1)} %get-tuple-element.723) | copy-start | bytes 6291460
  719.9 337.8 %copy-start.81 = (f32[256]{0:T(256)}, f32[256]{0:T(256)S(1)}, u32[]{:S(2)}) copy-start(f32[256]{0:T(256)S(1)} %fusion.197) | copy-start | bytes 3076
  1102.0 254.4 %all-gather.35.cloned.1.call-start = ((), (), s32[]{:S(2)}) async-start(), calls=%async_computation.27 | async-start | bytes 28311552 | tf_op jit(solution)/shard_map/all_gather | solution.py:32
  1131.0 535.3 %reduce-scatter.36.cloned.1.call-start = ((), (), s32[]{:S(2)}) async-start(), calls=%async_computation.29 | async-start | bytes 1081344
  1474.0 10.3 collective-permute-start.1
  1508.4 270.2 %reduce-scatter.40.cloned.1.call-start = ((), (), s32[]{:S(2)}) async-start(), calls=%async_computation.31 | async-start | bytes 1892352
  1510.5 401.4 %reduce-scatter.38.cloned.1.call-start = ((), (), s32[]{:S(2)}) async-start(), calls=%async_computation.30 | async-start | bytes 1081344
  1512.2 541.5 %reduce-scatter.22.cloned.1.call-start = ((), (), s32[]{:S(2)}) async-start(), calls=%async_computation.20 | async-start | bytes 4325376 | tf_op jit(solution)/shard_map/reduce_scatter | solution.py:444
  1515.0 690.2 %reduce-scatter.20.cloned.1.call-start = ((), (), s32[]{:S(2)}) async-start(), calls=%async_computation.19 | async-start | bytes 8650752 | tf_op jit(solution)/shard_map/reduce_scatter | solution.py:443
  1520.9 837.8 %reduce-scatter.24.cloned.1.call-start = ((), (), s32[]{:S(2)}) async-start(), calls=%async_computation.21 | async-start | bytes 8650752 | tf_op jit(solution)/shard_map/reduce_scatter | solution.py:445
  1527.0 1082.4 %reduce-scatter.28.cloned.1.call-start = ((), (), s32[]{:S(2)}) async-start(), calls=%async_computation.23 | async-start | bytes 25952256 | tf_op jit(solution)/shard_map/reduce_scatter | solution.py:449
  1538.7 1434.3 %reduce-scatter.32.cloned.1.call-start = ((), (), s32[]{:S(2)}) async-start(), calls=%async_computation.25 | async-start | bytes 34603008 | tf_op jit(solution)/shard_map/reduce_scatter | solution.py:355
  1554.8 2126.9 %reduce-scatter.30.cloned.1.call-start = ((), (), s32[]{:S(2)}) async-start(), calls=%async_computation.24 | async-start | bytes 69206016 | tf_op jit(solution)/shard_map/reduce_scatter | solution.py:354
  1582.6 2677.7 %reduce-scatter.26.cloned.1.call-start = ((), (), s32[]{:S(2)}) async-start(), calls=%async_computation.22 | async-start | bytes 56229888 | tf_op jit(solution)/shard_map/reduce_scatter | solution.py:446
  (127 other events, 2385.1 us)
Sparse Core Ops, SparseCore 0:
  11.0 59.1 all-gather.18
  73.1 166.2 all-gather.24
  241.6 28.9 all-gather.20
  273.5 61.3 all-gather.16
  336.3 218.4 all-gather.32
  557.7 94.2 all-gather.26
  655.0 60.3 all-gather.22
  718.3 193.3 all-gather.28
  914.7 113.0 all-gather.30
  1102.1 33.9 reduce-scatter.33
  1137.8 218.5 all-gather.34
  1508.5 134.9 reduce-scatter.35
  1645.9 132.7 reduce-scatter.39
  1780.7 131.1 reduce-scatter.37
  1914.8 138.8 reduce-scatter.21
  2056.5 148.6 reduce-scatter.19
  2208.0 150.7 reduce-scatter.23
  2366.7 242.6 reduce-scatter.27
  2612.3 360.6 reduce-scatter.31
  2975.8 705.9 reduce-scatter.29
  3684.6 575.6 reduce-scatter.25
where the time goes:
time: 4280 us; the launch traced here: 4270 us
  waiting for transfers between devices  3390 us (79%)
  matrix products  348 us (8%)
  other arithmetic  211 us (5%)
  blocking collectives  180 us (4%)
  local copies, waits for them, and re-layouts  122 us (3%)
    reduce_scatter x1, waiting for transfers between devices, body(): lax.psum_scatter(grad_gate_up, ('dp', 'seq'), scatter_dimension=0, tiled=...  709 us
    reduce_scatter x1, waiting for transfers between devices, body(): lax.psum_scatter(grad_in, ('dp', 'seq'), scatter_dimension=0, tiled=True)  579 us
    reduce_scatter x1, waiting for transfers between devices, body(): lax.psum_scatter(grad_down, ('dp', 'seq'), scatter_dimension=0, tiled=True)  364 us
    all_gather x2, waiting for transfers between devices, entering(): lax.all_gather(part.astype(kind), axis)  338 us
    reduce_scatter x1, waiting for transfers between devices, body(): lax.psum_scatter(grad_mamba_out, ('dp', 'seq'), scatter_dimension=0, tile...  251 us
    unnamed x25, waiting for transfers between devices  247 us
    all_gather x1, waiting for transfers between devices, body(): lax.all_gather(shards[8], ('dp', 'seq'), axis=0, tiled=True)  192 us
    reduce_scatter x1, waiting for transfers between devices, body(): lax.psum_scatter(grad_attn_out, ('dp', 'seq'), scatter_dimension=0, tiled...  154 us
  transfers between devices with their start and end apart: 23, of which 17 were waited for; matrix products, arithmetic and copies ran while one was open for 10% of the time, Pallas kernels for 0%

commit v1 on v0

v1 whole, which is shorter than its diff:
```python
import functools
import math

import jax
import jax.numpy as jnp
from jax import lax
from jax.experimental import pallas as pl
from jax.experimental.pallas import tpu as pltpu
from jax.sharding import Mesh
from jax.sharding import PartitionSpec as P

HQ = 8
KV = 2
HD = 128
MH = 48
MP = 64
NS = 256
KW = 4
MI = MH * MP

epsilon = 1e-05
rope_base = 100000000000.0
neg_big = -1e30
highest = lax.Precision.HIGHEST
bf16 = jnp.bfloat16
f32 = jnp.float32

ALL = ("dp", "g", "z", "c")
TEAM = ("z", "c")
PLANE = ("dp", "c")
LINE = ("g", "z")
SEQ = ("g", "z", "c")
SPREAD = ("dp", "g")


def rms_norm(values, gain):
    return values * lax.rsqrt(jnp.mean(values * values, -1, keepdims=True) + epsilon) * gain


def rope_tables(positions, head_size):
    half = head_size // 2
    freq = jnp.exp(jnp.arange(half, dtype=f32) * (-2.0 * math.log(rope_base) / head_size))
    angle = positions.astype(f32)[:, None] * freq[None, :]
    return (
        jnp.concatenate([jnp.cos(angle), jnp.cos(angle)], -1),
        jnp.concatenate([jnp.sin(angle), jnp.sin(angle)], -1),
    )


def rotate(values, cosine, sine):
    half = values.shape[-1] // 2
    turned = jnp.concatenate([-values[..., half:], values[..., :half]], -1)
    return values * cosine + turned * sine


def rotate_back(grads, cosine, sine):
    half = grads.shape[-1] // 2
    scaled = grads * sine
    return grads * cosine + jnp.concatenate([scaled[..., half:], -scaled[..., :half]], -1)


def dot(left, right, precision=None):
    return jnp.dot(left, right, preferred_element_type=f32, precision=precision)


def dot_first(left, right, precision=None):
    return lax.dot_general(
        left, right, (((0,), (0,)), ((), ())), preferred_element_type=f32, precision=precision
    )


def dot_last(left, right, precision=None):
    return lax.dot_general(
        left, right, (((1,), (1,)), ((), ())), preferred_element_type=f32, precision=precision
    )


def sigmoid(v):
    return 1.0 / (1.0 + jnp.exp(-v))


def softplus(v):
    return jnp.maximum(v, 0.0) + jnp.log(1.0 + jnp.exp(-jnp.abs(v)))


def params(count):
    return pltpu.CompilerParams(
        dimension_semantics=("arbitrary",) * count, vmem_limit_bytes=48 * 1024 * 1024
    )


def attend_mask(length_ref, start_ref, seq, block, width, first):
    qpos = start_ref[0] + first + lax.broadcasted_iota(jnp.int32, (block, width), 0)
    kpos = lax.broadcasted_iota(jnp.int32, (block, width), 1)
    return (kpos <= qpos) & (kpos < length_ref[seq])


def attend_fore_kernel(length_ref, start_ref, q_ref, k_ref, v_ref, o_ref, log_ref, *, scale, block):
    seq, at = pl.program_id(0), pl.program_id(1)
    keys = k_ref[0]
    scores = dot_last(q_ref[0], keys) * scale
    allowed = attend_mask(length_ref, start_ref, seq, block, keys.shape[0], at * block)
    scores = jnp.where(allowed, scores, neg_big)
    top = jnp.max(scores, -1, keepdims=True)
    expo = jnp.exp(scores - top)
    total = jnp.sum(expo, -1, keepdims=True)
    prob = (expo * (1.0 / total)).astype(bf16)
    o_ref[0] = dot(prob, v_ref[0]).astype(bf16)
    log_ref[0] = jnp.broadcast_to(top + jnp.log(total), log_ref.shape[1:])


def attend_fore(length, start, q, k, v, block):
    seqs, rows, width = q.shape
    kernel = functools.partial(attend_fore_kernel, scale=1.0 / math.sqrt(HD), block=block)
    qspec = pl.BlockSpec((1, block, width), lambda s, i: (s, i, 0))
    kspec = pl.BlockSpec((1, k.shape[1], width), lambda s, i: (s, 0, 0))
    smem = pl.BlockSpec(memory_space=pltpu.SMEM)
    return pl.pallas_call(
        kernel,
        grid=(seqs, rows // block),
        in_specs=[smem, smem, qspec, kspec, kspec],
        out_specs=[qspec, qspec],
        out_shape=[
            jax.ShapeDtypeStruct(q.shape, bf16),
            jax.ShapeDtypeStruct(q.shape, f32),
        ],
        compiler_params=params(2),
        name="attend_fore",
    )(length, start, q, k, v)


def attend_back_kernel(
    length_ref, start_ref, q_ref, k_ref, v_ref, do_ref, log_ref, dq_ref, dk_ref, dv_ref, *, scale, block
):
    seq, at = pl.program_id(0), pl.program_id(1)

    @pl.when(at == 0)
    def _():
        dk_ref[...] = jnp.zeros_like(dk_ref)
        dv_ref[...] = jnp.zeros_like(dv_ref)

    keys = k_ref[0]
    queries = q_ref[0]
    grad_out = do_ref[0]
    scores = dot_last(queries, keys) * scale
    allowed = attend_mask(length_ref, start_ref, seq, block, keys.shape[0], at * block)
    scores = jnp.where(allowed, scores, neg_big)
    prob = jnp.exp(scores - log_ref[0][:, :1])
    grad_prob = dot_last(grad_out, v_ref[0])
    centre = jnp.sum(prob * grad_prob, -1, keepdims=True)
    grad_score = (prob * (grad_prob - centre)).astype(bf16)
    dq_ref[0] = dot(grad_score, keys) * scale
    dk_ref[0] += dot_first(grad_score, queries) * scale
    dv_ref[0] += dot_first(prob.astype(bf16), grad_out)


def attend_back(length, start, q, k, v, grad_out, logs, block):
    seqs, rows, width = q.shape
    kernel = functools.partial(attend_back_kernel, scale=1.0 / math.sqrt(HD), block=block)
    qspec = pl.BlockSpec((1, block, width), lambda s, i: (s, i, 0))
    kspec = pl.BlockSpec((1, k.shape[1], width), lambda s, i: (s, 0, 0))
    smem = pl.BlockSpec(memory_space=pltpu.SMEM)
    return pl.pallas_call(
        kernel,
        grid=(seqs, rows // block),
        in_specs=[smem, smem, qspec, kspec, kspec, qspec, qspec],
        out_specs=[qspec, kspec, kspec],
        out_shape=[
            jax.ShapeDtypeStruct(q.shape, f32),
            jax.ShapeDtypeStruct(k.shape, f32),
            jax.ShapeDtypeStruct(k.shape, f32),
        ],
        compiler_params=params(2),
        name="attend_back",
    )(length, start, q, k, v, grad_out, logs)


def head_spread(heads):
    row = lax.broadcasted_iota(jnp.int32, (128, heads * MP), 0)
    col = lax.broadcasted_iota(jnp.int32, (128, heads * MP), 1)
    return (row == col // MP).astype(f32)


def triangle(span):
    row = lax.broadcasted_iota(jnp.int32, (span, span), 0)
    col = lax.broadcasted_iota(jnp.int32, (span, span), 1)
    return row >= col


def conv_pre(ext_ref, conv_ref, span):
    total = conv_ref[KW : KW + 1, :]
    for k in range(KW):
        total = total + conv_ref[k : k + 1, :] * ext_ref[pl.ds(8 - (KW - 1) + k, span), :]
    return total


def core_fore_kernel(
    x_ref, bc_ref, z_ref, dt_ref, halo_ref, conv_ref, head_ref, init_ref,
    gated_ref, y_ref, enter_ref, final_ref, decay_ref,
    ext, state, total, *, heads, span,
):
    inner = heads * MP
    at = pl.program_id(1)

    @pl.when(at == 0)
    def _():
        ext[0:8, :] = halo_ref[0]
        state[...] = init_ref[0]
        total[...] = jnp.zeros_like(total)

    ext[8:, :inner] = x_ref[...]
    ext[8:, inner:] = bc_ref[...]
    pre = conv_pre(ext, conv_ref, span)
    ext[0:8, :] = ext[span : span + 8, :]
    cv = pre * sigmoid(pre)
    xs = cv[:, :inner]
    bmat = cv[:, inner : inner + NS].astype(bf16)
    cmat = cv[:, inner + NS :].astype(bf16)
    spread = head_spread(heads)
    lower = triangle(span)
    step = softplus(dt_ref[...] + head_ref[0:1, :])
    decay_log = -jnp.exp(head_ref[1:2, :]) * step
    cum = dot(lower.astype(f32), decay_log, highest)
    cum_t = cum.T
    step_t = step.T
    last = cum[span - 1 : span, :]
    enter = state[...]
    enter_ref[0, 0] = enter
    pair = dot_last(cmat, bmat)
    xb = xs.astype(bf16)
    parts = []
    for h in range(heads):
        diff = cum[:, h : h + 1] - cum_t[h : h + 1, :]
        decay = jnp.exp(jnp.where(lower, diff, neg_big))
        mixing = (pair * decay * step_t[h : h + 1, :]).astype(bf16)
        parts.append(dot(mixing, xb[:, h * MP : (h + 1) * MP]))
    y = jnp.concatenate(parts, axis=1)
    y = y + dot_last(cmat, enter.astype(bf16)) * dot(jnp.exp(cum), spread, highest)
    y = y + xs * dot(jnp.broadcast_to(head_ref[2:3, :], (8, 128)), spread, highest)[0:1, :]
    tail = dot(jnp.exp(last - cum) * step, spread, highest)
    keep = jnp.broadcast_to(jnp.exp(cum_t[:, span - 1 : span]), (128, NS))
    new_state = dot_first(spread, keep, highest) * enter + dot_first((xs * tail).astype(bf16), bmat)
    state[...] = new_state
    final_ref[0] = new_state
    total[...] = total[...] + last
    decay_ref[0] = total[...]
    z = z_ref[...]
    y_ref[...] = y
    gated_ref[...] = (y * (z * sigmoid(z))).astype(bf16)


def core_fore(big, small, halo, conv, head, init, seqs, heads, span):
    rows = big.shape[0]
    inner = heads * MP
    wide = inner + 2 * NS
    count = rows // seqs // span
    dt_at = (small.shape[1] - 128) // 128

    def block(width, at):
        return pl.BlockSpec((span, width), lambda s, i: (s * count + i, at))

    state_spec = pl.BlockSpec((1, inner, NS), lambda s, i: (s, 0, 0))
    return pl.pallas_call(
        functools.partial(core_fore_kernel, heads=heads, span=span),
        grid=(seqs, count),
        in_specs=[
            block(inner, 1),
            block(2 * NS, 0),
            block(inner, 0),
            block(128, dt_at),
            pl.BlockSpec((1, 8, wide), lambda s, i: (s, 0, 0)),
            pl.BlockSpec((8, wide), lambda s, i: (0, 0)),
            pl.BlockSpec((8, 128), lambda s, i: (0, 0)),
            state_spec,
        ],
        out_specs=[
            block(inner, 0),
            block(inner, 0),
            pl.BlockSpec((1, 1, inner, NS), lambda s, i: (s, i, 0, 0)),
            state_spec,
            pl.BlockSpec((1, 8, 128), lambda s, i: (s, 0, 0)),
        ],
        out_shape=[
            jax.ShapeDtypeStruct((rows, inner), bf16),
            jax.ShapeDtypeStruct((rows, inner), f32),
            jax.ShapeDtypeStruct((seqs, count, inner, NS), f32),
            jax.ShapeDtypeStruct((seqs, inner, NS), f32),
            jax.ShapeDtypeStruct((seqs, 8, 128), f32),
        ],
        scratch_shapes=[
            pltpu.VMEM((span + 8, wide), f32),
            pltpu.VMEM((inner, NS), f32),
            pltpu.VMEM((8, 128), f32),
        ],
        compiler_params=params(2),
        name="core_fore",
    )(big, small, big, small, halo, conv, head, init)


def core_back_kernel(
    x_ref, bc_ref, z_ref, dt_ref, dg_ref, y_ref, enter_ref, halo_ref, conv_ref, head_ref, exit_ref,
    dzx_ref, dbc_ref, ddt_ref, gconv_ref, ghead_ref, dinit_ref, dfirst_ref,
    ext, dext, dstate, *, heads, span,
):
    inner = heads * MP
    seq, at = pl.program_id(0), pl.program_id(1)

    @pl.when((seq == 0) & (at == 0))
    def _():
        gconv_ref[...] = jnp.zeros_like(gconv_ref)
        ghead_ref[...] = jnp.zeros_like(ghead_ref)

    @pl.when(at == 0)
    def _():
        dext[span:, :] = jnp.zeros((8, dext.shape[1]), f32)
        dstate[...] = exit_ref[0]

    ext[0:8, :] = halo_ref[0, 0]
    ext[8:, :inner] = x_ref[...]
    ext[8:, inner:] = bc_ref[...]
    pre = conv_pre(ext, conv_ref, span)
    gate = sigmoid(pre)
    cv = pre * gate
    xs = cv[:, :inner]
    bmat = cv[:, inner : inner + NS].astype(bf16)
    cmat = cv[:, inner + NS :].astype(bf16)
    xb = xs.astype(bf16)
    z = z_ref[...]
    sig_z = sigmoid(z)
    grad_gated = dg_ref[...]
    dy = grad_gated * (z * sig_z)
    dzx_ref[:, :inner] = (grad_gated * y_ref[...] * (sig_z * (1.0 + z * (1.0 - sig_z)))).astype(bf16)
    dyb = dy.astype(bf16)
    spread = head_spread(heads)
    lower = triangle(span)
    raw = dt_ref[...] + head_ref[0:1, :]
    step = softplus(raw)
    rate = -jnp.exp(head_ref[1:2, :])
    decay_log = rate * step
    cum = dot(lower.astype(f32), decay_log, highest)
    cum_t = cum.T
    step_t = step.T
    last = cum[span - 1 : span, :]
    enter = enter_ref[0, 0]
    leave = dstate[...]
    pair = dot_last(cmat, bmat)
    dpair = jnp.zeros((span, span), f32)
    lane = lax.broadcasted_iota(jnp.int32, (span, 128), 1)
    line = lax.broadcasted_iota(jnp.int32, (128, span), 0)
    row_sums = jnp.zeros((span, 128), f32)
    col_sums = jnp.zeros((128, span), f32)
    parts = []
    for h in range(heads):
        diff = cum[:, h : h + 1] - cum_t[h : h + 1, :]
        decay = jnp.exp(jnp.where(lower, diff, neg_big))
        now = step_t[h : h + 1, :]
        cut = slice(h * MP, (h + 1) * MP)
        dmix = dot_last(dyb[:, cut], xb[:, cut]) * decay
        both = dmix * pair
        dmix_now = dmix * now
        dpair = dpair + dmix_now
        row_sums = jnp.where(lane == h, jnp.sum(both * now, 1, keepdims=True), row_sums)
        col_sums = jnp.where(line == h, jnp.sum(both, 0, keepdims=True), col_sums)
        mixing = (pair * decay * now).astype(bf16)
        parts.append(dot_first(mixing, dyb[:, cut]))
    dxs = jnp.concatenate(parts, axis=1)
    dstep = col_sums.T
    dcum = row_sums - dstep * step
    dpb = dpair.astype(bf16)
    dcm = dot(dpb, bmat)
    dbm = dot_first(dpb, cmat)
    grown = dot(jnp.exp(cum), spread, highest)
    enter_b = enter.astype(bf16)
    leave_b = leave.astype(bf16)
    dgrown = (dy * grown).astype(bf16)
    dcum = dcum + dot_last(dy * dot_last(cmat, enter_b) * grown, spread, highest)
    dcm = dcm + dot(dgrown, enter_b)
    fade = jnp.exp(last - cum)
    tail = dot(fade * step, spread, highest)
    into = dot_last(bmat, leave_b)
    dxs = dxs + into * tail
    owed = dot_last(xs * into, spread, highest) * fade
    dstep = dstep + owed
    owed = owed * step
    dcum = dcum - owed
    dbm = dbm + dot((xs * tail).astype(bf16), leave_b)
    held = dot(spread, enter * leave, highest)
    held = dot_last(jnp.ones((8, NS), f32), held, highest)[0:1, :]
    dlast = jnp.sum(owed, 0, keepdims=True) + jnp.exp(last) * held
    keep = jnp.broadcast_to(jnp.exp(cum_t[:, span - 1 : span]), (128, NS))
    new_dstate = dot_first(spread, keep, highest) * leave + dot_first(dgrown, cmat)
    dstate[...] = new_dstate
    dinit_ref[0] = new_dstate
    dlog = dot_first(lower.astype(f32), dcum, highest) + dlast
    dstep = dstep + dlog * rate
    ddt = dstep * sigmoid(raw)
    ddt_ref[...] = ddt.astype(bf16)
    skip = dot(jnp.broadcast_to(head_ref[2:3, :], (8, 128)), spread, highest)[0:1, :]
    dxs = dxs + skip * dy
    ghead_ref[0:1, :] += jnp.sum(ddt, 0, keepdims=True)
    ghead_ref[1:2, :] += jnp.sum(dlog * decay_log, 0, keepdims=True)
    ghead_ref[2:3, :] += jnp.sum(dot_last(dy * xs, spread, highest), 0, keepdims=True)
    slope = gate * (1.0 + pre * (1.0 - gate))
    dpre = jnp.concatenate([dxs, dbm, dcm], axis=1) * slope
    dext[0:span, :] = dpre
    gconv_ref[KW : KW + 1, :] += jnp.sum(dpre, 0, keepdims=True)
    dxbc = jnp.zeros_like(dpre)
    for k in range(KW):
        dxbc = dxbc + conv_ref[k : k + 1, :] * dext[pl.ds(KW - 1 - k, span), :]
        gconv_ref[k : k + 1, :] += jnp.sum(
            dpre * ext[pl.ds(8 - (KW - 1) + k, span), :], 0, keepdims=True
        )
    dzx_ref[:, inner:] = dxbc[:, :inner].astype(bf16)
    dbc_ref[...] = dxbc[:, inner:].astype(bf16)
    dext[span:, :] = dext[0:8, :]
    dfirst_ref[0] = dext[0:8, :]


def core_back(big, small, dmixed, y, enter, halos, conv, head, leave, seqs, heads, span):
    rows = big.shape[0]
    inner = heads * MP
    wide = inner + 2 * NS
    count = rows // seqs // span
    dt_at = (small.shape[1] - 128) // 128

    def block(width, at):
        return pl.BlockSpec((span, width), lambda s, i: (s * count + count - 1 - i, at))

    state_spec = pl.BlockSpec((1, inner, NS), lambda s, i: (s, 0, 0))
    return pl.pallas_call(
        functools.partial(core_back_kernel, heads=heads, span=span),
        grid=(seqs, count),
        in_specs=[
            block(inner, 1),
            block(2 * NS, 0),
            block(inner, 0),
            block(128, dt_at),
            block(inner, 0),
            block(inner, 0),
            pl.BlockSpec((1, 1, inner, NS), lambda s, i: (s, count - 1 - i, 0, 0)),
            pl.BlockSpec((1, 1, 8, wide), lambda s, i: (s, count - 1 - i, 0, 0)),
            pl.BlockSpec((8, wide), lambda s, i: (0, 0)),
            pl.BlockSpec((8, 128), lambda s, i: (0, 0)),
            state_spec,
        ],
        out_specs=[
            block(2 * inner, 0),
            block(2 * NS, 0),
            block(128, 0),
            pl.BlockSpec((8, wide), lambda s, i: (0, 0)),
            pl.BlockSpec((8, 128), lambda s, i: (0, 0)),
            state_spec,
            pl.BlockSpec((1, 8, wide), lambda s, i: (s, 0, 0)),
        ],
        out_shape=[
            jax.ShapeDtypeStruct((rows, 2 * inner), bf16),
            jax.ShapeDtypeStruct((rows, 2 * NS), bf16),
            jax.ShapeDtypeStruct((rows, 128), bf16),
            jax.ShapeDtypeStruct((8, wide), f32),
            jax.ShapeDtypeStruct((8, 128), f32),
            jax.ShapeDtypeStruct((seqs, inner, NS), f32),
            jax.ShapeDtypeStruct((seqs, 8, wide), f32),
        ],
        scratch_shapes=[
            pltpu.VMEM((span + 8, wide), f32),
            pltpu.VMEM((span + 8, wide), f32),
            pltpu.VMEM((inner, NS), f32),
        ],
        compiler_params=params(2),
        name="core_back",
    )(big, small, big, small, dmixed, y, enter, halos, conv, head, leave)


def passed_along(block, distance):
    devices = range(lax.axis_size("g"))
    route = [(i - distance, i) for i in devices if i - distance in devices]
    return lax.ppermute(block, "g", route)


def entering(decay, local, reverse):
    peers, here = lax.axis_size("g"), lax.axis_index("g")
    decays = lax.all_gather(decay, "g")
    locals_ = lax.all_gather(local.astype(bf16), "g")
    state = jnp.zeros_like(local)
    for k in range(peers):
        at = peers - 1 - k if reverse else k
        reached = (at > here) if reverse else (at < here)
        state = jnp.where(reached, decays[at] * state + locals_[at].astype(f32), state)
    return state


def head_decay(decay_log, heads):
    keep = jnp.exp(decay_log[:, 0, :heads])
    return jnp.repeat(keep, MP, axis=1)[:, :, None]


def body(
    tokens, lengths, gains, w_query, w_keyval, w_attn_out, w_in, w_dt, conv_params, head_params,
    w_mamba_out, w_gate_up, w_down, cotangent,
):
    seqs, rows_seq, width = tokens.shape
    own_rows = seqs * rows_seq
    dp, groups, team = lax.axis_size("dp"), lax.axis_size("g"), lax.axis_size(TEAM)
    devices, line, plane = lax.axis_size(ALL), lax.axis_size(LINE), lax.axis_size(PLANE)
    seq_size = groups * team
    me = lax.axis_index(TEAM)
    heads = MH // team
    inner = heads * MP
    query = HQ * HD // team
    block_len = rows_seq * team
    rows = seqs * block_len
    held = w_query.shape[0]
    span = math.gcd(256, block_len)
    start = (lax.axis_index("g") * block_len).astype(jnp.int32).reshape(1)
    kv_head = me * (HQ // team) * KV // HQ

    block_tokens = lax.all_gather(tokens, TEAM, axis=1, tiled=True).reshape(rows, width)
    conv_flat = conv_params.reshape(-1)
    conv_cols = -(-conv_flat.shape[0] // held)
    conv_flat = jnp.pad(conv_flat, (0, conv_cols * held - conv_flat.shape[0]))
    packed = jnp.concatenate(
        [w_in[:, 2 * MI :], w_keyval, w_dt, gains.T, conv_flat.reshape(held, conv_cols)], axis=1
    )
    packed = lax.all_gather(packed, ALL, axis=0, tiled=True)
    at = 2 * NS
    w_bc, at = packed[:, :at], at
    w_kv = packed[:, at : at + 2 * KV * HD].reshape(width, 2, KV, HD)
    at += 2 * KV * HD
    w_step = packed[:, at : at + MH]
    at += MH
    gain_all = packed[:, at : at + 2].astype(f32).T
    at += 2
    conv_size = conv_params.size
    conv_all = packed[:, at:].reshape(devices, held * conv_cols)[:, :conv_size]
    conv_all = (
        conv_all.reshape(devices, KW + 1, -1).transpose(1, 0, 2).reshape(KW + 1, -1).astype(f32)
    )
    conv_own = jnp.concatenate(
        [lax.dynamic_slice_in_dim(conv_all, me * inner, inner, 1), conv_all[:, MI:]], axis=1
    )
    conv_own = jnp.pad(conv_own, ((0, 8 - KW - 1), (0, 0)))
    head_own = jnp.pad(
        lax.dynamic_slice_in_dim(head_params, me * heads, heads, 1), ((0, 5), (0, 128 - heads))
    )
    w_small = jnp.concatenate(
        [
            w_bc,
            lax.dynamic_index_in_dim(w_kv, kv_head, 2, keepdims=False).reshape(width, 2 * HD),
            jnp.pad(
                lax.dynamic_slice_in_dim(w_step, me * heads, heads, 1), ((0, 0), (0, 128 - heads))
            ),
        ],
        axis=1,
    )
    w_big = jnp.concatenate(
        [
            w_in[:, :MI].reshape(held, team, inner),
            w_in[:, MI : 2 * MI].reshape(held, team, inner),
            w_query.reshape(held, team, query),
        ],
        axis=2,
    ).transpose(1, 0, 2)
    w_big = lax.all_to_all(w_big, TEAM, 0, 0, tiled=True).reshape(team * held, 2 * inner + query)
    w_big = lax.all_gather(w_big, SPREAD, axis=0, tiled=True)

    ratio = team // dp
    part = seq_size // ratio
    attn_rows, mamba_rows = w_attn_out.shape[0], w_mamba_out.shape[0]
    out_rows = attn_rows + mamba_rows
    cut = width // dp
    my_seq = lax.axis_index(SEQ)
    w_out = jnp.concatenate([w_attn_out, w_mamba_out], axis=0)
    w_out = w_out.reshape(out_rows, dp, cut).transpose(1, 0, 2)
    w_out = lax.all_to_all(w_out, "dp", 0, 0, tiled=True)
    mine = (jnp.arange(ratio) == my_seq // part)[None, :, None, None]
    w_out = jnp.where(mine, w_out[:, None], jnp.zeros((), bf16)).reshape(1, team, out_rows, cut)
    w_out = jnp.broadcast_to(w_out, (groups, team, out_rows, cut)).reshape(-1, out_rows, cut)
    w_out = lax.all_to_all(w_out, SEQ, 0, 0, tiled=True)
    w_out = lax.dynamic_slice_in_dim(w_out, (me % ratio) * part, part, 0)
    w_out = jnp.concatenate(
        [w_out[:, :attn_rows].reshape(-1, cut), w_out[:, attn_rows:].reshape(-1, cut)], axis=0
    )
    w_out = lax.all_gather(w_out, "dp", axis=1, tiled=True)

    ffn_block = w_down.shape[0]
    w_gu = w_gate_up.reshape(held, 2, dp, line, plane // dp, ffn_block).transpose(2, 4, 0, 1, 3, 5)
    w_gu = lax.all_to_all(
        w_gu.reshape(plane, held, 2 * line * ffn_block), PLANE, 0, 0, tiled=True
    ).reshape(dp, plane // dp, held, -1)
    w_gu = lax.all_gather(w_gu, LINE, axis=1, tiled=True).reshape(width, -1)
    w_dn = lax.all_gather(w_down, LINE, axis=0, tiled=True)

    norm1 = rms_norm(block_tokens.astype(f32), gain_all[0]).astype(bf16)
    big = dot(norm1, w_big)
    small = dot(norm1, w_small)
    positions = start[0] + jnp.arange(block_len, dtype=jnp.int32)
    cosine, sine = rope_tables(positions, HD)
    q = rotate(big[:, 2 * inner :].reshape(seqs, block_len, HD), cosine, sine).astype(bf16)
    k = rotate(
        small[:, 2 * NS : 2 * NS + HD].reshape(seqs, block_len, HD), cosine, sine
    ).astype(bf16)
    v = small[:, 2 * NS + HD : 2 * NS + 2 * HD].reshape(seqs, block_len, HD).astype(bf16)
    if groups > 1:
        k = lax.all_gather(k, "g", axis=1, tiled=True)
        v = lax.all_gather(v, "g", axis=1, tiled=True)
    attn, logs = attend_fore(lengths, start, q, k, v, span)
    wide = inner + 2 * NS
    xbc = jnp.concatenate([big[:, inner : 2 * inner], small[:, : 2 * NS]], axis=1)
    xbc = xbc.reshape(seqs, block_len // span, span, wide)
    ends = xbc[:, :, span - 8 :, :]
    if groups > 1:
        before = passed_along(ends[:, -1].astype(bf16), 1).astype(f32)
    else:
        before = jnp.zeros((seqs, 8, wide), f32)
    halos = jnp.concatenate([before[:, None], ends[:, :-1]], axis=1)
    init = jnp.zeros((seqs, inner, NS), f32)
    fore = functools.partial(core_fore, seqs=seqs, heads=heads, span=span)
    gated, y, enter, final, decay_log = fore(big, small, before, conv_own, head_own, init)
    if groups > 1:
        decay = head_decay(decay_log, heads)
        init = entering(decay, final, False)
        gated, y, enter, final, _ = fore(big, small, before, conv_own, head_own, init)
    mixed_in = jnp.concatenate([attn.reshape(rows, HD), gated], axis=1)
    mix = dot(mixed_in, w_out).astype(bf16).reshape(seqs, block_len, width)
    mix = lax.psum_scatter(mix, TEAM, scatter_dimension=1, tiled=True)
    own_positions = my_seq * rows_seq + jnp.arange(rows_seq, dtype=jnp.int32)
    valid = (own_positions[None, :] < lengths[:, None]).astype(f32).reshape(own_rows, 1)
    token_f = tokens.astype(f32).reshape(own_rows, width)
    hidden = token_f + valid * mix.astype(f32).reshape(own_rows, width)

    norm2_f, norm2_pull = jax.vjp(rms_norm, hidden, gain_all[1])
    norm2 = lax.all_gather(norm2_f.astype(bf16), PLANE, axis=0, tiled=True)
    cot = cotangent.astype(f32).reshape(own_rows, width)
    grad_ffn = lax.all_gather((valid * cot).astype(bf16), PLANE, axis=0, tiled=True)
    gate_up = dot(norm2, w_gu)
    units = gate_up.shape[1] // 2
    gate, upper = gate_up[:, :units], gate_up[:, units:]
    sig_gate = sigmoid(gate)
    act = (gate * sig_gate * upper).astype(bf16)
    ffn = dot(act, w_dn).astype(bf16)
    ffn = lax.psum_scatter(ffn, PLANE, scatter_dimension=0, tiled=True)
    mixed = (hidden + valid * ffn.astype(f32)).astype(bf16).reshape(seqs, rows_seq, width)
    grad_act = dot_last(grad_ffn, w_dn)
    grad_gate = grad_act * upper * (sig_gate * (1.0 + gate * (1.0 - sig_gate)))
    grad_upper = grad_act * gate * sig_gate
    grad_gu = jnp.concatenate([grad_gate, grad_upper], 1).astype(bf16)
    grad_norm2 = dot_last(grad_gu, w_gu).astype(bf16)
    grad_norm2 = lax.psum_scatter(grad_norm2, PLANE, scatter_dimension=0, tiled=True)
    grad_hidden_norm, grad_gain2 = norm2_pull(grad_norm2.astype(f32))
    grad_hidden = cot + grad_hidden_norm
    grad_mix = (valid * grad_hidden).astype(bf16).reshape(seqs, rows_seq, width)
    grad_mix = lax.all_gather(grad_mix, TEAM, axis=1, tiled=True).reshape(rows, width)

    grad_w_gu = dot_first(norm2, grad_gu).astype(bf16)
    grad_w_gu = grad_w_gu.reshape(dp, line, plane // dp, held, 2 * line * ffn_block)
    grad_w_gu = grad_w_gu.transpose(1, 0, 2, 3, 4)
    grad_w_gu = lax.psum_scatter(grad_w_gu, LINE, scatter_dimension=0, tiled=True)
    grad_w_gu = lax.all_to_all(
        grad_w_gu.reshape(plane, held, 2 * line * ffn_block), PLANE, 0, 0, tiled=True
    )
    grad_gate_up = (
        grad_w_gu.reshape(dp, plane // dp, held, 2, line, ffn_block)
        .transpose(2, 3, 0, 4, 1, 5)
        .reshape(held, -1)
        .astype(f32)
    )
    grad_w_dn = dot_first(act, grad_ffn).astype(bf16)
    grad_down = lax.psum_scatter(grad_w_dn, LINE, scatter_dimension=0, tiled=True).astype(f32)

    grad_mixed_in = dot_last(grad_mix, w_out)
    grad_o = grad_mixed_in[:, :HD].astype(bf16).reshape(seqs, block_len, HD)
    grad_w_out = dot_first(mixed_in, grad_mix).astype(bf16)
    grad_w_out = lax.psum_scatter(grad_w_out, "dp", scatter_dimension=1, tiled=True)
    if groups > 1:
        grad_w_out = lax.psum(grad_w_out.astype(f32), "g").astype(bf16)
    split = part * attn_rows
    grad_w_out = jnp.concatenate(
        [
            grad_w_out[:split].reshape(part, attn_rows, cut),
            grad_w_out[split:].reshape(part, mamba_rows, cut),
        ],
        axis=1,
    )
    grad_w_out = lax.dynamic_update_slice_in_dim(
        jnp.zeros((seq_size, out_rows, cut), bf16), grad_w_out, (me % ratio) * part, 0
    )
    grad_w_out = lax.all_to_all(grad_w_out, SEQ, 0, 0, tiled=True)
    grad_w_out = grad_w_out.reshape(groups, dp, ratio, out_rows, cut)[0]
    grad_w_out = lax.dynamic_index_in_dim(grad_w_out, my_seq // part, 1, keepdims=False)
    grad_w_out = lax.all_to_all(grad_w_out, "dp", 0, 0, tiled=True)
    grad_w_out = grad_w_out.transpose(1, 0, 2).reshape(out_rows, width).astype(f32)
    grad_attn_out, grad_mamba_out = grad_w_out[:attn_rows], grad_w_out[attn_rows:]

    dq, dk, dv = attend_back(lengths, start, q, k, v, grad_o, logs, span)
    if groups > 1:
        dk = lax.psum_scatter(dk, "g", scatter_dimension=1, tiled=True)
        dv = lax.psum_scatter(dv, "g", scatter_dimension=1, tiled=True)
    dq = rotate_back(dq, cosine, sine).astype(bf16).reshape(rows, HD)
    dk = rotate_back(dk, cosine, sine).astype(bf16).reshape(rows, HD)
    dv = dv.astype(bf16).reshape(rows, HD)
    leave = jnp.zeros((seqs, inner, NS), f32)
    back = functools.partial(core_back, seqs=seqs, heads=heads, span=span)
    grad_gated = grad_mixed_in[:, HD:]
    dzx, dbc, ddt, gconv, ghead, dinit, dfirst = back(
        big, small, grad_gated, y, enter, halos, conv_own, head_own, leave
    )
    if groups > 1:
        leave = entering(decay, dinit, True)
        dzx, dbc, ddt, gconv, ghead, dinit, dfirst = back(
            big, small, grad_gated, y, enter, halos, conv_own, head_own, leave
        )
        padded = jnp.concatenate([jnp.zeros((seqs, KW - 1, wide), f32), dfirst], axis=1)
        rim = sum(
            conv_own[j][None, None] * padded[:, KW - 1 - j : 2 * (KW - 1) - j] for j in range(KW)
        )
        rim = passed_along(rim.astype(bf16), -1).astype(f32)
        rim = jnp.pad(rim, ((0, 0), (block_len - KW + 1, 0), (0, 0))).reshape(rows, wide)
        dzx = jnp.concatenate(
            [dzx[:, :inner], (dzx[:, inner:].astype(f32) + rim[:, :inner]).astype(bf16)], axis=1
        )
        dbc = (dbc.astype(f32) + rim[:, inner:]).astype(bf16)
    dbig = jnp.concatenate([dzx, dq], axis=1)
    dsmall = jnp.concatenate([dbc, dk, dv, ddt], axis=1)
    grad_norm1 = (dot_last(dbig, w_big) + dot_last(dsmall, w_small)).astype(bf16)
    grad_norm1 = lax.psum_scatter(
        grad_norm1.reshape(seqs, block_len, width), TEAM, scatter_dimension=1, tiled=True
    )
    _, norm1_pull = jax.vjp(rms_norm, token_f, gain_all[0])
    grad_token_norm, grad_gain1 = norm1_pull(grad_norm1.astype(f32).reshape(own_rows, width))
    grad_tokens = (
        (grad_hidden + grad_token_norm).astype(bf16).reshape(seqs, rows_seq, width)
    )

    grad_w_big = dot_first(norm1, dbig).astype(bf16)
    grad_w_big = lax.psum_scatter(grad_w_big, SPREAD, scatter_dimension=0, tiled=True)
    grad_w_big = lax.all_to_all(
        grad_w_big.reshape(team, held, 2 * inner + query), TEAM, 0, 0, tiled=True
    )
    grad_w_big = grad_w_big.transpose(1, 0, 2).astype(f32)
    grad_z = grad_w_big[:, :, :inner].reshape(held, MI)
    grad_x = grad_w_big[:, :, inner : 2 * inner].reshape(held, MI)
    grad_query = grad_w_big[:, :, 2 * inner :].reshape(held, -1)

    grad_w_small = dot_first(norm1, dsmall).astype(bf16)
    grad_kv = lax.dynamic_update_slice_in_dim(
        jnp.zeros((width, 2, KV, HD), bf16),
        grad_w_small[:, 2 * NS : 2 * NS + 2 * HD].reshape(width, 2, 1, HD),
        kv_head,
        2,
    ).reshape(width, 2 * KV * HD)
    grad_step = lax.dynamic_update_slice_in_dim(
        jnp.zeros((width, MH), bf16),
        grad_w_small[:, 2 * NS + 2 * HD : 2 * NS + 2 * HD + heads],
        me * heads,
        1,
    )
    grad_pack = jnp.concatenate([grad_w_small[:, : 2 * NS], grad_kv, grad_step], axis=1)
    grad_pack = lax.all_to_all(
        grad_pack.reshape(devices, held, -1), ALL, 0, 0, tiled=True
    )
    grad_pack = jnp.sum(grad_pack.astype(f32), axis=0)
    grad_in = jnp.concatenate([grad_z, grad_x, grad_pack[:, : 2 * NS]], axis=1)
    grad_keyval = grad_pack[:, 2 * NS : 2 * NS + 2 * KV * HD]
    grad_dt = grad_pack[:, 2 * NS + 2 * KV * HD :]

    grad_gains = jnp.stack([grad_gain1, grad_gain2])
    grad_conv = jnp.concatenate(
        [
            lax.dynamic_update_slice_in_dim(
                jnp.zeros((KW + 1, MI), f32), gconv[: KW + 1, :inner], me * inner, 1
            ),
            gconv[: KW + 1, inner:],
        ],
        axis=1,
    )
    grad_head = lax.dynamic_update_slice_in_dim(
        jnp.zeros((3, MH), f32), ghead[:3, :heads], me * heads, 1
    )
    own_conv, own_gain = conv_params.shape[1], gains.shape[1]
    rest = jnp.concatenate(
        [
            grad_conv.reshape(KW + 1, devices, own_conv).transpose(1, 0, 2).reshape(devices, -1),
            grad_gains.reshape(2, devices, own_gain).transpose(1, 0, 2).reshape(devices, -1),
            jnp.broadcast_to(grad_head.reshape(1, -1), (devices, 3 * MH)),
        ],
        axis=1,
    )
    rest = jnp.sum(lax.all_to_all(rest, ALL, 0, 0, tiled=True), axis=0)
    conv_end = (KW + 1) * own_conv
    gain_end = conv_end + 2 * own_gain
    head_total = rest[gain_end:].reshape(3, MH)
    return (
        mixed,
        grad_tokens,
        rest[conv_end:gain_end].reshape(2, own_gain),
        grad_query,
        grad_keyval,
        grad_attn_out,
        grad_in,
        grad_dt,
        rest[:conv_end].reshape(KW + 1, own_conv),
        head_total[:2],
        head_total[2],
        grad_mamba_out,
        grad_gate_up,
        grad_down,
    )


def solution(mesh):
    dp, seq = mesh.shape["dp"], mesh.shape["seq"]
    team = math.gcd(math.gcd(HQ, MH), seq)
    split = Mesh(mesh.devices.reshape(dp, seq // team, team // 2, 2), ALL)
    rows = P(ALL, None)
    cols = P(None, ALL)
    acts = P("dp", SEQ, None)
    return jax.shard_map(
        body,
        mesh=split,
        in_specs=(
            acts, P("dp"), cols, rows, rows, rows, rows, rows, cols, P(), rows, rows, rows, acts,
        ),
        out_specs=(
            acts, acts, cols, rows, rows, rows, rows, rows, cols, P(), P(), rows, rows, rows,
        ),
        check_vma=False,
    )
```

time: 4280 us -> 1290 us (0.30)
  waiting for transfers between devices: 3390 us -> 690 us
  matrix products: 348 us -> 176 us
  other arithmetic: 211 us -> 60.7 us
  blocking collectives: 180 us -> 55.5 us
  Pallas kernels: 0 us -> 104 us
    reduce_scatter x7, waiting for transfers between devices: 2350 us -> 201 us  [the longest x1 130 us: body(): mix = lax.psum_scatter(mix, TEAM, scatter_dimension=1, tiled=True)]
    all_gather x10 -> x9, waiting for transfers between devices: 791 us -> 290 us  [the longest x1 82.2 us: body(): lax.all_gather(grad_mix, TEAM, axis=1, tiled=True).reshape(rows, width)]
    unnamed x25 -> x18, waiting for transfers between devices: 247 us -> 34.9 us
    all_to_all x0 -> x8, waiting for transfers between devices: none -> 164 us  [the longest x1 85.5 us: body(): lax.all_to_all(grad_pack.reshape(devices, held, -1), ALL, 0, 0, tiled=True)]
    all_gather x4 -> x0, blocking collectives: 139 us -> none  [the longest x1 43.2 us: body(): lax.all_gather(shards[0], ('dp', 'seq'), axis=1, tiled=True)]
    select_n x17 -> x1, other arithmetic: 129 us -> 1.11 us  [body(): jnp.where(mine, w_out[:, None], jnp.zeros((), bf16))]
    dot_general x25 -> x5, matrix products: 170 us -> 57 us  [dot(): return jnp.dot(left, right, preferred_element_type=f32, precision=precision)]
    pallas_call x0 -> x4, Pallas kernels: none -> 104 us  [the longest x1 59.2 us: core_back(): pl.pallas_call(functools.partial(core_back_kernel, heads=heads, span=span...]
  transfers between devices with their start and end apart: 23 -> 25, of which waited for: 17 -> 16; matrix products, arithmetic and copies ran while one was open for 10% -> 24% of each run, Pallas kernels for 0% -> 8%
where the time goes in v1:
time: 1290 us; the launch traced here: 1280 us
  waiting for transfers between devices  690 us (53%)
  matrix products  176 us (14%)
  local copies, waits for them, and re-layouts  143 us (11%)
  Pallas kernels  104 us (8%)
  other arithmetic  60.7 us (5%)
  blocking collectives  55.5 us (4%)
  starting transfers between devices  32.4 us (3%)
  between operations  16.9 us (1%)
    reduce_scatter x1, waiting for transfers between devices, body(): mix = lax.psum_scatter(mix, TEAM, scatter_dimension=1, tiled=True)  130 us
    all_to_all x1, waiting for transfers between devices, body(): lax.all_to_all(grad_pack.reshape(devices, held, -1), ALL, 0, 0, tiled=True)  85.5 us
    all_gather x1, waiting for transfers between devices, body(): lax.all_gather(grad_mix, TEAM, axis=1, tiled=True).reshape(rows, width)  82.2 us
    reduce_scatter x1, waiting for transfers between devices, body(): lax.psum_scatter(grad_norm2, PLANE, scatter_dimension=0, tiled=True)  71.2 us
    dot_general x5, matrix products, dot_last(): lax.dot_general(left, right, (((1,), (1,)), ((), ())), preferred_element_...  64.3 us
    pallas_call x1, Pallas kernels, core_back(): pl.pallas_call(functools.partial(core_back_kernel, heads=heads, span=span...  59.2 us
    dot_general x5, matrix products, dot(): return jnp.dot(left, right, preferred_element_type=f32, precision=precision)  57 us
    all_gather x1, waiting for transfers between devices, body(): lax.all_gather((valid * cot).astype(bf16), PLANE, axis=0, tiled=True)  55.5 us
  transfers between devices with their start and end apart: 25, of which 16 were waited for; matrix products, arithmetic and copies ran while one was open for 24% of the time, Pallas kernels for 8%

profile of v1, /device:TPU:0, one launch (start us, length us, event | category | flops | bytes accessed | tf_op | source)
XLA Modules:
  0.0 1278.1 jit_solution(16122747650833040260)
XLA Ops:
  16.3 35.9 %all_to_all.54 = bf16[8,64,896]{2,1,0:T(8,128)(2,1)} all-to-all(bf16[8,64,896]{2,1,0:T(8,128)(2,1)S(1)} %copy.110), channel_id=1, replica_groups=mesh['dp'=4,'g'=1,'z'=4,'c'=2] {'z','c'}, dimensions={0} | all-to-all | bytes 1835008 | tf_op jit(solution)/shard_map/all_to_all | solution.py:563
  59.0 10.3 all-to-all-done.1
  77.4 30.8 %all-to-all-done.2 = bf16[8,128,512]{2,1,0:T(8,128)(2,1)S(1)} async-done(((bf16[8,128,512]{2,1,0:T(8,128)(2,1)}), bf16[8,128,512]{2,1,0:T(8,128)(2,1)S(1)}, u32[]{:S(2)}, u32[]{:S(2)}) %all-to-all-start.2) | async-done | bytes 1048608 | tf_op jit(solution)/shard_map/all_to_all | solution.py:578
  124.4 49.1 %all-gather.10.cloned.1.call-done = bf16[2,1024,2048]{2,1,0:T(8,128)(2,1)} async-done(((bf16[2,128,2048]{2,1,0:T(8,128)(2,1)}), bf16[2,1024,2048]{2,1,0:T(8,128)(2,1)}) %all-gather.10.cloned.1.call-update) | async-done | bytes 8388624 | tf_op jit(solution)/shard_map/all_gather | solution.py:517
  188.2 11.2 fusion.27.bc_ref.dt_ref
  202.5 19.7 %all-gather.14.cloned.1.call-done = bf16[2048,896]{1,0:T(8,128)(2,1)} async-done(((bf16[512,896]{1,0:T(8,128)(2,1)}), bf16[2048,896]{1,0:T(8,128)(2,1)}) %all-gather.14.cloned.1.call-update) | async-done | bytes 3670032 | tf_op jit(solution)/shard_map/all_gather | solution.py:564
  222.1 12.3 fusion.50.x_ref.z_ref
  237.4 25.8 %core_fore.1 = (bf16[2048,384]{1,0:T(8,128)(2,1)S(1)}, f32[2048,384]{1,0:T(8,128)}, f32[2,4,384,256]{3,2,1,0:T(8,128)}, f32[2,384,256]{2,1,0:T(8,128)}, f32[2,8,128]{2,1,0:T(8,128)}) custom-call(f32[2048,896]{1,0:T(8,128)} %copy-done.10, f32[2048,896]{1,0:T(8,128)} %copy-done.9, f32[2048,896]{1,0:T(8,128)} %copy-done.10, f32[2048,896]{1,0:T(8,128)} %copy-done.9, ...), custom_call_target="tpu_custom_call" | custom-call | tf_op jit(solution)/shard_map/core_fore/pallas_call | solution.py:263
  274.0 10.0 convolution_convert_fusion.2
  291.8 19.6 %all_to_all.55 = bf16[8,64,1024]{2,1,0:T(8,128)(2,1)} all-to-all(bf16[8,64,1024]{2,1,0:T(8,128)(2,1)} %reshape.366), channel_id=1, replica_groups=mesh['dp'=4,'g'=1,'z'=4,'c'=2] {'dp','c'}, dimensions={0} | all-to-all | bytes 2097152 | tf_op jit(solution)/shard_map/all_to_all | solution.py:587
  311.6 129.8 %reduce-scatter.11.cloned.1.call-done = bf16[2,128,2048]{2,1,0:T(8,128)(2,1)} async-done(((bf16[2,1024,2048]{2,1,0:T(8,128)(2,1)}), bf16[2,128,2048]{2,1,0:T(8,128)(2,1)}) %reduce-scatter.11.cloned.1.call-update) | async-done | bytes 1048592 | tf_op jit(solution)/shard_map/reduce_scatter | solution.py:625
  449.2 51.2 %all-gather.18.cloned.1.call-done = bf16[2048,2048]{1,0:T(8,128)(2,1)} async-done(((bf16[256,2048]{1,0:T(8,128)(2,1)}), bf16[2048,2048]{1,0:T(8,128)(2,1)}) %all-gather.18.cloned.1.call-update) | async-done | bytes 8388624 | tf_op jit(solution)/shard_map/all_gather | solution.py:632
  500.5 14.9 %fusion.51 = f32[2048,1024]{0,1:T(8,128)} fusion(bf16[2048,2048]{1,0:T(8,128)(2,1)} %all-gather.18.cloned.1.call-done, bf16[2048,1024]{1,0:T(8,128)(2,1)} %bitcast.245), kind=kOutput, calls=%fused_computation.152 | convolution fusion | flops 8589934592 | bytes 20971520 | tf_op jit(solution)/shard_map/dot_general | solution.py:63
  515.3 32.2 %all-gather.22.cloned.1.call-done = bf16[512,2048]{1,0:T(8,128)(2,1)} async-done(((bf16[128,2048]{1,0:T(8,128)(2,1)}), bf16[512,2048]{1,0:T(8,128)(2,1)}) %all-gather.22.cloned.1.call-update) | async-done | bytes 2097168 | tf_op jit(solution)/shard_map/all_gather | solution.py:591
  547.5 55.5 %all-gather.24.cloned.1.call-done = bf16[2048,2048]{1,0:T(8,128)(2,1)} async-done(((bf16[256,2048]{1,0:T(8,128)(2,1)}), bf16[2048,2048]{1,0:T(8,128)(2,1)}) %all-gather.24.cloned.1.call-update) | async-done | bytes 8388624 | tf_op jit(solution)/shard_map/all_gather | solution.py:634
  603.0 13.8 %multiply_convert_fusion.1 = (bf16[2048,512]{0,1:T(8,128)(2,1)S(1)}, bf16[2048,512]{0,1:T(8,128)(2,1)S(1)}, bf16[2048,512]{0,1:T(8,128)(2,1)}) fusion(f32[2048,1024]{0,1:T(8,128)} %fusion.51, bf16[2048,2048]{1,0:T(8,128)(2,1)} %all-gather.24.cloned.1.call-done, bf16[512,2048]{1,0:T(8,128)(2,1)} %all-gather.22.cloned.1.call-done), kind=kOutput, calls=%fused_computation.15 | convolution fusion | flops 4311744512 | bytes 25165824 | tf_op jit(solution)/shard_map/dot_general | solution.py:73
  618.9 11.8 convolution_convert_fusion
  630.7 71.2 %reduce-scatter.15.cloned.1.call-done = bf16[256,2048]{1,0:T(8,128)(2,1)} async-done(((bf16[2048,2048]{1,0:T(8,128)(2,1)}), bf16[256,2048]{1,0:T(8,128)(2,1)}) %reduce-scatter.15.cloned.1.call-update) | async-done | bytes 1048592 | tf_op jit(solution)/shard_map/reduce_scatter | solution.py:648
  708.9 82.2 %all-gather.26.cloned.1.call-done = bf16[2,1024,2048]{2,1,0:T(8,128)(2,1)} async-done(((bf16[2,128,2048]{2,1,0:T(8,128)(2,1)}), bf16[2,1024,2048]{2,1,0:T(8,128)(2,1)}) %all-gather.26.cloned.1.call-update) | async-done | bytes 8388624 | tf_op jit(solution)/shard_map/all_gather | solution.py:652
  791.1 9.8 convolution_convert_fusion.7
  800.9 14.1 %convolution_convert_fusion.3 = bf16[2048,1024]{1,0:T(8,128)(2,1)} fusion(bf16[2048,2048]{1,0:T(8,128)(2,1)} %all-gather.18.cloned.1.call-done, bf16[2048,512]{0,1:T(8,128)(2,1)} %copy-done.53, bf16[2048,512]{0,1:T(8,128)(2,1)} %copy-done.52), kind=kOutput, calls=%fused_computation.18 | convolution fusion | flops 8600420352 | bytes 16777216 | tf_op jit(solution)/shard_map/dot_general | solution.py:67
  846.7 11.2 attend_back.1
  857.9 59.2 %core_back.1 = (bf16[2048,768]{1,0:T(8,128)(2,1)}, bf16[2048,512]{1,0:T(8,128)(2,1)S(1)}, bf16[2048,128]{1,0:T(8,128)(2,1)S(1)}, f32[8,896]{1,0:T(8,128)S(1)}, f...) custom-call(f32[2048,896]{1,0:T(8,128)} %copy-done.10, f32[2048,896]{1,0:T(8,128)} %copy-done.9, ...), custom_call_target="tpu_custom_call" | custom-call | tf_op jit(solution)/shard_map/core_back/pallas_call | solution.py:430
  924.0 10.8 convolution_convert_fusion.5
  935.0 16.1 %fusion.6 = f32[2048,2048]{1,0:T(8,128)} fusion(bf16[2048,896]{1,0:T(8,128)(2,1)} %all-gather.14.cloned.1.call-done, bf16[2048,128]{1,0:T(8,128)(2,1)} %bitcast.236, bf16[2048,768]{1,0:T(8,128)(2,1)} %get-tuple-element.31), kind=kOutput, calls=%fused_computation.34 | convolution fusion | flops 7523532800 | bytes 24117248 | tf_op jit(solution)/shard_map/dot_general | solution.py:73
  951.1 15.5 %add_convert_fusion = bf16[2048,2048]{1,0:T(8,128)(2,1)} fusion(f32[2048,2048]{1,0:T(8,128)} %fusion.6, bf16[2048,128]{1,0:T(8,128)(2,1)S(1)} %copy-done.8, bf16[2048,128]{1,0:T(8,128)(2,1)S(1)} %bitcast.228, bf16[2048,128]{1,0:T(8,128)(2,1)} %bitcast.233, bf16[2048,512]{1,0:T(8,128)(2,1)S(1)} %copy-done.5, bf16[2048,6]{1,0:T(8,128)(2,1)S(1)} %copy-done.29, ...), kind=kOutput, calls=%fused_computation.3 | convolution fusion | flops 7553941504 | bytes 32006144 | tf_op jit(solution)/shard_map/dot_general | solution.py:73
  975.4 32.8 %all-reduce.8.cloned.1.call-done = bf16[4,4,2,64,1024]{4,3,2,0,1:T(8,128)(2,1)} async-done(((bf16[4,4,2,64,1024]{4,3,2,0,1:T(8,128)(2,1)}), bf16[4,4,2,64,1024]{4,3,2,0,1:T(8,128)(2,1)}) %all-reduce.8.cloned.1.call-update) | async-done | bytes 4194320
  1011.0 12.1 all-to-all-done.7
  1027.6 10.5 convolution_convert_fusion.4
  1045.8 46.4 %dynamic_update_slice.17 = bf16[2048,2,2,128]{3,2,1,0:T(2,128)(2,1)} dynamic-update-slice(bf16[2048,2,2,128]{3,2,1,0:T(2,128)(2,1)} %broadcast_in_dim.85, bf16[2048,2,1,128]{3,2,1,0:T(2,128)(2,1)S(1)} %copy.122, s32[]{:T(128)} %constant.97.clone.1, s32[]{:T(128)} %constant.97.clone.1, s32[]{:T(128)S(6)} %select_n.48, s32[]{:T(128)} %constant.97.clone.1) | dynamic-update-slice | bytes 2097156 | tf_op jit(solution)/shard_map/dynamic_update_slice | solution.py:745
  1138.8 85.5 %all-to-all-done.6 = bf16[32,64,1072]{2,1,0:T(8,128)(2,1)} async-done(((bf16[32,64,1072]{2,1,0:T(8,128)(2,1)}), bf16[32,64,1072]{2,1,0:T(8,128)(2,1)}, u32[]{:S(2)}, u32[]{:S(2)}) %all-to-all-start.6) | async-done | bytes 4390944 | tf_op jit(solution)/shard_map/all_to_all | solution.py:758
  1234.5 17.0 %all-to-all-done.5 = bf16[8,64,896]{2,1,0:T(8,128)(2,1)S(1)} async-done(((bf16[8,64,896]{2,1,0:T(8,128)(2,1)}), bf16[8,64,896]{2,1,0:T(8,128)(2,1)S(1)}, u32[]{:S(2)}, u32[]{:S(2)}) %all-to-all-start.5) | async-done | bytes 917536 | tf_op jit(solution)/shard_map/all_to_all | solution.py:736
  (319 shorter events, 233.2 us)
Async XLA Ops:
  8.0 66.0 %copy-start = (f32[3,48]{1,0:T(4,128)S(1)}, f32[3,48]{1,0:T(4,128)}, u32[]{:S(2)}) copy-start(f32[3,48]{1,0:T(4,128)} %param.23) | copy-start | bytes 1732
  8.0 101.2 %all-gather.12.cloned.1.call-start = ((), (), s32[]{:S(2)}) async-start(), calls=%async_computation.18 | async-start | bytes 4866048 | tf_op jit(solution)/shard_map/all_gather | solution.py:524
  13.0 160.5 %all-gather.10.cloned.1.call-start = ((), (), s32[]{:S(2)}) async-start(), calls=%async_computation.17 | async-start | bytes 9437184 | tf_op jit(solution)/shard_map/all_gather | solution.py:517
  13.8 208.3 %all-gather.14.cloned.1.call-start = ((), (), s32[]{:S(2)}) async-start(), calls=%async_computation.19 | async-start | bytes 4587520 | tf_op jit(solution)/shard_map/all_gather | solution.py:564
  54.1 15.2 %all-to-all-start.1 = ((bf16[4,128,512]{2,1,0:T(8,128)(2,1)}), bf16[4,128,512]{2,1,0:T(8,128)(2,1)S(1)}, u32[]{:S(2)}, u32[]{:S(2)}) async-start(bf16[4,128,512]{2,1,0:T(8,128)(2,1)} %copy.116), calls=%async_computation.1 | async-start | bytes 1048576 | tf_op jit(solution)/shard_map/all_to_all | solution.py:574
  70.4 37.8 %all-to-all-start.2 = ((bf16[8,128,512]{2,1,0:T(8,128)(2,1)}), bf16[8,128,512]{2,1,0:T(8,128)(2,1)S(1)}, u32[]{:S(2)}, u32[]{:S(2)}) async-start(bf16[8,128,512]{2,1,0:T(8,128)(2,1)} %bitcast_select_fusion), calls=%async_computation.2 | async-start | bytes 2097152 | tf_op jit(solution)/shard_map/all_to_all | solution.py:578
  74.0 200.0 %all-gather.16.cloned.1.call-start = ((), (), s32[]{:S(2)}) async-start(), calls=%async_computation.20 | async-start | bytes 2621440 | tf_op jit(solution)/shard_map/all_gather | solution.py:583
  109.1 332.3 %reduce-scatter.11.cloned.1.call-start = ((), (), s32[]{:S(2)}) async-start(), calls=%async_computation.21 | async-start | bytes 9437184 | tf_op jit(solution)/shard_map/reduce_scatter | solution.py:625
  115.7 62.9 %copy-start.35 = (f32[2048]{0:T(1024)}, f32[2048]{0:T(1024)S(1)}, u32[]{:S(2)}) copy-start(f32[2048]{0:T(1024)S(1)} %get-tuple-element.130) | copy-start | bytes 24580
  115.7 589.8 %copy-start.32 = (f32[2048]{0:T(1024)}, f32[2048]{0:T(1024)S(1)}, u32[]{:S(2)}) copy-start(f32[2048]{0:T(1024)S(1)} %get-tuple-element.131) | copy-start | bytes 24580
  124.4 63.8 %copy-start.24 = (bf16[2048,256]{1,0:T(8,128)(2,1)}, bf16[2048,256]{1,0:T(8,128)(2,1)S(1)}, u32[]{:S(2)}) copy-start(bf16[2048,256]{1,0:T(8,128)(2,1)S(1)} %copy.112) | copy-start | bytes 3145732
  284.0 165.2 %all-gather.20.cloned.1.call-start = ((), (), s32[]{:S(2)}) async-start(), calls=%async_computation.23 | async-start | bytes 5242880 | tf_op jit(solution)/shard_map/all_gather | solution.py:590
  311.4 189.1 %all-gather.18.cloned.1.call-start = ((), (), s32[]{:S(2)}) async-start(), calls=%async_computation.22 | async-start | bytes 9437184 | tf_op jit(solution)/shard_map/all_gather | solution.py:632
  311.6 394.0 %copy-start.39 = (f32[256]{0:T(256)}, f32[256]{0:T(256)S(1)}, u32[]{:S(2)}) copy-start(f32[256]{0:T(256)S(1)} %get-tuple-element.165) | copy-start | bytes 3076
  444.1 261.4 %copy-start.41 = (f32[256]{0:T(256)}, f32[256]{0:T(256)S(1)}, u32[]{:S(2)}) copy-start(f32[256]{0:T(256)S(1)} %bitcast_rsqrt_fusion.1) | copy-start | bytes 3076
  447.9 99.6 %all-gather.22.cloned.1.call-start = ((), (), s32[]{:S(2)}) async-start(), calls=%async_computation.24 | async-start | bytes 2621440 | tf_op jit(solution)/shard_map/all_gather | solution.py:591
  448.4 154.6 %all-gather.24.cloned.1.call-start = ((), (), s32[]{:S(2)}) async-start(), calls=%async_computation.26 | async-start | bytes 9437184 | tf_op jit(solution)/shard_map/all_gather | solution.py:634
  449.2 252.8 %reduce-scatter.15.cloned.1.call-start = ((), (), s32[]{:S(2)}) async-start(), calls=%async_computation.27 | async-start | bytes 9437184 | tf_op jit(solution)/shard_map/reduce_scatter | solution.py:648
  630.7 160.4 %all-gather.26.cloned.1.call-start = ((), (), s32[]{:S(2)}) async-start(), calls=%async_computation.28 | async-start | bytes 9437184 | tf_op jit(solution)/shard_map/all_gather | solution.py:652
  705.6 95.2 %copy-start.44 = (f32[256]{0:T(256)}, f32[256]{0:T(256)S(1)}, u32[]{:S(2)}) copy-start(f32[256]{0:T(256)S(1)} %multiply_multiply_fusion) | copy-start | bytes 3076
  708.8 257.8 %reduce-scatter.21.cloned.1.call-start = ((), (), s32[]{:S(2)}) async-start(), calls=%async_computation.31 | async-start | bytes 2621440 | tf_op jit(solution)/shard_map/reduce_scatter | solution.py:673
  800.8 207.3 %all-reduce.8.cloned.1.call-start = ((), (), s32[]{:S(2)}) async-start(), calls=%async_computation.33 | async-start | bytes 8388608
  815.0 312.4 %reduce-scatter.23.cloned.1.call-start = ((), (), s32[]{:S(2)}) async-start(), calls=%async_computation.32 | async-start | bytes 2621440 | tf_op jit(solution)/shard_map/reduce_scatter | solution.py:668
  833.3 305.4 %reduce-scatter.19.cloned.1.call-start = ((), (), s32[]{:S(2)}) async-start(), calls=%async_computation.30 | async-start | bytes 4587520 | tf_op jit(solution)/shard_map/reduce_scatter | solution.py:735
  934.8 319.3 %reduce-scatter.17.cloned.1.call-start = ((), (), s32[]{:S(2)}) async-start(), calls=%async_computation.29 | async-start | bytes 9437184 | tf_op jit(solution)/shard_map/reduce_scatter | solution.py:725
  970.5 52.7 %all-to-all-start.7 = ((bf16[8,128,512]{2,1,0:T(8,128)(2,1)}), bf16[8,128,512]{2,1,0:T(8,128)(2,1)}, u32[]{:S(2)}, u32[]{:S(2)}) async-start(bf16[8,128,512]{2,1,0:T(8,128)(2,1)} %maximum_dynamic-update-slice_fusion), calls=%async_computation.13 | async-start | bytes 2097152 | tf_op jit(solution)/shard_map/all_to_all | solution.py:687
  1023.2 77.3 %all-to-all-start.9 = ((bf16[8,64,1024]{2,1,0:T(8,128)(2,1)}), bf16[8,64,1024]{2,1,0:T(8,128)(2,1)}, u32[]{:S(2)}, u32[]{:S(2)}) async-start(bf16[8,64,1024]{2,1,0:T(8,128)(2,1)} %bitcast.206), calls=%async_computation.15 | async-start | bytes 2097152 | tf_op jit(solution)/shard_map/all_to_all | solution.py:658
  1100.5 13.1 %all-to-all-start.8 = ((bf16[4,128,512]{2,1,0:T(8,128)(2,1)}), bf16[4,128,512]{2,1,0:T(8,128)(2,1)S(1)}, u32[]{:S(2)}, u32[]{:S(2)}) async-start(bf16[4,128,512]{2,1,0:T(8,128)(2,1)} %dynamic-slice_bitcast_fusion), calls=%async_computation.14 | async-start | bytes 1048576 | tf_op jit(solution)/shard_map/all_to_all | solution.py:690
  1113.6 110.7 %all-to-all-start.6 = ((bf16[32,64,1072]{2,1,0:T(8,128)(2,1)}), bf16[32,64,1072]{2,1,0:T(8,128)(2,1)}, u32[]{:S(2)}, u32[]{:S(2)}) async-start(bf16[32,64,1072]{2,1,0:T(8,128)(2,1)} %pad_maximum_fusion.1), calls=%async_computation.11 | async-start | bytes 9437184 | tf_op jit(solution)/shard_map/all_to_all | solution.py:758
  1118.0 142.1 %reduce-scatter.13.cloned.1.call-start = ((), (), s32[]{:S(2)}) async-start(), calls=%async_computation.25 | async-start | bytes 9437184 | tf_op jit(solution)/shard_map/reduce_scatter | solution.py:641
  1224.3 27.3 %all-to-all-start.5 = ((bf16[8,64,896]{2,1,0:T(8,128)(2,1)}), bf16[8,64,896]{2,1,0:T(8,128)(2,1)S(1)}, u32[]{:S(2)}, u32[]{:S(2)}) async-start(bf16[8,64,896]{2,1,0:T(8,128)(2,1)} %bitcast.225), calls=%async_computation.10 | async-start | bytes 1835008 | tf_op jit(solution)/shard_map/all_to_all | solution.py:736
  1257.5 10.6 all-to-all-start.4
  (50 other events, 520.9 us)
Sparse Core Ops, SparseCore 0:
  13.2 73.4 all-gather.11
  88.3 85.2 all-gather.9
  175.4 46.6 all-gather.13
  224.4 35.1 all-gather.15
  284.1 157.1 reduce-scatter.10
  709.0 82.0 all-gather.25
  801.0 33.7 reduce-scatter.20
  837.0 87.4 reduce-scatter.22
  934.9 47.2 reduce-scatter.18
  984.5 104.3 reduce-scatter.16
  1126.8 91.8 reduce-scatter.12
Sparse Core Ops, SparseCore 1:
  311.5 116.3 all-gather.19
  447.9 52.5 all-gather.17
  501.9 45.5 all-gather.21
  550.0 53.0 all-gather.23
  630.8 71.1 reduce-scatter.14
  815.1 193.0 all-reduce.7

commit v2 on v1

v2 whole, which is shorter than its diff:
```python
import functools
import math

import jax
import jax.numpy as jnp
from jax import lax
from jax.experimental import pallas as pl
from jax.experimental.pallas import tpu as pltpu
from jax.sharding import Mesh
from jax.sharding import PartitionSpec as P

HQ = 8
KV = 2
HD = 128
MH = 48
MP = 64
NS = 256
KW = 4
MI = MH * MP

epsilon = 1e-05
rope_base = 100000000000.0
neg_big = -1e30
highest = lax.Precision.HIGHEST
bf16 = jnp.bfloat16
f32 = jnp.float32

ALL = ("dp", "g", "z", "c")
TEAM = ("z", "c")
PLANE = ("dp", "c")
LINE = ("g", "z")
SEQ = ("g", "z", "c")
SPREAD = ("dp", "g")


def rms_norm(values, gain):
    return values * lax.rsqrt(jnp.mean(values * values, -1, keepdims=True) + epsilon) * gain


def rope_tables(positions, head_size):
    half = head_size // 2
    freq = jnp.exp(jnp.arange(half, dtype=f32) * (-2.0 * math.log(rope_base) / head_size))
    angle = positions.astype(f32)[:, None] * freq[None, :]
    return (
        jnp.concatenate([jnp.cos(angle), jnp.cos(angle)], -1),
        jnp.concatenate([jnp.sin(angle), jnp.sin(angle)], -1),
    )


def rotate(values, cosine, sine):
    half = values.shape[-1] // 2
    turned = jnp.concatenate([-values[..., half:], values[..., :half]], -1)
    return values * cosine + turned * sine


def rotate_back(grads, cosine, sine):
    half = grads.shape[-1] // 2
    scaled = grads * sine
    return grads * cosine + jnp.concatenate([scaled[..., half:], -scaled[..., :half]], -1)


def dot(left, right, precision=None):
    return jnp.dot(left, right, preferred_element_type=f32, precision=precision)


def dot_first(left, right, precision=None):
    return lax.dot_general(
        left, right, (((0,), (0,)), ((), ())), preferred_element_type=f32, precision=precision
    )


def dot_last(left, right, precision=None):
    return lax.dot_general(
        left, right, (((1,), (1,)), ((), ())), preferred_element_type=f32, precision=precision
    )


def sigmoid(v):
    return 1.0 / (1.0 + jnp.exp(-v))


def softplus(v):
    return jnp.maximum(v, 0.0) + jnp.log(1.0 + jnp.exp(-jnp.abs(v)))


def cost(rows, gigaflops, arrays):
    return pl.CostEstimate(
        flops=int(rows * gigaflops * 1e9 / 2048),
        bytes_accessed=sum(a.size * a.dtype.itemsize for a in arrays),
        transcendentals=0,
    )


def params(count):
    return pltpu.CompilerParams(
        dimension_semantics=("arbitrary",) * count, vmem_limit_bytes=48 * 1024 * 1024
    )


def after(value, *others):
    return lax.optimization_barrier((value, *others))[0]


def assemble(scalars, sources, shapes, plan, count, name):
    def kernel(scalar_ref, *refs):
        sems = refs[-1]
        plan(scalar_ref, refs[: len(sources)], refs[len(sources) : -1], sems)

    anywhere = pl.BlockSpec(memory_space=pl.ANY)
    return pl.pallas_call(
        kernel,
        in_specs=[pl.BlockSpec(memory_space=pltpu.SMEM)] + [anywhere] * len(sources),
        out_specs=[pl.BlockSpec(memory_space=pltpu.VMEM)] * len(shapes),
        out_shape=[jax.ShapeDtypeStruct(shape, bf16) for shape in shapes],
        scratch_shapes=[pltpu.SemaphoreType.DMA((count,))],
        compiler_params=pltpu.CompilerParams(vmem_limit_bytes=48 * 1024 * 1024),
        cost_estimate=pl.CostEstimate(
            flops=0, bytes_accessed=4 * sum(math.prod(shape) for shape in shapes), transcendentals=0
        ),
        name=name,
    )(jnp.stack([jnp.asarray(v, jnp.int32) for v in scalars]), *sources)


def run_copies(pairs, sems):
    copies = [pltpu.make_async_copy(a, b, sems.at[i]) for i, (a, b) in enumerate(pairs)]
    for copy in copies:
        copy.start()
    for copy in copies:
        copy.wait()


def join_weights(blocks, others, inner, key_at, shared, kv_head):
    peers, here = lax.axis_size("dp"), lax.axis_index("dp")
    size = sum(part.shape[0] for part, k, _ in blocks if k == 0)
    width = size * peers
    own = inner + key_at
    keys_size = 2 * KV * HD
    many = len(blocks)

    def plan(scalar_ref, sources, outs, sems):
        early, late, rest = outs

        def pairs(turned):
            moves = []
            for i, (part, k, first) in enumerate(blocks):
                rows = part.shape[0]
                at = pl.ds(pl.multiple_of(scalar_ref[k] * size + first, rows), rows)
                source = sources[i]
                near, far = source.at[:, pl.ds(own, shared)], sources[many + i]
                steps, keys = (far, near) if turned else (near, far)
                moves.append((source.at[:, pl.ds(0, key_at)], early.at[at, pl.ds(0, key_at)]))
                moves.append((source.at[:, pl.ds(key_at, inner)], late.at[at, pl.ds(0, inner)]))
                moves.append((steps, late.at[at, pl.ds(inner, shared)]))
                for j in range(2):
                    lane = (j * KV + scalar_ref[peers]) * HD
                    if not turned:
                        keys_at = pl.multiple_of(lane, HD)
                        key_view = keys.at[:, pl.ds(keys_at, HD)]
                    else:
                        key_view = source.at[:, pl.ds(pl.multiple_of(own + lane, HD), HD)]
                    moves.append((key_view, early.at[at, pl.ds(key_at + j * HD, HD)]))
                tail = far if not turned else source
                tail_at = keys_size if not turned else own + keys_size
                moves.append((tail.at[:, pl.ds(tail_at, 128)], rest.at[at, :]))
            return moves

        @pl.when(scalar_ref[peers + 1] == 0)
        def _():
            run_copies(pairs(False), sems)

        @pl.when(scalar_ref[peers + 1] != 0)
        def _():
            run_copies(pairs(True), sems)

    scalars = [here ^ k for k in range(peers)] + [kv_head, lax.axis_index("c")]
    shapes = [(width, key_at + 2 * HD), (width, inner + shared), (width, shared - keys_size)]
    sources = [part for part, _, _ in blocks] + others
    return assemble(scalars, sources, shapes, plan, 6 * many, "join_weights")


def join_hidden(gathered, count, held, dp, width):
    line, _, columns = gathered.shape
    low = count * held
    rows = (gathered.shape[1] - low) * columns // width
    folds = width // columns

    def plan(scalar_ref, sources, outs, sems):
        moves = [
            (
                sources[0].at[:, pl.ds(i * held, held)],
                outs[0].at[scalar_ref[i], :, scalar_ref[count + i]],
            )
            for i in range(count)
        ]
        for i in range(folds):
            moves.append(
                (
                    sources[0].at[:, pl.ds(low + i * rows, rows)],
                    outs[1].at[:, :, pl.ds(i * columns, columns)],
                )
            )
        run_copies(moves, sems)

    near, core = lax.axis_index("dp"), lax.axis_index("c")
    scalars = [near ^ (i % dp) for i in range(count)] + [core ^ (i // dp) for i in range(count)]
    shapes = [(dp, line, count // dp, held, columns), (line, rows, width)]
    return assemble(scalars, [gathered], shapes, plan, count + folds, "join_hidden")


def join_rows(slots, place):
    count, rows, width = len(slots), *slots[0].shape

    def plan(scalar_ref, sources, outs, sems):
        run_copies([(sources[k], outs[0].at[scalar_ref[k]]) for k in range(count)], sems)

    scalars = [place ^ k for k in range(count)]
    whole = assemble(scalars, slots, [(count, rows, width)], plan, count, "join_rows")[0]
    return whole.reshape(count * rows, width)


def join_columns(pieces):
    peers, here = lax.axis_size("dp"), lax.axis_index("dp")
    rows, cut = pieces[0].shape

    def plan(scalar_ref, sources, outs, sems):
        run_copies(
            [
                (sources[k], outs[0].at[:, pl.ds(pl.multiple_of(scalar_ref[k] * cut, cut), cut)])
                for k in range(peers)
            ],
            sems,
        )

    scalars = [here ^ k for k in range(peers)]
    return assemble(scalars, pieces, [(rows, cut * peers)], plan, peers, "join_columns")[0]


def join_out(blocks, place, attn_rows, mamba_rows):
    peers, here = lax.axis_size("dp"), lax.axis_index("dp")
    parts, rows, cut = blocks[0].shape

    def plan(scalar_ref, sources, outs, sems):
        moves = []
        for k in range(peers):
            lane = pl.ds(pl.multiple_of(scalar_ref[k] * cut, cut), cut)
            for i in range(parts):
                at = scalar_ref[peers + i]
                low = pl.multiple_of(at * mamba_rows, 16)
                high = pl.multiple_of(parts * mamba_rows + at * attn_rows, 16)
                moves.append(
                    (
                        sources[k].at[i, pl.ds(attn_rows, mamba_rows)],
                        outs[0].at[pl.ds(low, mamba_rows), lane],
                    )
                )
                moves.append(
                    (
                        sources[k].at[i, pl.ds(0, attn_rows)],
                        outs[0].at[pl.ds(high, attn_rows), lane],
                    )
                )
        run_copies(moves, sems)

    scalars = [here ^ k for k in range(peers)] + [place ^ i for i in range(parts)]
    shape = (parts * rows, cut * peers)
    return assemble(scalars, blocks, [shape], plan, 2 * peers * parts, "join_out")[0]


def swap(block, axis, distance):
    return lax.ppermute(block, axis, [(i, i ^ distance) for i in range(lax.axis_size(axis))])


def gather_plane(block):
    near = [block] + [swap(block, "dp", k) for k in range(1, lax.axis_size("dp"))]
    return jnp.concatenate(near + [swap(piece, "c", 1) for piece in near], axis=0)


def scatter_core(partial):
    half = partial.shape[0] // 2
    near = partial[:half].astype(f32) + swap(partial[half:], "c", 1).astype(f32)
    return near.astype(bf16)


def scatter_near(near):
    near = jnp.split(near, lax.axis_size("dp"), axis=0)
    return sum(
        (swap(near[k], "dp", k) if k else near[k]).astype(f32) for k in range(len(near))
    )


def scatter_plane(partial):
    return scatter_near(scatter_core(partial))


def from_dp(block):
    return [block] + [swap(block, "dp", k) for k in range(1, lax.axis_size("dp"))]


def parts_dp(block):
    if lax.axis_size("dp") != 4:
        return [(part, k, 0) for k, part in enumerate(from_dp(block))]
    half = block.shape[0] // 2
    one, two = swap(block, "dp", 1), swap(block, "dp", 2)
    top, bottom = swap(one[:half], "dp", 2), swap(two[half:], "dp", 1)
    return [(block, 0, 0), (one, 1, 0), (two, 2, 0), (top, 3, 0), (bottom, 3, half)]


def cuts_dp(partial, axis):
    peers, here = lax.axis_size("dp"), lax.axis_index("dp")
    size = partial.shape[axis] // peers
    return [lax.dynamic_slice_in_dim(partial, (here ^ k) * size, size, axis) for k in range(peers)]


def sum_cuts(cuts):
    return sum((swap(cut, "dp", k) if k else cut).astype(f32) for k, cut in enumerate(cuts))


def scatter_dp(partial, axis):
    return sum_cuts(cuts_dp(partial, axis))


def attend_mask(length_ref, start_ref, seq, block, width, first):
    qpos = start_ref[0] + first + lax.broadcasted_iota(jnp.int32, (block, width), 0)
    kpos = lax.broadcasted_iota(jnp.int32, (block, width), 1)
    return (kpos <= qpos) & (kpos < length_ref[seq])


def attend_fore_kernel(
    length_ref, start_ref, q_ref, k_ref, v_ref, o_ref, log_ref, *, scale, block, seq
):
    at = pl.program_id(0)
    keys = k_ref[0]
    scores = dot_last(q_ref[0], keys) * scale
    allowed = attend_mask(length_ref, start_ref, seq, block, keys.shape[0], at * block)
    scores = jnp.where(allowed, scores, neg_big)
    top = jnp.max(scores, -1, keepdims=True)
    expo = jnp.exp(scores - top)
    total = jnp.sum(expo, -1, keepdims=True)
    prob = (expo * (1.0 / total)).astype(bf16)
    o_ref[0] = dot(prob, v_ref[0]).astype(bf16)
    log_ref[0] = jnp.broadcast_to(top + jnp.log(total), log_ref.shape[1:])


def attend_fore(length, start, q, k, v, block, seq):
    _, rows, width = q.shape
    kernel = functools.partial(
        attend_fore_kernel, scale=1.0 / math.sqrt(HD), block=block, seq=seq
    )
    qspec = pl.BlockSpec((1, block, width), lambda i: (seq, i, 0))
    ospec = pl.BlockSpec((1, block, width), lambda i: (0, i, 0))
    kspec = pl.BlockSpec((1, k.shape[1], width), lambda i: (seq, 0, 0))
    smem = pl.BlockSpec(memory_space=pltpu.SMEM)
    return pl.pallas_call(
        kernel,
        grid=(rows // block,),
        in_specs=[smem, smem, qspec, kspec, kspec],
        out_specs=[ospec, ospec],
        out_shape=[
            jax.ShapeDtypeStruct((1, rows, width), bf16),
            jax.ShapeDtypeStruct((1, rows, width), f32),
        ],
        compiler_params=params(1),
        cost_estimate=cost(rows, 7, (q, k, v)),
        name="attend_fore",
    )(length, start, q, k, v)


def attend_back_kernel(
    length_ref, start_ref, q_ref, k_ref, v_ref, do_ref, log_ref, dq_ref, dk_ref, dv_ref,
    *, scale, block, seq,
):
    at = pl.program_id(0)

    @pl.when(at == 0)
    def _():
        dk_ref[...] = jnp.zeros_like(dk_ref)
        dv_ref[...] = jnp.zeros_like(dv_ref)

    keys = k_ref[0]
    queries = q_ref[0]
    grad_out = do_ref[0].astype(bf16)
    scores = dot_last(queries, keys) * scale
    allowed = attend_mask(length_ref, start_ref, seq, block, keys.shape[0], at * block)
    scores = jnp.where(allowed, scores, neg_big)
    prob = jnp.exp(scores - log_ref[0][:, :1])
    grad_prob = dot_last(grad_out, v_ref[0])
    centre = jnp.sum(prob * grad_prob, -1, keepdims=True)
    grad_score = (prob * (grad_prob - centre)).astype(bf16)
    dq_ref[0] = dot(grad_score, keys) * scale
    dk_ref[0] += dot_first(grad_score, queries) * scale
    dv_ref[0] += dot_first(prob.astype(bf16), grad_out)


def attend_back(length, start, q, k, v, grad_out, logs, block, seq):
    _, rows, width = q.shape
    out_at = grad_out.shape[1] // width - 1
    kernel = functools.partial(
        attend_back_kernel, scale=1.0 / math.sqrt(HD), block=block, seq=seq
    )
    qspec = pl.BlockSpec((1, block, width), lambda i: (seq, i, 0))
    ospec = pl.BlockSpec((1, block, width), lambda i: (0, i, 0))
    kspec = pl.BlockSpec((1, k.shape[1], width), lambda i: (seq, 0, 0))
    gspec = pl.BlockSpec((1, k.shape[1], width), lambda i: (0, 0, 0))
    smem = pl.BlockSpec(memory_space=pltpu.SMEM)
    return pl.pallas_call(
        kernel,
        grid=(rows // block,),
        in_specs=[
            smem,
            smem,
            qspec,
            kspec,
            kspec,
            pl.BlockSpec((1, block, width), lambda i: (0, i, out_at)),
            ospec,
        ],
        out_specs=[ospec, gspec, gspec],
        out_shape=[
            jax.ShapeDtypeStruct((1, rows, width), f32),
            jax.ShapeDtypeStruct((1, *k.shape[1:]), f32),
            jax.ShapeDtypeStruct((1, *k.shape[1:]), f32),
        ],
        compiler_params=params(1),
        cost_estimate=cost(rows, 11, (q, k, v, logs)),
        name="attend_back",
    )(length, start, q, k, v, grad_out[None], logs)


def head_spread(heads):
    row = lax.broadcasted_iota(jnp.int32, (128, heads * MP), 0)
    col = lax.broadcasted_iota(jnp.int32, (128, heads * MP), 1)
    return (row == col // MP).astype(f32)


def triangle(span):
    row = lax.broadcasted_iota(jnp.int32, (span, span), 0)
    col = lax.broadcasted_iota(jnp.int32, (span, span), 1)
    return row >= col


def conv_pre(ext_ref, conv_ref, span):
    total = conv_ref[KW : KW + 1, :]
    for k in range(KW):
        total = total + conv_ref[k : k + 1, :] * ext_ref[pl.ds(8 - (KW - 1) + k, span), :]
    return total


def core_fore_kernel(
    turn_ref, x_ref, bc_ref, z_ref, dt_ref, halo_ref, conv_ref, head_ref, init_ref,
    gated_ref, y_ref, enter_ref, final_ref, decay_ref,
    ext, state, total, *, heads, span,
):
    inner = heads * MP
    at = pl.program_id(0)

    @pl.when(at == 0)
    def _():
        ext[0:8, :] = halo_ref[0]
        state[...] = init_ref[0]
        total[...] = jnp.zeros_like(total)

    ext[8:, :inner] = x_ref[...]
    ext[8:, inner:] = bc_ref[...]
    pre = conv_pre(ext, conv_ref, span)
    ext[0:8, :] = ext[span : span + 8, :]
    cv = pre * sigmoid(pre)
    xs = cv[:, :inner]
    bmat = cv[:, inner : inner + NS].astype(bf16)
    cmat = cv[:, inner + NS :].astype(bf16)
    spread = head_spread(heads)
    lower = triangle(span)
    step = softplus(pltpu.roll(dt_ref[...], 128 - turn_ref[0], 1) + head_ref[0:1, :])
    decay_log = -jnp.exp(head_ref[1:2, :]) * step
    cum = dot(lower.astype(f32), decay_log, highest)
    cum_t = cum.T
    step_t = step.T
    last = cum[span - 1 : span, :]
    enter = state[...]
    enter_ref[0, 0] = enter
    pair = dot_last(cmat, bmat)
    xb = xs.astype(bf16)
    parts = []
    for h in range(heads):
        diff = cum[:, h : h + 1] - cum_t[h : h + 1, :]
        decay = jnp.exp(jnp.where(lower, diff, neg_big))
        mixing = (pair * decay * step_t[h : h + 1, :]).astype(bf16)
        parts.append(dot(mixing, xb[:, h * MP : (h + 1) * MP]))
    y = jnp.concatenate(parts, axis=1)
    y = y + dot_last(cmat, enter.astype(bf16)) * dot(jnp.exp(cum), spread, highest)
    y = y + xs * dot(jnp.broadcast_to(head_ref[2:3, :], (8, 128)), spread, highest)[0:1, :]
    tail = dot(jnp.exp(last - cum) * step, spread, highest)
    keep = jnp.broadcast_to(jnp.exp(cum_t[:, span - 1 : span]), (128, NS))
    new_state = dot_first(spread, keep, highest) * enter + dot_first((xs * tail).astype(bf16), bmat)
    state[...] = new_state
    final_ref[0] = new_state
    total[...] = total[...] + last
    decay_ref[0] = total[...]
    z = z_ref[...]
    y_ref[...] = y
    gated_ref[...] = (y * (z * sigmoid(z))).astype(bf16)


def core_fore(turn, early, late, halo, conv, head, init, seq, rows, heads, span):
    inner = heads * MP
    wide = inner + 2 * NS
    count = rows // span
    first = seq * count

    def block(width, at):
        return pl.BlockSpec((span, width), lambda i: (first + i, at))

    def whole(*shape):
        return pl.BlockSpec(shape, lambda i: (0,) * len(shape))

    out = pl.BlockSpec((span, inner), lambda i: (i, 0))
    return pl.pallas_call(
        functools.partial(core_fore_kernel, heads=heads, span=span),
        grid=(count,),
        in_specs=[
            pl.BlockSpec(memory_space=pltpu.SMEM),
            block(inner, 0),
            block(2 * NS, (inner + 128) // (2 * NS)),
            block(inner, 0),
            block(128, inner // 128),
            whole(1, 8, wide),
            whole(8, wide),
            whole(8, 128),
            whole(1, inner, NS),
        ],
        out_specs=[
            out,
            out,
            pl.BlockSpec((1, 1, inner, NS), lambda i: (0, i, 0, 0)),
            whole(1, inner, NS),
            whole(1, 8, 128),
        ],
        out_shape=[
            jax.ShapeDtypeStruct((rows, inner), bf16),
            jax.ShapeDtypeStruct((rows, inner), f32),
            jax.ShapeDtypeStruct((1, count, inner, NS), f32),
            jax.ShapeDtypeStruct((1, inner, NS), f32),
            jax.ShapeDtypeStruct((1, 8, 128), f32),
        ],
        scratch_shapes=[
            pltpu.VMEM((span + 8, wide), f32),
            pltpu.VMEM((inner, NS), f32),
            pltpu.VMEM((8, 128), f32),
        ],
        compiler_params=params(1),
        cost_estimate=cost(rows, 26, (late, init)),
        name="core_fore",
    )(turn, late, late, early, late, halo, conv, head, init)


def core_back_kernel(
    turn_ref, x_ref, bc_ref, z_ref, dt_ref, dg_ref, enter_ref, halo_ref, conv_ref, head_ref, exit_ref,
    dlate_ref, gconv_ref, ghead_ref, dinit_ref, dfirst_ref,
    ext, dext, dstate, *, heads, span,
):
    inner = heads * MP
    at = pl.program_id(0)

    @pl.when(at == 0)
    def _():
        gconv_ref[...] = jnp.zeros_like(gconv_ref)
        ghead_ref[...] = jnp.zeros_like(ghead_ref)

    @pl.when(at == 0)
    def _():
        dext[span:, :] = jnp.zeros((8, dext.shape[1]), f32)
        dstate[...] = exit_ref[0]

    ext[0:8, :] = halo_ref[0, 0]
    ext[8:, :inner] = x_ref[...]
    ext[8:, inner:] = bc_ref[...]
    pre = conv_pre(ext, conv_ref, span)
    gate = sigmoid(pre)
    cv = pre * gate
    xs = cv[:, :inner]
    bmat = cv[:, inner : inner + NS].astype(bf16)
    cmat = cv[:, inner + NS :].astype(bf16)
    xb = xs.astype(bf16)
    z = z_ref[...]
    dy = dg_ref[...] * (z * sigmoid(z))
    dyb = dy.astype(bf16)
    spread = head_spread(heads)
    lower = triangle(span)
    raw = pltpu.roll(dt_ref[...], 128 - turn_ref[0], 1) + head_ref[0:1, :]
    step = softplus(raw)
    rate = -jnp.exp(head_ref[1:2, :])
    decay_log = rate * step
    cum = dot(lower.astype(f32), decay_log, highest)
    cum_t = cum.T
    step_t = step.T
    last = cum[span - 1 : span, :]
    enter = enter_ref[0, 0]
    leave = dstate[...]
    pair = dot_last(cmat, bmat)
    dpair = jnp.zeros((span, span), f32)
    lane = lax.broadcasted_iota(jnp.int32, (span, 128), 1)
    line = lax.broadcasted_iota(jnp.int32, (128, span), 0)
    row_sums = jnp.zeros((span, 128), f32)
    col_sums = jnp.zeros((128, span), f32)
    parts = []
    for h in range(heads):
        diff = cum[:, h : h + 1] - cum_t[h : h + 1, :]
        decay = jnp.exp(jnp.where(lower, diff, neg_big))
        now = step_t[h : h + 1, :]
        cut = slice(h * MP, (h + 1) * MP)
        dmix = dot_last(dyb[:, cut], xb[:, cut]) * decay
        both = dmix * pair
        dmix_now = dmix * now
        dpair = dpair + dmix_now
        row_sums = jnp.where(lane == h, jnp.sum(both * now, 1, keepdims=True), row_sums)
        col_sums = jnp.where(line == h, jnp.sum(both, 0, keepdims=True), col_sums)
        mixing = (pair * decay * now).astype(bf16)
        parts.append(dot_first(mixing, dyb[:, cut]))
    dxs = jnp.concatenate(parts, axis=1)
    dstep = col_sums.T
    dcum = row_sums - dstep * step
    dpb = dpair.astype(bf16)
    dcm = dot(dpb, bmat)
    dbm = dot_first(dpb, cmat)
    grown = dot(jnp.exp(cum), spread, highest)
    enter_b = enter.astype(bf16)
    leave_b = leave.astype(bf16)
    dgrown = (dy * grown).astype(bf16)
    dcum = dcum + dot_last(dy * dot_last(cmat, enter_b) * grown, spread, highest)
    dcm = dcm + dot(dgrown, enter_b)
    fade = jnp.exp(last - cum)
    tail = dot(fade * step, spread, highest)
    into = dot_last(bmat, leave_b)
    dxs = dxs + into * tail
    owed = dot_last(xs * into, spread, highest) * fade
    dstep = dstep + owed
    owed = owed * step
    dcum = dcum - owed
    dbm = dbm + dot((xs * tail).astype(bf16), leave_b)
    held = dot(spread, enter * leave, highest)
    held = dot_last(jnp.ones((8, NS), f32), held, highest)[0:1, :]
    dlast = jnp.sum(owed, 0, keepdims=True) + jnp.exp(last) * held
    keep = jnp.broadcast_to(jnp.exp(cum_t[:, span - 1 : span]), (128, NS))
    new_dstate = dot_first(spread, keep, highest) * leave + dot_first(dgrown, cmat)
    dstate[...] = new_dstate
    dinit_ref[0] = new_dstate
    dlog = dot_first(lower.astype(f32), dcum, highest) + dlast
    dstep = dstep + dlog * rate
    ddt = dstep * sigmoid(raw)
    dlate_ref[:, inner : inner + 128] = pltpu.roll(ddt, turn_ref[0], 1).astype(bf16)
    skip = dot(jnp.broadcast_to(head_ref[2:3, :], (8, 128)), spread, highest)[0:1, :]
    dxs = dxs + skip * dy
    ghead_ref[0:1, :] += jnp.sum(ddt, 0, keepdims=True)
    ghead_ref[1:2, :] += jnp.sum(dlog * decay_log, 0, keepdims=True)
    ghead_ref[2:3, :] += jnp.sum(dot_last(dy * xs, spread, highest), 0, keepdims=True)
    slope = gate * (1.0 + pre * (1.0 - gate))
    dpre = jnp.concatenate([dxs, dbm, dcm], axis=1) * slope
    dext[0:span, :] = dpre
    gconv_ref[KW : KW + 1, :] += jnp.sum(dpre, 0, keepdims=True)
    dxbc = jnp.zeros_like(dpre)
    for k in range(KW):
        dxbc = dxbc + conv_ref[k : k + 1, :] * dext[pl.ds(KW - 1 - k, span), :]
        gconv_ref[k : k + 1, :] += jnp.sum(
            dpre * ext[pl.ds(8 - (KW - 1) + k, span), :], 0, keepdims=True
        )
    dlate_ref[:, :inner] = dxbc[:, :inner].astype(bf16)
    dlate_ref[:, inner + 128 :] = dxbc[:, inner:].astype(bf16)
    dext[span:, :] = dext[0:8, :]
    dfirst_ref[0] = dext[0:8, :]


def core_back(turn, early, late, dmixed, enter, halos, conv, head, leave, seq, heads, span):
    rows = dmixed.shape[0]
    inner = heads * MP
    wide = inner + 2 * NS
    count = rows // span
    first = seq * count

    def block(width, at):
        return pl.BlockSpec((span, width), lambda i: (first + count - 1 - i, at))

    def own(width):
        return pl.BlockSpec((span, width), lambda i: (count - 1 - i, 0))

    def whole(*shape):
        return pl.BlockSpec(shape, lambda i: (0,) * len(shape))

    return pl.pallas_call(
        functools.partial(core_back_kernel, heads=heads, span=span),
        grid=(count,),
        in_specs=[
            pl.BlockSpec(memory_space=pltpu.SMEM),
            block(inner, 0),
            block(2 * NS, (inner + 128) // (2 * NS)),
            block(inner, 0),
            block(128, inner // 128),
            own(inner),
            pl.BlockSpec((1, 1, inner, NS), lambda i: (0, count - 1 - i, 0, 0)),
            pl.BlockSpec((1, 1, 8, wide), lambda i: (0, count - 1 - i, 0, 0)),
            whole(8, wide),
            whole(8, 128),
            whole(1, inner, NS),
        ],
        out_specs=[
            own(late.shape[1]),
            whole(8, wide),
            whole(8, 128),
            whole(1, inner, NS),
            whole(1, 8, wide),
        ],
        out_shape=[
            jax.ShapeDtypeStruct((rows, late.shape[1]), bf16),
            jax.ShapeDtypeStruct((8, wide), f32),
            jax.ShapeDtypeStruct((8, 128), f32),
            jax.ShapeDtypeStruct((1, inner, NS), f32),
            jax.ShapeDtypeStruct((1, 8, wide), f32),
        ],
        scratch_shapes=[
            pltpu.VMEM((span + 8, wide), f32),
            pltpu.VMEM((span + 8, wide), f32),
            pltpu.VMEM((inner, NS), f32),
        ],
        compiler_params=params(1),
        cost_estimate=cost(rows, 60, (late, enter)),
        name="core_back",
    )(turn, late, late, early, late, dmixed, enter, halos, conv, head, leave)


def passed_along(block, distance):
    devices = range(lax.axis_size("g"))
    route = [(i - distance, i) for i in devices if i - distance in devices]
    return lax.ppermute(block, "g", route)


def entering(decay, local, reverse):
    peers, here = lax.axis_size("g"), lax.axis_index("g")
    decays = lax.all_gather(decay, "g")
    locals_ = lax.all_gather(local.astype(bf16), "g")
    state = jnp.zeros_like(local)
    for k in range(peers):
        at = peers - 1 - k if reverse else k
        reached = (at > here) if reverse else (at < here)
        state = jnp.where(reached, decays[at] * state + locals_[at].astype(f32), state)
    return state


def head_decay(decay_log, heads):
    keep = jnp.exp(decay_log[:, 0, :heads])
    return jnp.repeat(keep, MP, axis=1)[:, :, None]


def body(
    tokens, lengths, gains, w_query, w_keyval, w_attn_out, w_in, w_dt, conv_params, head_params,
    w_mamba_out, w_gate_up, w_down, cotangent,
):
    seqs, rows_seq, width = tokens.shape
    dp, groups, team = lax.axis_size("dp"), lax.axis_size("g"), lax.axis_size(TEAM)
    devices, line, plane = lax.axis_size(ALL), lax.axis_size(LINE), lax.axis_size(PLANE)
    seq_size = groups * team
    me = lax.axis_index(TEAM)
    heads = MH // team
    inner = heads * MP
    query = HQ * HD // team
    block_len = rows_seq * team
    rows = seqs * block_len
    held = w_query.shape[0]
    span = math.gcd(256, block_len)
    start = (lax.axis_index("g") * block_len).astype(jnp.int32).reshape(1)
    kv_head = me * (HQ // team) * KV // HQ

    core = lax.axis_index("c")
    conv_flat = conv_params.reshape(-1)
    conv_cols = -(-conv_flat.shape[0] // held)
    conv_flat = jnp.pad(conv_flat, (0, conv_cols * held - conv_flat.shape[0]))
    shared = 128 + 2 * NS
    keys_size = 2 * KV * HD
    packed = jnp.concatenate(
        [
            jnp.pad(w_dt, ((0, 0), (0, 128 - MH))),
            w_in[:, 2 * MI :],
            w_keyval,
            gains.T,
            conv_flat.reshape(held, conv_cols),
            jnp.zeros((held, shared - keys_size - 2 - conv_cols), bf16),
        ],
        axis=1,
    )
    w_big = jnp.concatenate(
        [
            w_in[:, :MI].reshape(held, team, inner),
            w_query.reshape(held, team, query),
            w_in[:, MI : 2 * MI].reshape(held, team, inner),
            jnp.tile(packed.reshape(held, 2, shared), (1, team // 2, 1)),
        ],
        axis=2,
    ).transpose(1, 0, 2)
    slots = []
    for k in range(team):
        slot = lax.dynamic_index_in_dim(w_big, me ^ k, 0, keepdims=False)
        route = [(i, i ^ k) for i in range(team)]
        slots.append(lax.ppermute(slot, TEAM, route) if k else slot)
    w_big = join_rows(slots, me)
    if groups > 1:
        w_big = lax.all_gather(w_big, "g", axis=0, tiled=True)
    block_tokens = lax.all_gather(after(tokens, w_big), TEAM, axis=1, tiled=True)
    block_tokens = block_tokens.reshape(rows, width)
    ffn_block = w_down.shape[0]
    w_gu = w_gate_up.reshape(held, 2, dp, line, plane // dp, ffn_block).transpose(4, 2, 0, 1, 3, 5)
    w_gu = w_gu.reshape(plane // dp, dp, held, 2 * line * ffn_block)
    mine_dp = lax.axis_index("dp")
    slots = []
    for j in range(2):
        for k in range(dp):
            slot = lax.dynamic_slice(
                w_gu, (core ^ j, mine_dp ^ k, 0, 0), (1, 1, held, 2 * line * ffn_block)
            )[0, 0]
            if j or k:
                route = [(2 * a + b, 2 * (a ^ k) + (b ^ j)) for a in range(dp) for b in range(2)]
                slot = lax.ppermute(slot, PLANE, route)
            slots.append(slot)
    w_gu = jnp.stack(slots)
    ratio = team // dp
    part = seq_size // ratio
    attn_rows, mamba_rows = w_attn_out.shape[0], w_mamba_out.shape[0]
    out_rows = attn_rows + mamba_rows
    cut = width // dp
    w_out = jnp.concatenate([w_attn_out, w_mamba_out], axis=0)
    w_out = w_out.reshape(out_rows, dp, cut)
    quarters = []
    for k in range(dp):
        quarter = lax.dynamic_index_in_dim(w_out, mine_dp ^ k, 1, keepdims=False)
        quarters.append(swap(quarter, "dp", k) if k else quarter)
    w_out = jnp.stack(quarters)
    positions = start[0] + jnp.arange(block_len, dtype=jnp.int32)
    cosine, sine = rope_tables(positions, HD)
    w_big, w_gu, w_out, cosine, sine = lax.optimization_barrier(
        (w_big, w_gu, w_out, cosine, sine)
    )
    blocks = parts_dp(w_big)
    key_at = inner + query
    others = [swap(part[:, inner + key_at :], "c", 1) for part, _, _ in blocks]
    w_early, w_late, rest = join_weights(blocks, others, inner, key_at, shared, kv_head)
    gain_all = rest[:, :2].astype(f32).T
    conv_all = rest[:, 2 : 2 + conv_cols]
    conv_all = conv_all.reshape(devices, held * conv_cols)[:, : conv_params.size]
    conv_all = (
        conv_all.reshape(devices, KW + 1, -1).transpose(1, 0, 2).reshape(KW + 1, -1).astype(f32)
    )
    conv_own = jnp.concatenate(
        [lax.dynamic_slice_in_dim(conv_all, me * inner, inner, 1), conv_all[:, MI:]], axis=1
    )
    conv_own = jnp.pad(conv_own, ((0, 8 - KW - 1), (0, 0)))
    head_own = jnp.pad(
        lax.dynamic_slice_in_dim(head_params, me * heads, heads, 1), ((0, 5), (0, 128 - heads))
    )
    turn = (me * heads).astype(jnp.int32).reshape(1)
    block_tokens, w_gu, w_early, w_late, gain_all = lax.optimization_barrier(
        (block_tokens, w_gu, w_early, w_late, gain_all)
    )
    columns = w_gu.shape[-1]
    folded = [w_down[:, i * columns : (i + 1) * columns] for i in range(width // columns)]
    w_ffn = jnp.concatenate([w_gu.reshape(-1, columns), *folded], axis=0)
    w_ffn = lax.all_gather(w_ffn, LINE, axis=0, tiled=False).reshape(line, -1, columns)
    my_seq = lax.axis_index(SEQ)
    w_out = after(w_out, block_tokens)
    if part == dp and groups == 1:
        parts = []
        for k in range(part):
            block = lax.dynamic_index_in_dim(w_out, mine_dp ^ (me % part) ^ k, 0, keepdims=False)
            route = [(i, ratio * ((i % part) ^ k) + i // part) for i in range(team)]
            parts.append(lax.ppermute(block, TEAM, route))
        w_out = jnp.stack(parts)
    else:
        order = mine_dp ^ jnp.arange(dp)
        w_out = jnp.take(w_out, order, axis=0)
        mine = (jnp.arange(ratio) == my_seq // part)[None, :, None, None]
        w_out = jnp.where(mine, w_out[:, None], jnp.zeros((), bf16))
        w_out = jnp.broadcast_to(
            w_out.reshape(1, team, out_rows, cut), (groups, team, out_rows, cut)
        ).reshape(-1, out_rows, cut)
        w_out = lax.all_to_all(w_out, SEQ, 0, 0, tiled=True)
        w_out = lax.dynamic_slice_in_dim(w_out, (me % ratio) * part, part, 0)
        w_out = jnp.concatenate(
            [w_out[:, attn_rows:].reshape(-1, cut), w_out[:, :attn_rows].reshape(-1, cut)], axis=0
        )

    own_positions = my_seq * rows_seq + jnp.arange(rows_seq, dtype=jnp.int32)
    valid = (own_positions[None, :] < lengths[:, None]).astype(f32)[:, :, None]
    cot = cotangent.astype(f32)

    norm1 = rms_norm(block_tokens.astype(f32), gain_all[0]).astype(bf16)
    early = dot(norm1, w_early)
    late = dot(norm1, w_late)
    early, late, w_out = lax.optimization_barrier((early, late, w_out))
    if w_out.ndim == 3:
        w_out = join_out(from_dp(w_out), me // ratio, attn_rows, mamba_rows)
    else:
        w_out = join_columns(from_dp(w_out))
    q = rotate(early[:, inner:key_at].reshape(seqs, block_len, HD), cosine, sine).astype(bf16)
    k = rotate(
        early[:, key_at : key_at + HD].reshape(seqs, block_len, HD), cosine, sine
    ).astype(bf16)
    v = early[:, key_at + HD :].reshape(seqs, block_len, HD).astype(bf16)
    if groups > 1:
        k = lax.all_gather(k, "g", axis=1, tiled=True)
        v = lax.all_gather(v, "g", axis=1, tiled=True)
    wide = inner + 2 * NS
    ends = late.reshape(seqs, block_len // span, span, -1)[:, :, span - 8 :, :]
    ends = jnp.concatenate([ends[..., :inner], ends[..., inner + 128 :]], axis=-1)
    if groups > 1:
        before = passed_along(ends[:, -1].astype(bf16), 1).astype(f32)
    else:
        before = jnp.zeros((seqs, 8, wide), f32)
    halos = jnp.concatenate([before[:, None], ends[:, :-1]], axis=1)
    nothing = jnp.zeros((1, inner, NS), f32)
    mixed_in, ys, enters, decays, logs, mix = [], [], [], [], [], []
    for s in range(seqs):
        fore = functools.partial(core_fore, seq=s, rows=block_len, heads=heads, span=span)
        halo = before[s : s + 1]
        gated, y, enter, final, decay_log = fore(
            turn, early, late, halo, conv_own, head_own, nothing
        )
        if groups > 1:
            decays.append(head_decay(decay_log, heads))
            init = entering(decays[s], final, False)
            gated, y, enter, final, _ = fore(turn, early, late, halo, conv_own, head_own, init)
        attn, log = attend_fore(lengths, start, q, k, v, span, s)
        mixed_in.append(jnp.concatenate([gated, attn[0]], axis=1))
        ys.append(y)
        enters.append(enter)
        logs.append(log)
        partial = dot(mixed_in[s], w_out).astype(bf16)
        mix.append(partial)
        if s == 0:
            early, late, _ = lax.optimization_barrier((early, late, partial))
            grad_ffn = [
                gather_plane((valid[n] * after(cot[n], partial)).astype(bf16)) for n in range(seqs)
            ]
    mix[0], mix[-1], w_ffn = lax.optimization_barrier((mix[0], mix[-1], w_ffn))
    mix = [lax.psum_scatter(partial, TEAM, scatter_dimension=0, tiled=True) for partial in mix]
    mix[0], *grad_ffn = lax.optimization_barrier((mix[0], *grad_ffn))
    w_gu, w_dn = join_hidden(w_ffn, plane, held, dp, width)
    w_gu, w_dn = w_gu.reshape(width, -1), w_dn.reshape(-1, width)

    units = w_dn.shape[0]
    hidden, norm2, act, ffn, grad_gu, grad_hidden, grad_mix = [], [], [], [], [], [], []
    for s in range(seqs):
        hidden.append(tokens[s].astype(f32) + valid[s] * mix[s].astype(f32))
        norm2_f, norm2_pull = jax.vjp(lambda h: rms_norm(h, gain_all[1]), hidden[s])
        norm2.append(gather_plane(norm2_f.astype(bf16)))
        if s > 0:
            norm2[s], local = lax.optimization_barrier((norm2[s], local))
            grad_mix.append(lax.all_gather(local, TEAM, axis=0, tiled=True))
        gate_up = dot(norm2[s], w_gu)
        gate, upper = gate_up[:, :units], gate_up[:, units:]
        sig_gate = sigmoid(gate)
        act.append((gate * sig_gate * upper).astype(bf16))
        grad_act = dot_last(grad_ffn[s], w_dn)
        grad_gate = grad_act * upper * (sig_gate * (1.0 + gate * (1.0 - sig_gate)))
        grad_upper = grad_act * gate * sig_gate
        grad_gu.append(jnp.concatenate([grad_gate, grad_upper], 1).astype(bf16))
        partial = dot_last(grad_gu[s], w_gu).astype(bf16)
        if s < seqs - 1:
            mix[s + 1] = after(mix[s + 1], partial)
        (grad_hidden_norm,) = norm2_pull(scatter_plane(partial))
        grad_hidden.append(cot[s] + grad_hidden_norm)
        local = (valid[s] * grad_hidden[s]).astype(bf16)
        ffn.append(dot(act[s], w_dn).astype(bf16))
    grad_w_gu = sum(map(dot_first, norm2, grad_gu)).astype(bf16)
    grad_w_dn = sum(map(dot_first, act, grad_ffn)).astype(bf16)
    grad_w_gu = grad_w_gu.reshape(dp, line, plane // dp, held, 2 * line * ffn_block)
    grad_w_gu = grad_w_gu.transpose(1, 0, 2, 3, 4).reshape(width, -1)
    local, grad_w_gu, grad_w_dn, *ffn = lax.optimization_barrier(
        (local, grad_w_gu, grad_w_dn, *ffn)
    )
    grad_mix.append(lax.all_gather(local, TEAM, axis=0, tiled=True))
    grad_mix[0], grad_w_gu, grad_w_dn = lax.optimization_barrier(
        (grad_mix[0], grad_w_gu, grad_w_dn)
    )
    grad_w_gu = lax.psum_scatter(grad_w_gu, LINE, scatter_dimension=0, tiled=True)
    grad_down = lax.psum_scatter(grad_w_dn, LINE, scatter_dimension=0, tiled=True).astype(f32)
    ffn = [scatter_core(after(partial, local)) for partial in ffn]

    def to_owners(partial):
        if groups > 1:
            partial = lax.psum_scatter(partial, "g", scatter_dimension=0, tiled=True)
        partial = partial.astype(bf16).reshape(team, held, -1)
        return lax.all_to_all(partial, TEAM, 0, 0, tiled=True).transpose(1, 0, 2).astype(f32)

    def small_grads(gconv, ghead):
        grad_conv = jnp.concatenate(
            [
                lax.dynamic_update_slice_in_dim(
                    jnp.zeros((KW + 1, MI), f32), gconv[: KW + 1, :inner], me * inner, 1
                ),
                gconv[: KW + 1, inner:],
            ],
            axis=1,
        )
        grad_head = lax.dynamic_update_slice_in_dim(
            jnp.zeros((3, MH), f32), ghead[:3, :heads], me * heads, 1
        )
        flat = jnp.concatenate([grad_conv.reshape(-1), grad_head.reshape(-1)])
        return jnp.pad(flat, (0, -flat.shape[0] % 1024)).reshape(-1, 128)

    dearly, dlate, grad_norm1 = [], [], []
    gconv, ghead = 0.0, 0.0
    for s in range(seqs):
        grad_mixed_in = dot_last(grad_mix[s], w_out)
        if s == 0:
            grad_mixed_in, *ffn = lax.optimization_barrier((grad_mixed_in, *ffn))
            ffn = [scatter_near(near) for near in ffn]
            mixed = [(hidden[n] + valid[n] * ffn[n]).astype(bf16) for n in range(seqs)]
            mixed = jnp.stack(mixed)
        if s == seqs - 1:
            grad_w_out = sum(map(dot_first, mixed_in, grad_mix)).astype(bf16)
            grad_mixed_in, grad_w_out = lax.optimization_barrier((grad_mixed_in, grad_w_out))
            grad_w_out = scatter_dp(grad_w_out, 1)
            if groups > 1:
                grad_w_out = lax.psum(grad_w_out, "g")
            grad_w_out = grad_w_out.astype(bf16)
        dq, dk, dv = attend_back(lengths, start, q, k, v, grad_mixed_in, logs[s], span, s)
        if groups > 1:
            dk = lax.psum_scatter(dk, "g", scatter_dimension=1, tiled=True)
            dv = lax.psum_scatter(dv, "g", scatter_dimension=1, tiled=True)
        dq = rotate_back(dq[0], cosine, sine).astype(bf16)
        dk = rotate_back(dk[0], cosine, sine).astype(bf16)
        z = early[s * block_len : (s + 1) * block_len, :inner]
        sig_z = sigmoid(z)
        dz = grad_mixed_in[:, :inner] * ys[s] * (sig_z * (1.0 + z * (1.0 - sig_z)))
        dearly.append(jnp.concatenate([dz.astype(bf16), dq, dk, dv[0].astype(bf16)], axis=1))
        if s == seqs - 1:
            grad_early = dot_first(norm1, jnp.concatenate(dearly, axis=0)).astype(bf16)
            grad_mixed_in, grad_early, grad_w_out, grad_w_gu = lax.optimization_barrier(
                (grad_mixed_in, grad_early, grad_w_out, grad_w_gu)
            )
            grad_w_gu = lax.all_to_all(
                grad_w_gu.reshape(plane, held, 2 * line * ffn_block), PLANE, 0, 0, tiled=True
            )
            grad_w_out = jnp.concatenate(
                [
                    grad_w_out[inner:].reshape(part, attn_rows, cut),
                    grad_w_out[:inner].reshape(part, mamba_rows, cut),
                ],
                axis=1,
            )
            if part == dp and groups == 1:
                parts = []
                for n in range(part):
                    piece = lax.dynamic_index_in_dim(
                        grad_w_out, (me // ratio) ^ n, 0, keepdims=False
                    )
                    route = [(ratio * ((i % part) ^ n) + i // part, i) for i in range(team)]
                    parts.append(lax.ppermute(piece, TEAM, route))
                grad_w_out = jnp.stack(parts)
            else:
                grad_w_out = lax.dynamic_update_slice_in_dim(
                    jnp.zeros((seq_size, out_rows, cut), bf16),
                    grad_w_out,
                    (me % ratio) * part,
                    0,
                )
                grad_w_out = lax.all_to_all(grad_w_out, SEQ, 0, 0, tiled=True)
                grad_w_out = grad_w_out.reshape(groups, dp, ratio, out_rows, cut)[0]
                grad_w_out = lax.dynamic_index_in_dim(
                    grad_w_out, my_seq // part, 1, keepdims=False
                )
                grad_w_out = jnp.take(grad_w_out, (my_seq % part % dp) ^ jnp.arange(dp), axis=0)
            grad_early = scatter_dp(grad_early, 0)
        back = functools.partial(core_back, seq=s, heads=heads, span=span)
        halo = halos[s : s + 1]
        dlate_s, gconv_s, ghead_s, dinit, dfirst = back(
            turn, early, late, grad_mixed_in, enters[s], halo, conv_own, head_own, nothing
        )
        if groups > 1:
            leave = entering(decays[s], dinit, True)
            dlate_s, gconv_s, ghead_s, dinit, dfirst = back(
                turn, early, late, grad_mixed_in, enters[s], halo, conv_own, head_own, leave
            )
            padded = jnp.concatenate([jnp.zeros((1, KW - 1, wide), f32), dfirst], axis=1)
            rim = sum(
                conv_own[j][None, None] * padded[:, KW - 1 - j : 2 * (KW - 1) - j]
                for j in range(KW)
            )
            rim = passed_along(rim.astype(bf16), -1).astype(f32)
            rim = jnp.pad(rim[0], ((block_len - KW + 1, 0), (0, 0)))
            step_gap = jnp.zeros((block_len, 128), f32)
            rim = jnp.concatenate([rim[:, :inner], step_gap, rim[:, inner:]], axis=1)
            dlate_s = (dlate_s.astype(f32) + rim).astype(bf16)
        gconv, ghead = gconv + gconv_s, ghead + ghead_s
        if s == seqs - 1:
            grad_late = dot_first(norm1, jnp.concatenate([*dlate, dlate_s], axis=0)).astype(bf16)
            small = small_grads(gconv, ghead)
            small = small + swap(small, "c", 1)
            late_cuts = cuts_dp(grad_late, 0)
            parts = []
            for n in range(dp):
                piece = lax.dynamic_index_in_dim(
                    grad_w_out, (my_seq % part % dp) ^ mine_dp ^ n, 0, keepdims=False
                )
                parts.append(swap(piece, "dp", n) if n else piece)
            dlate_s, small, grad_early, parts, late_cuts, grad_w_gu = lax.optimization_barrier(
                (dlate_s, small, grad_early, parts, late_cuts, grad_w_gu)
            )
            grad_late = sum_cuts(late_cuts)
            small = sum(swap(small, "dp", n) if n else small for n in range(dp))
        dlate.append(dlate_s)
        partial = (dot_last(dearly[s], w_early) + dot_last(dlate_s, w_late)).astype(bf16)
        if s == seqs - 1:
            grad_w_out = jnp.take(jnp.stack(parts), mine_dp ^ jnp.arange(dp), axis=0)
            grad_w_out = grad_w_out.transpose(1, 0, 2).reshape(out_rows, width).astype(f32)
            partial, grad_down, small = lax.optimization_barrier((partial, grad_down, small))
            size_z = lax.axis_size("z")
            small = sum(
                lax.ppermute(small, "z", [(i, (i + n) % size_z) for i in range(size_z)])
                if n
                else small
                for n in range(size_z)
            )
            if groups > 1:
                small = lax.psum(small, "g")
            grad_early = to_owners(grad_early)
        grad_norm1.append(lax.psum_scatter(partial, TEAM, scatter_dimension=0, tiled=True))
        if s == 0:
            grad_mix[1:], mixed, _ = lax.optimization_barrier((grad_mix[1:], mixed, partial))
    grad_gate_up = (
        grad_w_gu.reshape(dp, plane // dp, held, 2, line, ffn_block)
        .transpose(2, 3, 0, 4, 1, 5)
        .reshape(held, -1)
        .astype(f32)
    )
    grad_late, grad_w_out, grad_early, small = lax.optimization_barrier(
        (grad_late, grad_w_out, grad_early, small)
    )
    grad_late = to_owners(grad_late)
    grad_z = grad_early[:, :, :inner].reshape(held, MI)
    grad_query = grad_early[:, :, inner:key_at].reshape(held, -1)
    grad_keyval = grad_early[:, :, key_at:].reshape(held, KV, team // KV, 2, HD)
    grad_keyval = jnp.sum(grad_keyval, axis=2).transpose(0, 2, 1, 3).reshape(held, -1)
    grad_x = grad_late[:, :, :inner].reshape(held, MI)
    grad_dt = jnp.sum(grad_late[:, :, inner : inner + MH], axis=1)
    grad_bc = jnp.sum(grad_late[:, :, inner + 128 :], axis=1)
    grad_in = jnp.concatenate([grad_z, grad_x, grad_bc], axis=1)

    grad_gains = [
        jnp.sum(w_in.astype(f32) * grad_in, 1)
        + jnp.sum(w_query.astype(f32) * grad_query, 1)
        + jnp.sum(w_keyval.astype(f32) * grad_keyval, 1)
        + jnp.sum(w_dt.astype(f32) * grad_dt, 1),
        jnp.sum(w_gate_up.astype(f32) * grad_gate_up, 1),
    ]
    grad_gains = jnp.stack(grad_gains) / gains.astype(f32)
    own_conv = conv_params.shape[1]
    small = small.reshape(-1)
    conv_end = (KW + 1) * conv_params.shape[1] * devices
    grad_conv = lax.dynamic_slice_in_dim(
        small[:conv_end].reshape(KW + 1, -1), lax.axis_index(ALL) * own_conv, own_conv, 1
    )
    head_total = small[conv_end : conv_end + 3 * MH].reshape(3, MH)
    grad_tokens = []
    for s in range(seqs):
        _, norm1_pull = jax.vjp(lambda v: rms_norm(v, gain_all[0]), tokens[s].astype(f32))
        (grad_token_norm,) = norm1_pull(grad_norm1[s].astype(f32))
        grad_tokens.append((grad_hidden[s] + grad_token_norm).astype(bf16))
    grad_tokens = jnp.stack(grad_tokens)
    grad_attn_out, grad_mamba_out = grad_w_out[:attn_rows], grad_w_out[attn_rows:]
    return (
        mixed,
        grad_tokens,
        grad_gains,
        grad_query,
        grad_keyval,
        grad_attn_out,
        grad_in,
        grad_dt,
        grad_conv,
        head_total[:2],
        head_total[2],
        grad_mamba_out,
        grad_gate_up,
        grad_down,
    )


def solution(mesh):
    dp, seq = mesh.shape["dp"], mesh.shape["seq"]
    team = math.gcd(math.gcd(HQ, MH), seq)
    split = Mesh(mesh.devices.reshape(dp, seq // team, team // 2, 2), ALL)
    rows = P(ALL, None)
    cols = P(None, ALL)
    acts = P("dp", SEQ, None)
    return jax.shard_map(
        body,
        mesh=split,
        in_specs=(
            acts, P("dp"), cols, rows, rows, rows, rows, rows, cols, P(), rows, rows, rows, acts,
        ),
        out_specs=(
            acts, acts, cols, rows, rows, rows, rows, rows, cols, P(), P(), rows, rows, rows,
        ),
        check_vma=False,
    )
```

time: 1290 us -> 947 us (0.73)
  waiting for transfers between devices: 690 us -> 287 us
  starting transfers between devices: 32.4 us -> 129 us
  blocking collectives: 55.5 us -> 0 us
  local copies, waits for them, and re-layouts: 143 us -> 107 us
  other arithmetic: 60.7 us -> 87.3 us
  Pallas kernels: 104 us -> 127 us
    all_gather x9 -> x4, waiting for transfers between devices: 290 us -> 35.4 us  [the longest x1 35.3 us: body(): lax.all_gather(w_ffn, LINE, axis=0, tiled=False).reshape(line, -1, columns)]
    ppermute x0 -> x100, waiting for transfers between devices: none -> 230 us  [the longest x75 178 us: swap(): lax.ppermute(block, axis, [(i, i ^ distance) for i in range(lax.axis_size...]
    reduce_scatter x6 -> x5, waiting for transfers between devices: 201 us -> 17.9 us  [the longest x1 17.9 us: body(): lax.psum_scatter(grad_w_gu, LINE, scatter_dimension=0, tiled=True)]
    all_to_all x7 -> x2, waiting for transfers between devices: 164 us -> 3.01 us  [to_owners(): lax.all_to_all(partial, TEAM, 0, 0, tiled=True).transpose(1, 0, 2)]
    ppermute x0 -> x100, starting transfers between devices: none -> 114 us  [the longest x75 61.7 us: swap(): lax.ppermute(block, axis, [(i, i ^ distance) for i in range(lax.axis_size...]
    all_to_all x2 -> x0, blocking collectives: 55.5 us -> none  [the longest x1 35.9 us: body(): lax.all_to_all(w_big, TEAM, 0, 0, tiled=True)]
    dynamic_update_slice x4 -> x2, local copies, waits for them, and re-layouts: 48.5 us -> 0.16 us  [the longest x1 0.15 us: small_grads(): lax.dynamic_update_slice_in_dim(jnp.zeros((3, MH), f32), ghead[:3, :heads...]
    unnamed x18 -> x10, waiting for transfers between devices: 34.9 us -> 0.82 us
  transfers between devices with their start and end apart: 25 -> 113, of which waited for: 16 -> 39; matrix products, arithmetic and copies ran while one was open for 24% -> 35% of each run, Pallas kernels for 8% -> 13%
where the time goes in v2:
time: 947 us; the launch traced here: 938 us
  waiting for transfers between devices  287 us (30%)
  matrix products  183 us (19%)
  starting transfers between devices  129 us (14%)
  Pallas kernels  127 us (13%)
  local copies, waits for them, and re-layouts  107 us (11%)
  other arithmetic  87.3 us (9%)
  between operations  17.3 us (2%)
    ppermute x75, waiting for transfers between devices, swap(): lax.ppermute(block, axis, [(i, i ^ distance) for i in range(lax.axis_size...  178 us
    dot_general x8, matrix products, dot_first(): lax.dot_general(left, right, (((0,), (0,)), ((), ())), preferred_element_...  62.7 us
    dot_general x10, matrix products, dot_last(): lax.dot_general(left, right, (((1,), (1,)), ((), ())), preferred_element_...  62.5 us
    ppermute x75, starting transfers between devices, swap(): lax.ppermute(block, axis, [(i, i ^ distance) for i in range(lax.axis_size...  61.7 us
    pallas_call x2, Pallas kernels, core_back(): pl.pallas_call(functools.partial(core_back_kernel, heads=heads, span=span...  61.5 us
    dot_general x8, matrix products, dot(): return jnp.dot(left, right, preferred_element_type=f32, precision=precision)  58.1 us
    unnamed x336, local copies, waits for them, and re-layouts  38.5 us
    all_gather x1, waiting for transfers between devices, body(): lax.all_gather(w_ffn, LINE, axis=0, tiled=False).reshape(line, -1, columns)  35.3 us
  transfers between devices with their start and end apart: 113, of which 39 were waited for; matrix products, arithmetic and copies ran while one was open for 35% of the time, Pallas kernels for 13%

profile of v2, /device:TPU:0, one launch (start us, length us, event | category | flops | bytes accessed | tf_op | source)
XLA Modules:
  0.0 937.5 jit_solution(13554976916742143979)
XLA Ops:
  35.4 11.6 %collective-permute-done.4.refs_5_ = bf16[64,1536]{1,0:T(8,128)(2,1)S(1)} collective-permute-done((bf16[64,1536]{1,0:T(8,128)(2,1)}, bf16[64,1536]{1,0:T(8,128)(2,1)S(1)}, u32[]{:S(2)}, u32[]{:S(2)}) %collective-permute-start.4) | collective-permute-done | bytes 196640 | tf_op jit(solution)/shard_map/ppermute | solution.py:800
  86.9 34.9 %collective-permute-done.17.refs_1_ = bf16[512,1536]{1,0:T(8,128)(2,1)S(1)} collective-permute-done((bf16[512,1536]{1,0:T(8,128)(2,1)S(1)}, bf16[512,1536]{1,0:T(8,128)(2,1)S(1)}, u32[]{:S(2)}, u32[]{:S(2)}) %collective-permute-start.17) | collective-permute-done | bytes 1572896 | tf_op jit(solution)/shard_map/ppermute | solution.py:270
  128.6 13.2 %collective-permute-done.19.refs_3_ = bf16[256,1536]{1,0:T(8,128)(2,1)S(1)} collective-permute-done((bf16[256,1536]{1,0:T(8,128)(2,1)}, bf16[256,1536]{1,0:T(8,128)(2,1)S(1)}, u32[]{:S(2)}, u32[]{:S(2)}) %collective-permute-start.19) | collective-permute-done | bytes 786464 | tf_op jit(solution)/shard_map/ppermute | solution.py:270
  165.6 7.9 collective-permute-start.28
  175.6 14.7 %fusion.93.x_ref.bc_ref.dt_ref = f32[2048,1024]{1,0:T(8,128)} fusion(bf16[2048,1024]{1,0:T(8,128)(2,1)} %get-tuple-element.118, bf16[2048,2048]{1,0:T(8,128)(2,1)} %bitcast.323, f32[2048]{0:T(1024)S(1)} %get-tuple-element.254, f32[2048]{0:T(1024)S(1)} %add_rsqrt_fusion), kind=kOutput, calls=%fused_computation.334 | convolution fusion | flops 8606711808 | bytes 20987904 | tf_op jit(solution)/shard_map/dot_general | solution.py:63
  190.2 9.2 fusion.95.z_ref
  205.6 14.5 %core_fore.2 = (bf16[1024,384]{1,0:T(8,128)(2,1)S(1)}, f32[1024,384]{1,0:T(8,128)S(1)}, f32[1,4,384,256]{3,2,1,0:T(8,128)S(1)}, f32[1,384,256]{2,1,0:T(8,128)}, f32[1,8,128]{2,1,0:T(8,128)}) custom-call(s32[1]{0:T(128)} %bitcast.2.turn_ref, f32[2048,1024]{1,0:T(8,128)} %fusion.93.x_ref.bc_ref.dt_ref, f32[2048,1024]{1,0:T(8,128)} %fusion.93.x_ref.bc_ref.dt_ref, ...), custom_call_target="tpu_custom_call" | custom-call | flops 12999999488 | bytes 8781824 | tf_op jit(solution)/shard_map/core_fore/pallas_call | solution.py:516
  236.3 14.1 %core_fore.3 = (bf16[1024,384]{1,0:T(8,128)(2,1)S(1)}, f32[1024,384]{1,0:T(8,128)S(1)}, f32[1,4,384,256]{3,2,1,0:T(8,128)S(1)}, f32[1,384,256]{2,1,0:T(8,128)}, f32[1,8,128]{2,1,0:T(8,128)}) custom-call(s32[1]{0:T(128)} %bitcast.2.turn_ref, f32[2048,1024]{1,0:T(8,128)} %fusion.93.x_ref.bc_ref.dt_ref, f32[2048,1024]{1,0:T(8,128)} %fusion.93.x_ref.bc_ref.dt_ref, ...), custom_call_target="tpu_custom_call" | custom-call | flops 12999999488 | bytes 8781824 | tf_op jit(solution)/shard_map/core_fore/pallas_call | solution.py:516
  258.0 35.3 %all-gather.12.cloned.1.call-done = bf16[3072,1024]{1,0:T(8,128)(2,1)} async-done(((bf16[768,1024]{1,0:T(8,128)(2,1)}), bf16[3072,1024]{1,0:T(8,128)(2,1)}) %all-gather.12.cloned.1.call-update) | async-done | bytes 6291472 | tf_op jit(solution)/shard_map/all_gather | solution.py:862
  301.3 8.9 collective-permute-done.33
  311.7 10.1 %collective-permute-done.34 = bf16[128,2048]{1,0:T(8,128)(2,1)S(1)} collective-permute-done((bf16[128,2048]{1,0:T(8,128)(2,1)S(1)}, bf16[128,2048]{1,0:T(8,128)(2,1)S(1)}, u32[]{:S(2)}, u32[]{:S(2)}) %collective-permute-start.34) | collective-permute-done | bytes 524320 | tf_op jit(solution)/shard_map/ppermute | solution.py:270
  323.6 9.1 collective-permute-done.40
  333.6 10.6 %collective-permute-done.41 = bf16[128,2048]{1,0:T(8,128)(2,1)S(1)} collective-permute-done((bf16[128,2048]{1,0:T(8,128)(2,1)S(1)}, bf16[128,2048]{1,0:T(8,128)(2,1)S(1)}, u32[]{:S(2)}, u32[]{:S(2)}) %collective-permute-start.41) | collective-permute-done | bytes 524320 | tf_op jit(solution)/shard_map/ppermute | solution.py:270
  370.2 9.9 %collective-permute-done.48 = bf16[128,2048]{1,0:T(8,128)(2,1)} collective-permute-done((bf16[128,2048]{1,0:T(8,128)(2,1)}, bf16[128,2048]{1,0:T(8,128)(2,1)}, u32[]{:S(2)}, u32[]{:S(2)}) %collective-permute-start.48) | collective-permute-done | bytes 524320 | tf_op jit(solution)/shard_map/ppermute | solution.py:270
  421.4 10.9 %collective-permute-done.63 = bf16[128,2048]{1,0:T(8,128)(2,1)} collective-permute-done((bf16[128,2048]{1,0:T(8,128)(2,1)}, bf16[128,2048]{1,0:T(8,128)(2,1)}, u32[]{:S(2)}, u32[]{:S(2)}) %collective-permute-start.63) | collective-permute-done | bytes 524320 | tf_op jit(solution)/shard_map/ppermute | solution.py:270
  441.9 8.0 collective-permute-done.54
  450.0 11.4 %collective-permute-done.55 = bf16[128,2048]{1,0:T(8,128)(2,1)S(1)} collective-permute-done((bf16[128,2048]{1,0:T(8,128)(2,1)S(1)}, bf16[128,2048]{1,0:T(8,128)(2,1)S(1)}, u32[]{:S(2)}, u32[]{:S(2)}) %collective-permute-start.55) | collective-permute-done | bytes 524320 | tf_op jit(solution)/shard_map/ppermute | solution.py:270
  466.1 10.0 %fusion.112 = f32[1024,1024]{0,1:T(8,128)} fusion(bf16[1024,2048]{1,0:T(8,128)(2,1)} %copy-done.121, bf16[2048,1024]{1,0:T(8,128)(2,1)} %bitcast.371), kind=kOutput, calls=%fused_computation.349 | convolution fusion | flops 4294967296 | bytes 12582912 | tf_op jit(solution)/shard_map/dot_general | solution.py:63
  496.1 8.0 fusion.41
  504.1 9.8 %add_convert_fusion.2 = bf16[2048,1024]{1,0:T(8,128)(2,1)} fusion(f32[2048,1024]{1,0:T(8,128)} %fusion.41, bf16[1024,2048]{1,0:T(8,128)(2,1)S(1)} %copy-done.120, bf16[1024,512]{0,1:T(8,128)(2,1)S(1)} %copy-done.145, bf16[1024,512]{0,1:T(8,128)(2,1)S(1)} %copy-done.143), kind=kOutput, calls=%fused_computation.8 | convolution fusion | flops 4303355904 | bytes 18874368 | tf_op jit(solution)/shard_map/dot_general | solution.py:67
  534.2 10.0 %collective-permute-done.67 = bf16[128,2048]{1,0:T(8,128)(2,1)} collective-permute-done((bf16[128,2048]{1,0:T(8,128)(2,1)}, bf16[128,2048]{1,0:T(8,128)(2,1)}, u32[]{:S(2)}, u32[]{:S(2)}) %collective-permute-start.67) | collective-permute-done | bytes 524320 | tf_op jit(solution)/shard_map/ppermute | solution.py:270
  595.5 30.7 %core_back.2 = (bf16[1024,1024]{1,0:T(8,128)(2,1)S(1)}, f32[8,896]{1,0:T(8,128)S(1)}, f32[8,128]{1,0:T(8,128)S(1)}, f32[1,384,256]{2,1,0:T(8,128)}, f32[1,8,896]{2,1,0:T(8,128)}) custom-call(s32[1]{0:T(128)} %bitcast.2.turn_ref, f32[2048,1024]{1,0:T(8,128)} %fusion.93.x_ref.bc_ref.dt_ref, f32[2048,1024]{1,0:T(8,128)} %fusion.93.x_ref.bc_ref.dt_ref, ...), custom_call_target="tpu_custom_call" | custom-call | flops 30000001024 | bytes 9961472 | tf_op jit(solution)/shard_map/core_back/pallas_call | solution.py:687
  627.5 8.8 add_convert_fusion.1
  676.9 9.3 convolution_convert_fusion.6
  686.2 7.6 fusion.33
  699.8 17.9 %reduce-scatter.13.cloned.1.call-done = bf16[512,1024]{1,0:T(8,128)(2,1)} async-done(((bf16[2048,1024]{1,0:T(8,128)(2,1)}), bf16[512,1024]{1,0:T(8,128)(2,1)}) %reduce-scatter.13.cloned.1.call-update) | async-done | bytes 1048592 | tf_op jit(solution)/shard_map/reduce_scatter | solution.py:979
  717.7 30.8 %core_back.3 = (bf16[1024,1024]{1,0:T(8,128)(2,1)S(1)}, f32[8,896]{1,0:T(8,128)S(1)}, f32[8,128]{1,0:T(8,128)S(1)}, f32[1,384,256]{2,1,0:T(8,128)}, f32[1,8,896]{2,1,0:T(8,128)}) custom-call(s32[1]{0:T(128)} %bitcast.2.turn_ref, f32[2048,1024]{1,0:T(8,128)} %fusion.93.x_ref.bc_ref.dt_ref, f32[2048,1024]{1,0:T(8,128)} %fusion.93.x_ref.bc_ref.dt_ref, ...), custom_call_target="tpu_custom_call" | custom-call | flops 30000001024 | bytes 9961472 | tf_op jit(solution)/shard_map/core_back/pallas_call | solution.py:687
  760.7 14.3 %fusion.7 = bf16[2048,1024]{1,0:T(8,128)(2,1)} fusion(bf16[1024,1024]{1,0:T(8,128)(2,1)S(1)} %copy-done.43, bf16[1024,1024]{1,0:T(8,128)(2,1)S(1)} %copy-done.41, bf16[2048,2048]{1,0:T(8,128)(2,1)} %bitcast.325, f32[2048]{0:T(1024)S(1)} %copy-done.110, f32[2048]{0:T(1024)S(1)} %copy-done.129), kind=kOutput, calls=%fused_computation.19 | convolution fusion | flops 8617197568 | bytes 16793600 | tf_op jit(solution)/shard_map/dot_general | solution.py:67
  798.6 7.5 collective-permute-done.88
  812.2 9.5 %add_convert_fusion = bf16[1024,2048]{1,0:T(8,128)(2,1)} fusion(f32[1024,2048]{1,0:T(8,128)} %fusion.33, bf16[1024,1024]{1,0:T(8,128)(2,1)S(1)} %copy-done.44, bf16[2048,1024]{1,0:T(8,128)(2,1)} %get-tuple-element.118), kind=kOutput, calls=%fused_computation.6 | convolution fusion | flops 4299161600 | bytes 18874368 | tf_op jit(solution)/shard_map/dot_general | solution.py:73
  837.3 23.5 %collective-permute-done.99 = f32[144,128]{1,0:T(8,128)S(1)} collective-permute-done((f32[144,128]{1,0:T(8,128)S(1)}, f32[144,128]{1,0:T(8,128)S(1)}, u32[]{:S(2)}, u32[]{:S(2)}) %collective-permute-start.99) | collective-permute-done | bytes 73760 | tf_op jit(solution)/shard_map/ppermute | solution.py:1114
  860.8 11.4 %collective-permute-start.97 = (f32[144,128]{1,0:T(8,128)S(1)}, f32[144,128]{1,0:T(8,128)}, u32[]{:S(2)}, u32[]{:S(2)}) collective-permute-start(f32[144,128]{1,0:T(8,128)S(1)} %add_add_fusion.5), channel_id=1, source_target_pairs={{0,2},{2,4},{4,6},{6,0},{1,3},{3,5},{5,7},{7,1},{8,10},{10,12},{12... | collective-permute-start | bytes 221192 | tf_op jit(solution)/shard_map/ppermute | solution.py:1114
  (767 shorter events, 476.7 us)
Async XLA Ops:
  7.2 146.6 %all-gather.6.cloned.1.call-start = ((), (), s32[]{:S(2)}) async-start(), calls=%async_computation.9 | async-start | bytes 9437184 | tf_op jit(solution)/shard_map/all_gather | solution.py:804
  49.7 243.6 %all-gather.12.cloned.1.call-start = ((), (), s32[]{:S(2)}) async-start(), calls=%async_computation.18 | async-start | bytes 7864320 | tf_op jit(solution)/shard_map/all_gather | solution.py:862
  85.3 36.4 %collective-permute-start.17 = (bf16[512,1536]{1,0:T(8,128)(2,1)S(1)}, bf16[512,1536]{1,0:T(8,128)(2,1)S(1)}, u32[]{:S(2)}, u32[]{:S(2)}) collective-permute-start(bf16[512,1536]{1,0:T(8,128)(2,1)S(1)} %bitcast.297), channel_id=1, source_target_pairs={{0,8},{8,0},{16,24},{24,16},{1,9},{9,1},{17,25},{25,17},{2,10},{10... | collective-permute-start | bytes 4718600 | tf_op jit(solution)/shard_map/ppermute | solution.py:270
  85.8 37.6 %collective-permute-start.18 = (bf16[512,1536]{1,0:T(8,128)(2,1)S(1)}, bf16[512,1536]{1,0:T(8,128)(2,1)S(1)}, u32[]{:S(2)}, u32[]{:S(2)}) collective-permute-start(bf16[512,1536]{1,0:T(8,128)(2,1)S(1)} %bitcast.298), channel_id=1, source_target_pairs={{0,16},{8,24},{16,0},{24,8},{1,17},{9,25},{17,1},{25,9},{2,18},{10... | collective-permute-start | bytes 4718600 | tf_op jit(solution)/shard_map/ppermute | solution.py:270
  160.1 39.4 %collective-permute-start.29 = (bf16[128,512]{1,0:T(8,128)(2,1)S(1)}, bf16[128,512]{1,0:T(8,128)(2,1)S(1)}, u32[]{:S(2)}, u32[]{:S(2)}) collective-permute-start(bf16[128,512]{1,0:T(8,128)(2,1)S(1)} %get-tuple-element.357), channel_id=1, source_target_pairs={{0,6},{1,4},{2,2},{3,0},{4,7},{5,5},{6,3},{7,1},{8,14},{9,12},{10,... | collective-permute-start | bytes 393224 | tf_op jit(solution)/shard_map/ppermute | solution.py:870
  165.6 33.9 %collective-permute-start.28 = (bf16[128,512]{1,0:T(8,128)(2,1)S(1)}, bf16[128,512]{1,0:T(8,128)(2,1)S(1)}, u32[]{:S(2)}, u32[]{:S(2)}) collective-permute-start(bf16[128,512]{1,0:T(8,128)(2,1)S(1)} %get-tuple-element.358), channel_id=1, source_target_pairs={{0,4},{1,6},{2,0},{3,2},{4,5},{5,7},{6,1},{7,3},{8,12},{9,14},{10,... | collective-permute-start | bytes 393224 | tf_op jit(solution)/shard_map/ppermute | solution.py:870
  175.5 175.6 %reduce-scatter.7.cloned.1.call-start = ((), (), s32[]{:S(2)}) async-start(), calls=%async_computation.10 | async-start | bytes 4718592 | tf_op jit(solution)/shard_map/reduce_scatter | solution.py:939
  199.6 30.6 %collective-permute-start.30 = (bf16[4,128,512]{2,1,0:T(8,128)(2,1)S(1)}, bf16[4,128,512]{2,1,0:T(8,128)(2,1)S(1)}, u32[]{:S(2)}, u32[]{:S(2)}) collective-permute-start(bf16[4,128,512]{2,1,0:T(8,128)(2,1)S(1)} %pad_maximum_fusion.21.refs_0_), channel_id=1, source_target_pairs={{0,8},{8,0},{16,24},{24,16},{1,9},{9,1},{17,25},{25,17},{2,10},{10... | collective-permute-start | bytes 1572872 | tf_op jit(solution)/shard_map/ppermute | solution.py:270
  293.4 115.5 %reduce-scatter.9.cloned.1.call-start = ((), (), s32[]{:S(2)}) async-start(), calls=%async_computation.11 | async-start | bytes 4718592 | tf_op jit(solution)/shard_map/reduce_scatter | solution.py:939
  299.9 32.9 %collective-permute-start.40 = (bf16[128,2048]{1,0:T(8,128)(2,1)S(1)}, bf16[128,2048]{1,0:T(8,128)(2,1)S(1)}, u32[]{:S(2)}, u32[]{:S(2)}) collective-permute-start(bf16[128,2048]{1,0:T(8,128)(2,1)S(1)} %get-tuple-element.268), channel_id=1, source_target_pairs={{0,8},{8,0},{16,24},{24,16},{1,9},{9,1},{17,25},{25,17},{2,10},{10... | collective-permute-start | bytes 1572872 | tf_op jit(solution)/shard_map/ppermute | solution.py:270
  310.2 34.0 %collective-permute-start.41 = (bf16[128,2048]{1,0:T(8,128)(2,1)S(1)}, bf16[128,2048]{1,0:T(8,128)(2,1)S(1)}, u32[]{:S(2)}, u32[]{:S(2)}) collective-permute-start(bf16[128,2048]{1,0:T(8,128)(2,1)S(1)} %get-tuple-element.268), channel_id=1, source_target_pairs={{0,16},{8,24},{16,0},{24,8},{1,17},{9,25},{17,1},{25,9},{2,18},{10... | collective-permute-start | bytes 1572872 | tf_op jit(solution)/shard_map/ppermute | solution.py:270
  355.2 194.8 %all-gather.10.cloned.1.call-start = ((), (), s32[]{:S(2)}) async-start(), calls=%async_computation.13 | async-start | bytes 4718592 | tf_op jit(solution)/shard_map/all_gather | solution.py:952
  476.1 177.7 %all-gather.8.cloned.1.call-start = ((), (), s32[]{:S(2)}) async-start(), calls=%async_computation.12 | async-start | bytes 4718592 | tf_op jit(solution)/shard_map/all_gather | solution.py:975
  550.0 147.5 %reduce-scatter.15.cloned.1.call-start = ((), (), s32[]{:S(2)}) async-start(), calls=%async_computation.16 | async-start | bytes 2621440 | tf_op jit(solution)/shard_map/reduce_scatter | solution.py:980
  550.7 166.9 %reduce-scatter.13.cloned.1.call-start = ((), (), s32[]{:S(2)}) async-start(), calls=%async_computation.15 | async-start | bytes 5242880 | tf_op jit(solution)/shard_map/reduce_scatter | solution.py:979
  566.8 359.0 %reduce-scatter.11.cloned.1.call-start = ((), (), s32[]{:S(2)}) async-start(), calls=%async_computation.14 | async-start | bytes 4718592 | tf_op jit(solution)/shard_map/reduce_scatter | solution.py:1122
  572.9 63.5 %collective-permute-start.73 = (bf16[128,2048]{1,0:T(8,128)(2,1)}, bf16[128,2048]{1,0:T(8,128)(2,1)}, u32[]{:S(2)}, u32[]{:S(2)}) collective-permute-start(bf16[128,2048]{1,0:T(8,128)(2,1)} %get-tuple-element.290), channel_id=1, source_target_pairs={{0,24},{8,16},{16,8},{24,0},{1,25},{9,17},{17,9},{25,1},{2,26},{10... | collective-permute-start | bytes 1572872 | tf_op jit(solution)/shard_map/ppermute | solution.py:270
  574.2 70.8 %collective-permute-start.72 = (bf16[128,2048]{1,0:T(8,128)(2,1)}, bf16[128,2048]{1,0:T(8,128)(2,1)}, u32[]{:S(2)}, u32[]{:S(2)}) collective-permute-start(bf16[128,2048]{1,0:T(8,128)(2,1)} %get-tuple-element.291), channel_id=1, source_target_pairs={{0,16},{8,24},{16,0},{24,8},{1,17},{9,25},{17,1},{25,9},{2,18},{10... | collective-permute-start | bytes 1572872 | tf_op jit(solution)/shard_map/ppermute | solution.py:270
  574.8 70.2 %collective-permute-start.71 = (bf16[128,2048]{1,0:T(8,128)(2,1)}, bf16[128,2048]{1,0:T(8,128)(2,1)}, u32[]{:S(2)}, u32[]{:S(2)}) collective-permute-start(bf16[128,2048]{1,0:T(8,128)(2,1)} %get-tuple-element.289), channel_id=1, source_target_pairs={{0,8},{8,0},{16,24},{24,16},{1,9},{9,1},{17,25},{25,17},{2,10},{10... | collective-permute-start | bytes 1572872 | tf_op jit(solution)/shard_map/ppermute | solution.py:270
  577.6 67.4 %collective-permute-start.76 = (bf16[128,2048]{1,0:T(8,128)(2,1)}, bf16[128,2048]{1,0:T(8,128)(2,1)}, u32[]{:S(2)}, u32[]{:S(2)}) collective-permute-start(bf16[128,2048]{1,0:T(8,128)(2,1)} %get-tuple-element.293), channel_id=1, source_target_pairs={{0,24},{8,16},{16,8},{24,0},{1,25},{9,17},{17,9},{25,1},{2,26},{10... | collective-permute-start | bytes 1572872 | tf_op jit(solution)/shard_map/ppermute | solution.py:270
  578.9 66.1 %collective-permute-start.75 = (bf16[128,2048]{1,0:T(8,128)(2,1)}, bf16[128,2048]{1,0:T(8,128)(2,1)}, u32[]{:S(2)}, u32[]{:S(2)}) collective-permute-start(bf16[128,2048]{1,0:T(8,128)(2,1)} %get-tuple-element.294), channel_id=1, source_target_pairs={{0,16},{8,24},{16,0},{24,8},{1,17},{9,25},{17,1},{25,9},{2,18},{10... | collective-permute-start | bytes 1572872 | tf_op jit(solution)/shard_map/ppermute | solution.py:270
  753.7 41.8 %collective-permute-start.83 = (bf16[512,768]{1,0:T(8,128)(2,1)}, bf16[512,768]{1,0:T(8,128)(2,1)}, u32[]{:S(2)}, u32[]{:S(2)}) collective-permute-start(bf16[512,768]{1,0:T(8,128)(2,1)} %get-tuple-element.284), channel_id=1, source_target_pairs={{0,24},{8,16},{16,8},{24,0},{1,25},{9,17},{17,9},{25,1},{2,26},{10... | collective-permute-start | bytes 2359304 | tf_op jit(solution)/shard_map/ppermute | solution.py:270
  756.1 39.5 %collective-permute-start.82 = (bf16[512,768]{1,0:T(8,128)(2,1)}, bf16[512,768]{1,0:T(8,128)(2,1)}, u32[]{:S(2)}, u32[]{:S(2)}) collective-permute-start(bf16[512,768]{1,0:T(8,128)(2,1)} %get-tuple-element.285), channel_id=1, source_target_pairs={{0,16},{8,24},{16,0},{24,8},{1,17},{9,25},{17,1},{25,9},{2,18},{10... | collective-permute-start | bytes 2359304 | tf_op jit(solution)/shard_map/ppermute | solution.py:270
  756.6 38.9 %collective-permute-start.81 = (bf16[512,768]{1,0:T(8,128)(2,1)}, bf16[512,768]{1,0:T(8,128)(2,1)}, u32[]{:S(2)}, u32[]{:S(2)}) collective-permute-start(bf16[512,768]{1,0:T(8,128)(2,1)} %get-tuple-element.283), channel_id=1, source_target_pairs={{0,8},{8,0},{16,24},{24,16},{1,9},{9,1},{17,25},{25,17},{2,10},{10... | collective-permute-start | bytes 2359304 | tf_op jit(solution)/shard_map/ppermute | solution.py:270
  775.0 33.7 %all-to-all-start = ((bf16[8,64,1024]{2,1,0:T(8,128)(2,1)}), bf16[8,64,1024]{2,1,0:T(8,128)(2,1)}, u32[]{:S(2)}, u32[]{:S(2)}) async-start(bf16[8,64,1024]{2,1,0:T(8,128)(2,1)} %bitcast.342), calls=%async_computation.4 | async-start | bytes 2097152 | tf_op jit(solution)/shard_map/all_to_all | solution.py:1036
  779.7 146.1 %reduce-scatter.17.cloned.1.call-start = ((), (), s32[]{:S(2)}) async-start(), calls=%async_computation.17 | async-start | bytes 4718592 | tf_op jit(solution)/shard_map/reduce_scatter | solution.py:1122
  823.4 53.7 %collective-permute-start.96 = (bf16[512,1024]{1,0:T(8,128)(2,1)}, bf16[512,1024]{1,0:T(8,128)(2,1)}, u32[]{:S(2)}, u32[]{:S(2)}) collective-permute-start(bf16[512,1024]{1,0:T(8,128)(2,1)} %get-tuple-element.191), channel_id=1, source_target_pairs={{0,24},{8,16},{16,8},{24,0},{1,25},{9,17},{17,9},{25,1},{2,26},{10... | collective-permute-start | bytes 3145736 | tf_op jit(solution)/shard_map/ppermute | solution.py:270
  825.9 51.2 %collective-permute-start.95 = (bf16[512,1024]{1,0:T(8,128)(2,1)}, bf16[512,1024]{1,0:T(8,128)(2,1)}, u32[]{:S(2)}, u32[]{:S(2)}) collective-permute-start(bf16[512,1024]{1,0:T(8,128)(2,1)} %get-tuple-element.190), channel_id=1, source_target_pairs={{0,16},{8,24},{16,0},{24,8},{1,17},{9,25},{17,1},{25,9},{2,18},{10... | collective-permute-start | bytes 3145736 | tf_op jit(solution)/shard_map/ppermute | solution.py:270
  826.4 50.7 %collective-permute-start.94 = (bf16[512,1024]{1,0:T(8,128)(2,1)}, bf16[512,1024]{1,0:T(8,128)(2,1)}, u32[]{:S(2)}, u32[]{:S(2)}) collective-permute-start(bf16[512,1024]{1,0:T(8,128)(2,1)} %get-tuple-element.189), channel_id=1, source_target_pairs={{0,8},{8,0},{16,24},{24,16},{1,9},{9,1},{17,25},{25,17},{2,10},{10... | collective-permute-start | bytes 3145736 | tf_op jit(solution)/shard_map/ppermute | solution.py:270
  827.0 53.9 %all-to-all-start.1 = ((bf16[8,64,768]{2,1,0:T(8,128)(2,1)}), bf16[8,64,768]{2,1,0:T(8,128)(2,1)}, u32[]{:S(2)}, u32[]{:S(2)}) async-start(bf16[8,64,768]{2,1,0:T(8,128)(2,1)} %bitcast.122), calls=%async_computation.7 | async-start | bytes 1572864 | tf_op jit(solution)/shard_map/all_to_all | solution.py:987
  837.2 38.9 %collective-permute-start.98 = (f32[144,128]{1,0:T(8,128)S(1)}, f32[144,128]{1,0:T(8,128)S(1)}, u32[]{:S(2)}, u32[]{:S(2)}) collective-permute-start(f32[144,128]{1,0:T(8,128)S(1)} %add_add_fusion.5), channel_id=1, source_target_pairs={{0,4},{2,6},{4,0},{6,2},{1,5},{3,7},{5,1},{7,3},{8,12},{10,14},{12... | collective-permute-start | bytes 221192 | tf_op jit(solution)/shard_map/ppermute | solution.py:1114
  883.3 35.2 %all-to-all-start.2 = ((bf16[8,64,1024]{2,1,0:T(8,128)(2,1)}), bf16[8,64,1024]{2,1,0:T(8,128)(2,1)}, u32[]{:S(2)}, u32[]{:S(2)}) async-start(bf16[8,64,1024]{2,1,0:T(8,128)(2,1)} %bitcast.124), calls=%async_computation.8 | async-start | bytes 2097152 | tf_op jit(solution)/shard_map/all_to_all | solution.py:987
  (231 other events, 3805.3 us)
Sparse Core Ops, SparseCore 0:
  49.8 90.8 all-gather.5
  175.6 117.6 all-gather.11
  295.6 48.2 reduce-scatter.6
  355.3 48.7 reduce-scatter.8
  476.2 44.3 all-gather.9
  550.1 44.1 all-gather.7
  596.6 42.5 reduce-scatter.14
  641.6 76.0 reduce-scatter.12
  720.0 53.3 reduce-scatter.10
  823.5 69.1 reduce-scatter.16

commit v3 on v2

--- a/solution.py
+++ b/solution.py
@@ -270,9 +270,12 @@
     return lax.ppermute(block, axis, [(i, i ^ distance) for i in range(lax.axis_size(axis))])
 
 
+def gather_core(near):
+    return jnp.concatenate(near + [swap(piece, "c", 1) for piece in near], axis=0)
+
+
 def gather_plane(block):
-    near = [block] + [swap(block, "dp", k) for k in range(1, lax.axis_size("dp"))]
-    return jnp.concatenate(near + [swap(piece, "c", 1) for piece in near], axis=0)
+    return gather_core(from_dp(block))
 
 
 def scatter_core(partial):
@@ -798,11 +801,7 @@
         slot = lax.dynamic_index_in_dim(w_big, me ^ k, 0, keepdims=False)
         route = [(i, i ^ k) for i in range(team)]
         slots.append(lax.ppermute(slot, TEAM, route) if k else slot)
-    w_big = join_rows(slots, me)
-    if groups > 1:
-        w_big = lax.all_gather(w_big, "g", axis=0, tiled=True)
-    block_tokens = lax.all_gather(after(tokens, w_big), TEAM, axis=1, tiled=True)
-    block_tokens = block_tokens.reshape(rows, width)
+    w_big = slots
     ffn_block = w_down.shape[0]
     w_gu = w_gate_up.reshape(held, 2, dp, line, plane // dp, ffn_block).transpose(4, 2, 0, 1, 3, 5)
     w_gu = w_gu.reshape(plane // dp, dp, held, 2 * line * ffn_block)
@@ -817,7 +816,7 @@
                 route = [(2 * a + b, 2 * (a ^ k) + (b ^ j)) for a in range(dp) for b in range(2)]
                 slot = lax.ppermute(slot, PLANE, route)
             slots.append(slot)
-    w_gu = jnp.stack(slots)
+    w_gu = slots
     ratio = team // dp
     part = seq_size // ratio
     attn_rows, mamba_rows = w_attn_out.shape[0], w_mamba_out.shape[0]
@@ -829,15 +828,24 @@
     for k in range(dp):
         quarter = lax.dynamic_index_in_dim(w_out, mine_dp ^ k, 1, keepdims=False)
         quarters.append(swap(quarter, "dp", k) if k else quarter)
-    w_out = jnp.stack(quarters)
+    w_big, w_gu, quarters = lax.optimization_barrier((w_big, w_gu, quarters))
+    w_big = join_rows(w_big, me)
+    if groups > 1:
+        w_big = lax.all_gather(w_big, "g", axis=0, tiled=True)
+    block_tokens = lax.all_gather(after(tokens, w_big), TEAM, axis=1, tiled=True)
+    block_tokens = block_tokens.reshape(rows, width)
     positions = start[0] + jnp.arange(block_len, dtype=jnp.int32)
     cosine, sine = rope_tables(positions, HD)
-    w_big, w_gu, w_out, cosine, sine = lax.optimization_barrier(
-        (w_big, w_gu, w_out, cosine, sine)
-    )
     blocks = parts_dp(w_big)
     key_at = inner + query
     others = [swap(part[:, inner + key_at :], "c", 1) for part, _, _ in blocks]
+    columns = 2 * line * ffn_block
+    folded = [w_down[:, i * columns : (i + 1) * columns] for i in range(width // columns)]
+    w_ffn = jnp.concatenate([*w_gu, *folded], axis=0)
+    w_out = jnp.stack(quarters)
+    others, w_ffn, w_out, cosine, sine = lax.optimization_barrier(
+        (others, w_ffn, w_out, cosine, sine)
+    )
     w_early, w_late, rest = join_weights(blocks, others, inner, key_at, shared, kv_head)
     gain_all = rest[:, :2].astype(f32).T
     conv_all = rest[:, 2 : 2 + conv_cols]
@@ -853,12 +861,9 @@
         lax.dynamic_slice_in_dim(head_params, me * heads, heads, 1), ((0, 5), (0, 128 - heads))
     )
     turn = (me * heads).astype(jnp.int32).reshape(1)
-    block_tokens, w_gu, w_early, w_late, gain_all = lax.optimization_barrier(
-        (block_tokens, w_gu, w_early, w_late, gain_all)
-    )
-    columns = w_gu.shape[-1]
-    folded = [w_down[:, i * columns : (i + 1) * columns] for i in range(width // columns)]
-    w_ffn = jnp.concatenate([w_gu.reshape(-1, columns), *folded], axis=0)
+    block_tokens, w_ffn, w_early, w_late, gain_all = lax.optimization_barrier(
+        (block_tokens, w_ffn, w_early, w_late, gain_all)
+    )
     w_ffn = lax.all_gather(w_ffn, LINE, axis=0, tiled=False).reshape(line, -1, columns)
     my_seq = lax.axis_index(SEQ)
     w_out = after(w_out, block_tokens)
@@ -946,10 +951,11 @@
     for s in range(seqs):
         hidden.append(tokens[s].astype(f32) + valid[s] * mix[s].astype(f32))
         norm2_f, norm2_pull = jax.vjp(lambda h: rms_norm(h, gain_all[1]), hidden[s])
-        norm2.append(gather_plane(norm2_f.astype(bf16)))
+        near = from_dp(norm2_f.astype(bf16))
         if s > 0:
-            norm2[s], local = lax.optimization_barrier((norm2[s], local))
+            near, local = lax.optimization_barrier((near, local))
             grad_mix.append(lax.all_gather(local, TEAM, axis=0, tiled=True))
+        norm2.append(gather_core(near))
         gate_up = dot(norm2[s], w_gu)
         gate, upper = gate_up[:, :units], gate_up[:, units:]
         sig_gate = sigmoid(gate)
@@ -961,24 +967,18 @@
         partial = dot_last(grad_gu[s], w_gu).astype(bf16)
         if s < seqs - 1:
             mix[s + 1] = after(mix[s + 1], partial)
-        (grad_hidden_norm,) = norm2_pull(scatter_plane(partial))
+        ffn.append(dot(act[s], w_dn).astype(bf16))
+        near = scatter_core(partial)
+        if s == seqs - 1:
+            ffn = [scatter_core(part_ffn) for part_ffn in ffn]
+            grad_mix[0], near, ffn = lax.optimization_barrier((grad_mix[0], near, ffn))
+        (grad_hidden_norm,) = norm2_pull(scatter_near(near))
         grad_hidden.append(cot[s] + grad_hidden_norm)
         local = (valid[s] * grad_hidden[s]).astype(bf16)
-        ffn.append(dot(act[s], w_dn).astype(bf16))
-    grad_w_gu = sum(map(dot_first, norm2, grad_gu)).astype(bf16)
-    grad_w_dn = sum(map(dot_first, act, grad_ffn)).astype(bf16)
-    grad_w_gu = grad_w_gu.reshape(dp, line, plane // dp, held, 2 * line * ffn_block)
-    grad_w_gu = grad_w_gu.transpose(1, 0, 2, 3, 4).reshape(width, -1)
-    local, grad_w_gu, grad_w_dn, *ffn = lax.optimization_barrier(
-        (local, grad_w_gu, grad_w_dn, *ffn)
-    )
-    grad_mix.append(lax.all_gather(local, TEAM, axis=0, tiled=True))
-    grad_mix[0], grad_w_gu, grad_w_dn = lax.optimization_barrier(
-        (grad_mix[0], grad_w_gu, grad_w_dn)
-    )
-    grad_w_gu = lax.psum_scatter(grad_w_gu, LINE, scatter_dimension=0, tiled=True)
-    grad_down = lax.psum_scatter(grad_w_dn, LINE, scatter_dimension=0, tiled=True).astype(f32)
-    ffn = [scatter_core(after(partial, local)) for partial in ffn]
+
+    own_conv = conv_params.shape[1]
+    rest_size = (KW + 1) * own_conv + 3 * MH
+    rest_cols = -(-rest_size // held)
 
     def to_owners(partial):
         if groups > 1:
@@ -999,18 +999,20 @@
         grad_head = lax.dynamic_update_slice_in_dim(
             jnp.zeros((3, MH), f32), ghead[:3, :heads], me * heads, 1
         )
-        flat = jnp.concatenate([grad_conv.reshape(-1), grad_head.reshape(-1)])
-        return jnp.pad(flat, (0, -flat.shape[0] % 1024)).reshape(-1, 128)
+        rest = jnp.concatenate(
+            [
+                grad_conv.reshape(KW + 1, devices, -1).transpose(1, 0, 2).reshape(devices, -1),
+                jnp.broadcast_to(grad_head.reshape(1, -1), (devices, 3 * MH)),
+            ],
+            axis=1,
+        )
+        rest = jnp.pad(rest, ((0, 0), (0, held * rest_cols - rest_size)))
+        return rest.reshape(width, rest_cols)
 
     dearly, dlate, grad_norm1 = [], [], []
     gconv, ghead = 0.0, 0.0
     for s in range(seqs):
         grad_mixed_in = dot_last(grad_mix[s], w_out)
-        if s == 0:
-            grad_mixed_in, *ffn = lax.optimization_barrier((grad_mixed_in, *ffn))
-            ffn = [scatter_near(near) for near in ffn]
-            mixed = [(hidden[n] + valid[n] * ffn[n]).astype(bf16) for n in range(seqs)]
-            mixed = jnp.stack(mixed)
         if s == seqs - 1:
             grad_w_out = sum(map(dot_first, mixed_in, grad_mix)).astype(bf16)
             grad_mixed_in, grad_w_out = lax.optimization_barrier((grad_mixed_in, grad_w_out))
@@ -1018,6 +1020,13 @@
             if groups > 1:
                 grad_w_out = lax.psum(grad_w_out, "g")
             grad_w_out = grad_w_out.astype(bf16)
+        if s == 0:
+            grad_mixed_in, local = lax.optimization_barrier((grad_mixed_in, local))
+            if seqs > 1:
+                grad_mix.append(lax.all_gather(local, TEAM, axis=0, tiled=True))
+            ffn = [scatter_near(near) for near in after(ffn, local)]
+            mixed = [(hidden[n] + valid[n] * ffn[n]).astype(bf16) for n in range(seqs)]
+            mixed = jnp.stack(mixed)
         dq, dk, dv = attend_back(lengths, start, q, k, v, grad_mixed_in, logs[s], span, s)
         if groups > 1:
             dk = lax.psum_scatter(dk, "g", scatter_dimension=1, tiled=True)
@@ -1030,12 +1039,7 @@
         dearly.append(jnp.concatenate([dz.astype(bf16), dq, dk, dv[0].astype(bf16)], axis=1))
         if s == seqs - 1:
             grad_early = dot_first(norm1, jnp.concatenate(dearly, axis=0)).astype(bf16)
-            grad_mixed_in, grad_early, grad_w_out, grad_w_gu = lax.optimization_barrier(
-                (grad_mixed_in, grad_early, grad_w_out, grad_w_gu)
-            )
-            grad_w_gu = lax.all_to_all(
-                grad_w_gu.reshape(plane, held, 2 * line * ffn_block), PLANE, 0, 0, tiled=True
-            )
+            early_cuts = cuts_dp(grad_early, 0)
             grad_w_out = jnp.concatenate(
                 [
                     grad_w_out[inner:].reshape(part, attn_rows, cut),
@@ -1043,29 +1047,17 @@
                 ],
                 axis=1,
             )
-            if part == dp and groups == 1:
-                parts = []
-                for n in range(part):
-                    piece = lax.dynamic_index_in_dim(
-                        grad_w_out, (me // ratio) ^ n, 0, keepdims=False
-                    )
-                    route = [(ratio * ((i % part) ^ n) + i // part, i) for i in range(team)]
-                    parts.append(lax.ppermute(piece, TEAM, route))
-                grad_w_out = jnp.stack(parts)
-            else:
-                grad_w_out = lax.dynamic_update_slice_in_dim(
-                    jnp.zeros((seq_size, out_rows, cut), bf16),
-                    grad_w_out,
-                    (me % ratio) * part,
-                    0,
-                )
-                grad_w_out = lax.all_to_all(grad_w_out, SEQ, 0, 0, tiled=True)
-                grad_w_out = grad_w_out.reshape(groups, dp, ratio, out_rows, cut)[0]
-                grad_w_out = lax.dynamic_index_in_dim(
-                    grad_w_out, my_seq // part, 1, keepdims=False
-                )
-                grad_w_out = jnp.take(grad_w_out, (my_seq % part % dp) ^ jnp.arange(dp), axis=0)
-            grad_early = scatter_dp(grad_early, 0)
+            grad_w_out = lax.dynamic_update_slice_in_dim(
+                jnp.zeros((seq_size, out_rows, cut), bf16), grad_w_out, (me % ratio) * part, 0
+            )
+            grad_w_gu = lax.all_to_all(
+                grad_w_gu.reshape(plane, held, 2 * line * ffn_block), PLANE, 0, 0, tiled=True
+            )
+            grad_mixed_in, early_cuts, grad_w_out, grad_w_gu = lax.optimization_barrier(
+                (grad_mixed_in, early_cuts, grad_w_out, grad_w_gu)
+            )
+            grad_early = sum_cuts(early_cuts)
+            grad_w_out = lax.all_to_all(grad_w_out, SEQ, 0, 0, tiled=True)
         back = functools.partial(core_back, seq=s, heads=heads, span=span)
         halo = halos[s : s + 1]
         dlate_s, gconv_s, ghead_s, dinit, dfirst = back(
@@ -1087,49 +1079,50 @@
             rim = jnp.concatenate([rim[:, :inner], step_gap, rim[:, inner:]], axis=1)
             dlate_s = (dlate_s.astype(f32) + rim).astype(bf16)
         gconv, ghead = gconv + gconv_s, ghead + ghead_s
+        if s == 0:
+            dlate_s, norm2, act = lax.optimization_barrier((dlate_s, norm2, act))
+            grad_w_gu = sum(map(dot_first, norm2, grad_gu)).astype(bf16)
+            grad_w_gu = grad_w_gu.reshape(dp, line, plane // dp, held, 2 * line * ffn_block)
+            grad_w_gu = grad_w_gu.transpose(1, 0, 2, 3, 4).reshape(width, -1)
+            dlate_s, grad_w_gu = lax.optimization_barrier((dlate_s, grad_w_gu))
+            grad_w_gu = lax.psum_scatter(grad_w_gu, LINE, scatter_dimension=0, tiled=True)
         if s == seqs - 1:
-            grad_late = dot_first(norm1, jnp.concatenate([*dlate, dlate_s], axis=0)).astype(bf16)
-            small = small_grads(gconv, ghead)
-            small = small + swap(small, "c", 1)
-            late_cuts = cuts_dp(grad_late, 0)
-            parts = []
-            for n in range(dp):
-                piece = lax.dynamic_index_in_dim(
-                    grad_w_out, (my_seq % part % dp) ^ mine_dp ^ n, 0, keepdims=False
-                )
-                parts.append(swap(piece, "dp", n) if n else piece)
-            dlate_s, small, grad_early, parts, late_cuts, grad_w_gu = lax.optimization_barrier(
-                (dlate_s, small, grad_early, parts, late_cuts, grad_w_gu)
+            dlate_s, grad_early, grad_w_out = lax.optimization_barrier(
+                (dlate_s, grad_early, grad_w_out)
             )
+            grad_late = dot_first(norm1, jnp.concatenate([*dlate, dlate_s], axis=0))
+            rest_at = inner + MH
+            grad_late = grad_late + jnp.pad(
+                small_grads(gconv, ghead),
+                ((0, 0), (rest_at, grad_late.shape[1] - rest_at - rest_cols)),
+            )
+            late_cuts = cuts_dp(grad_late.astype(bf16), 0)
+            dlate_s, late_cuts = lax.optimization_barrier((dlate_s, late_cuts))
             grad_late = sum_cuts(late_cuts)
-            small = sum(swap(small, "dp", n) if n else small for n in range(dp))
         dlate.append(dlate_s)
         partial = (dot_last(dearly[s], w_early) + dot_last(dlate_s, w_late)).astype(bf16)
         if s == seqs - 1:
-            grad_w_out = jnp.take(jnp.stack(parts), mine_dp ^ jnp.arange(dp), axis=0)
+            grad_w_out = grad_w_out.reshape(groups, dp, ratio, out_rows, cut)[0]
+            grad_w_out = lax.dynamic_index_in_dim(grad_w_out, my_seq // part, 1, keepdims=False)
+            grad_w_out = lax.all_to_all(after(grad_w_out, partial), "dp", 0, 0, tiled=True)
             grad_w_out = grad_w_out.transpose(1, 0, 2).reshape(out_rows, width).astype(f32)
-            partial, grad_down, small = lax.optimization_barrier((partial, grad_down, small))
-            size_z = lax.axis_size("z")
-            small = sum(
-                lax.ppermute(small, "z", [(i, (i + n) % size_z) for i in range(size_z)])
-                if n
-                else small
-                for n in range(size_z)
-            )
-            if groups > 1:
-                small = lax.psum(small, "g")
             grad_early = to_owners(grad_early)
         grad_norm1.append(lax.psum_scatter(partial, TEAM, scatter_dimension=0, tiled=True))
         if s == 0:
-            grad_mix[1:], mixed, _ = lax.optimization_barrier((grad_mix[1:], mixed, partial))
+            grad_w_dn = sum(map(dot_first, act, after(grad_ffn, partial))).astype(bf16)
+            grad_mix[1:], grad_w_dn, mixed = lax.optimization_barrier(
+                (grad_mix[1:], grad_w_dn, mixed)
+            )
+            grad_down = lax.psum_scatter(grad_w_dn, LINE, scatter_dimension=0, tiled=True)
+            grad_down = grad_down.astype(f32)
     grad_gate_up = (
         grad_w_gu.reshape(dp, plane // dp, held, 2, line, ffn_block)
         .transpose(2, 3, 0, 4, 1, 5)
         .reshape(held, -1)
         .astype(f32)
     )
-    grad_late, grad_w_out, grad_early, small = lax.optimization_barrier(
-        (grad_late, grad_w_out, grad_early, small)
+    grad_late, grad_w_out, grad_early = lax.optimization_barrier(
+        (grad_late, grad_w_out, grad_early)
     )
     grad_late = to_owners(grad_late)
     grad_z = grad_early[:, :, :inner].reshape(held, MI)
@@ -1149,13 +1142,10 @@
         jnp.sum(w_gate_up.astype(f32) * grad_gate_up, 1),
     ]
     grad_gains = jnp.stack(grad_gains) / gains.astype(f32)
-    own_conv = conv_params.shape[1]
-    small = small.reshape(-1)
-    conv_end = (KW + 1) * conv_params.shape[1] * devices
-    grad_conv = lax.dynamic_slice_in_dim(
-        small[:conv_end].reshape(KW + 1, -1), lax.axis_index(ALL) * own_conv, own_conv, 1
-    )
-    head_total = small[conv_end : conv_end + 3 * MH].reshape(3, MH)
+    rest = jnp.sum(grad_late[:, :, rest_at : rest_at + rest_cols], axis=1).reshape(-1)
+    conv_end = (KW + 1) * own_conv
+    grad_conv = rest[:conv_end].reshape(KW + 1, own_conv)
+    head_total = rest[conv_end:rest_size].reshape(3, MH)
     grad_tokens = []
     for s in range(seqs):
         _, norm1_pull = jax.vjp(lambda v: rms_norm(v, gain_all[0]), tokens[s].astype(f32))

time: 947 us -> 919 us (0.970)
  starting transfers between devices: 129 us -> 109 us
  local copies, waits for them, and re-layouts: 107 us -> 123 us
    ppermute x7 -> x0, waiting for transfers between devices: 29.5 us -> none  [the longest x3 26.3 us: body(): lax.ppermute(small, 'z', [(i, (i + n) % size_z) for i in range(size_z)])]
    ppermute x7 -> x0, starting transfers between devices: 21.4 us -> none  [the longest x3 15.3 us: body(): lax.ppermute(small, 'z', [(i, (i + n) % size_z) for i in range(size_z)])]
    unnamed x336 -> x327, local copies, waits for them, and re-layouts: 38.5 us -> 59 us
    reduce_scatter x1, waiting for transfers between devices: 17.9 us -> 0.01 us  [body(): lax.psum_scatter(grad_w_gu, LINE, scatter_dimension=0, tiled=True)]
    all_gather x1, waiting for transfers between devices: 0.02 us -> 17.7 us  [body(): lax.all_gather(after(tokens, w_big), TEAM, axis=1, tiled=True)]
    ppermute x75 -> x68, waiting for transfers between devices: 178 us -> 189 us  [swap(): lax.ppermute(block, axis, [(i, i ^ distance) for i in range(lax.axis_size...]
    ppermute x75 -> x68, starting transfers between devices: 61.7 us -> 62.1 us  [swap(): lax.ppermute(block, axis, [(i, i ^ distance) for i in range(lax.axis_size...]
  transfers between devices with their start and end apart: 113 -> 101, of which waited for: 39 -> 34; matrix products, arithmetic and copies ran while one was open for 35% -> 36% of each run, Pallas kernels for 13% -> 14%
where the time goes in v3:
time: 919 us; the launch traced here: 909 us
  waiting for transfers between devices  280 us (30%)
  matrix products  174 us (19%)
  Pallas kernels  127 us (14%)
  local copies, waits for them, and re-layouts  123 us (13%)
  starting transfers between devices  109 us (12%)
  other arithmetic  80.2 us (9%)
  between operations  17.2 us (2%)
    ppermute x68, waiting for transfers between devices, swap(): lax.ppermute(block, axis, [(i, i ^ distance) for i in range(lax.axis_size...  189 us
    dot_general x8, matrix products, dot_first(): lax.dot_general(left, right, (((0,), (0,)), ((), ())), preferred_element_...  63.8 us
    ppermute x68, starting transfers between devices, swap(): lax.ppermute(block, axis, [(i, i ^ distance) for i in range(lax.axis_size...  62.1 us
    pallas_call x2, Pallas kernels, core_back(): pl.pallas_call(functools.partial(core_back_kernel, heads=heads, span=span...  61.4 us
    dot_general x10, matrix products, dot_last(): lax.dot_general(left, right, (((1,), (1,)), ((), ())), preferred_element_...  59.9 us
    unnamed x327, local copies, waits for them, and re-layouts  59 us
    dot_general x8, matrix products, dot(): return jnp.dot(left, right, preferred_element_type=f32, precision=precision)  49.9 us
    all_gather x1, waiting for transfers between devices, body(): lax.all_gather(w_ffn, LINE, axis=0, tiled=False).reshape(line, -1, columns)  30.8 us
  transfers between devices with their start and end apart: 101, of which 34 were waited for; matrix products, arithmetic and copies ran while one was open for 36% of the time, Pallas kernels for 14%

profile of v3, /device:TPU:0, one launch (start us, length us, event | category | flops | bytes accessed | tf_op | source)
XLA Modules:
  0.0 909.2 jit_solution(1471482856822930917)
XLA Ops:
  44.4 17.2 %collective-permute-done.3.refs_4_ = bf16[64,1536]{1,0:T(8,128)(2,1)S(1)} collective-permute-done((bf16[64,1536]{1,0:T(8,128)(2,1)}, bf16[64,1536]{1,0:T(8,128)(2,1)S(1)}, u32[]{:S(2)}, u32[]{:S(2)}) %collective-permute-start.3) | collective-permute-done | bytes 196640 | tf_op jit(solution)/shard_map/ppermute | solution.py:803
  77.8 21.9 %collective-permute-done.18.refs_1_ = bf16[512,1536]{1,0:T(8,128)(2,1)} collective-permute-done((bf16[512,1536]{1,0:T(8,128)(2,1)S(1)}, bf16[512,1536]{1,0:T(8,128)(2,1)}, u32[]{:S(2)}, u32[]{:S(2)}) %collective-permute-start.18) | collective-permute-done | bytes 1572896 | tf_op jit(solution)/shard_map/ppermute | solution.py:270
  129.3 6.6 join_weights.1
  137.3 17.7 %all-gather.6.cloned.1.call-done = bf16[2,1024,2048]{2,1,0:T(8,128)(2,1)} async-done(((bf16[2,128,2048]{2,1,0:T(8,128)(2,1)}), bf16[2,1024,2048]{2,1,0:T(8,128)(2,1)}) %all-gather.6.cloned.1.call-update) | async-done | bytes 8388624 | tf_op jit(solution)/shard_map/all_gather | solution.py:835
  169.6 14.7 %fusion.82.x_ref.bc_ref.dt_ref = f32[2048,1024]{1,0:T(8,128)} fusion(bf16[2048,1024]{1,0:T(8,128)(2,1)} %get-tuple-element.170, bf16[2048,2048]{1,0:T(8,128)(2,1)} %bitcast.279, f32[2048]{0:T(1024)S(1)} %get-tuple-element.310, f32[2048]{0:T(1024)S(1)} %add_rsqrt_fusion), kind=kOutput, calls=%fused_computation.306 | convolution fusion | flops 8606711808 | bytes 20987904 | tf_op jit(solution)/shard_map/dot_general | solution.py:63
  184.3 9.2 %fusion.84.z_ref = f32[2048,768]{1,0:T(8,128)S(1)} fusion(bf16[2048,768]{1,0:T(8,128)(2,1)S(1)} %copy-done.129, bf16[2048,2048]{1,0:T(8,128)(2,1)} %bitcast.280, f32[2048]{0:T(1024)S(1)} %get-tuple-element.310, f32[2048]{0:T(1024)S(1)} %add_rsqrt_fusion), kind=kOutput, calls=%fused_computation.307 | convolution fusion | flops 6459228160 | bytes 17842176 | tf_op jit(solution)/shard_map/dot_general | solution.py:63
  201.3 14.4 %core_fore.2 = (bf16[1024,384]{1,0:T(8,128)(2,1)S(1)}, f32[1024,384]{1,0:T(8,128)S(1)}, f32[1,4,384,256]{3,2,1,0:T(8,128)S(1)}, f32[1,384,256]{2,1,0:T(8,128)}, f32[1,8,128]{2,1,0:T(8,128)}) custom-call(s32[1]{0:T(128)} %bitcast.2.turn_ref, f32[2048,1024]{1,0:T(8,128)} %fusion.82.x_ref.bc_ref.dt_ref, f32[2048,1024]{1,0:T(8,128)} %fusion.82.x_ref.bc_ref.dt_ref, ...), custom_call_target="tpu_custom_call" | custom-call | flops 12999999488 | bytes 8781824 | tf_op jit(solution)/shard_map/core_fore/pallas_call | solution.py:519
  232.0 14.1 %core_fore.3 = (bf16[1024,384]{1,0:T(8,128)(2,1)}, f32[1024,384]{1,0:T(8,128)S(1)}, f32[1,4,384,256]{3,2,1,0:T(8,128)S(1)}, f32[1,384,256]{2,1,0:T(8,128)}, f32[1,8,128]{2,1,0:T(8,128)}) custom-call(s32[1]{0:T(128)} %bitcast.2.turn_ref, f32[2048,1024]{1,0:T(8,128)} %fusion.82.x_ref.bc_ref.dt_ref, f32[2048,1024]{1,0:T(8,128)} %fusion.82.x_ref.bc_ref.dt_ref, ...), custom_call_target="tpu_custom_call" | custom-call | flops 12999999488 | bytes 8781824 | tf_op jit(solution)/shard_map/core_fore/pallas_call | solution.py:519
  253.8 30.8 %all-gather.12.cloned.1.call-done = bf16[3072,1024]{1,0:T(8,128)(2,1)} async-done(((bf16[768,1024]{1,0:T(8,128)(2,1)}), bf16[3072,1024]{1,0:T(8,128)(2,1)}) %all-gather.12.cloned.1.call-update) | async-done | bytes 6291472 | tf_op jit(solution)/shard_map/all_gather | solution.py:867
  295.3 8.9 collective-permute-done.40
  305.7 10.0 %collective-permute-done.41 = bf16[128,2048]{1,0:T(8,128)(2,1)S(1)} collective-permute-done((bf16[128,2048]{1,0:T(8,128)(2,1)S(1)}, bf16[128,2048]{1,0:T(8,128)(2,1)S(1)}, u32[]{:S(2)}, u32[]{:S(2)}) %collective-permute-start.41) | collective-permute-done | bytes 524320 | tf_op jit(solution)/shard_map/ppermute | solution.py:270
  317.5 9.1 %collective-permute-done.33 = bf16[128,2048]{1,0:T(8,128)(2,1)S(1)} collective-permute-done((bf16[128,2048]{1,0:T(8,128)(2,1)S(1)}, bf16[128,2048]{1,0:T(8,128)(2,1)S(1)}, u32[]{:S(2)}, u32[]{:S(2)}) %collective-permute-start.33) | collective-permute-done | bytes 524320 | tf_op jit(solution)/shard_map/ppermute | solution.py:270
  327.5 10.6 %collective-permute-done.34 = bf16[128,2048]{1,0:T(8,128)(2,1)S(1)} collective-permute-done((bf16[128,2048]{1,0:T(8,128)(2,1)S(1)}, bf16[128,2048]{1,0:T(8,128)(2,1)S(1)}, u32[]{:S(2)}, u32[]{:S(2)}) %collective-permute-start.34) | collective-permute-done | bytes 524320 | tf_op jit(solution)/shard_map/ppermute | solution.py:270
  365.3 8.5 collective-permute-done.48
  381.9 6.3 multiply_convert_fusion.5
  404.7 11.6 %collective-permute-done.58 = bf16[128,2048]{1,0:T(8,128)(2,1)} collective-permute-done((bf16[128,2048]{1,0:T(8,128)(2,1)}, bf16[128,2048]{1,0:T(8,128)(2,1)}, u32[]{:S(2)}, u32[]{:S(2)}) %collective-permute-start.58) | collective-permute-done | bytes 524320 | tf_op jit(solution)/shard_map/ppermute | solution.py:270
  416.2 12.4 %collective-permute-done.59 = bf16[128,2048]{1,0:T(8,128)(2,1)} collective-permute-done((bf16[128,2048]{1,0:T(8,128)(2,1)}, bf16[128,2048]{1,0:T(8,128)(2,1)}, u32[]{:S(2)}, u32[]{:S(2)}) %collective-permute-start.59) | collective-permute-done | bytes 524320 | tf_op jit(solution)/shard_map/ppermute | solution.py:270
  450.3 10.7 %collective-permute-done.55 = bf16[128,2048]{1,0:T(8,128)(2,1)S(1)} collective-permute-done((bf16[128,2048]{1,0:T(8,128)(2,1)S(1)}, bf16[128,2048]{1,0:T(8,128)(2,1)S(1)}, u32[]{:S(2)}, u32[]{:S(2)}) %collective-permute-start.55) | collective-permute-done | bytes 524320 | tf_op jit(solution)/shard_map/ppermute | solution.py:270
  478.3 6.8 fusion.100
  506.6 6.5 all-gather.8.cloned.1.call-done
  529.4 11.7 %collective-permute-done.69 = bf16[128,2048]{1,0:T(8,128)(2,1)S(1)} collective-permute-done((bf16[128,2048]{1,0:T(8,128)(2,1)S(1)}, bf16[128,2048]{1,0:T(8,128)(2,1)S(1)}, u32[]{:S(2)}, u32[]{:S(2)}) %collective-permute-start.69) | collective-permute-done | bytes 524320 | tf_op jit(solution)/shard_map/ppermute | solution.py:270
  548.4 30.9 %core_back.2 = (bf16[1024,1024]{1,0:T(8,128)(2,1)S(1)}, f32[8,896]{1,0:T(8,128)S(1)}, f32[8,128]{1,0:T(8,128)S(1)}, f32[1,384,256]{2,1,0:T(8,128)}, f32[1,8,896]{2,1,0:T(8,128)}) custom-call(s32[1]{0:T(128)} %bitcast.2.turn_ref, f32[2048,1024]{1,0:T(8,128)} %fusion.82.x_ref.bc_ref.dt_ref, f32[2048,1024]{1,0:T(8,128)} %fusion.82.x_ref.bc_ref.dt_ref, ...), custom_call_target="tpu_custom_call" | custom-call | flops 30000001024 | bytes 9961472 | tf_op jit(solution)/shard_map/core_back/pallas_call | solution.py:690
  579.3 10.8 %fusion.40 = f32[2048,1024]{1,0:T(8,128)} fusion(bf16[1024,2048]{1,0:T(8,128)(2,1)} %constant_dynamic-update-slice_fusion.32, bf16[1024,512]{0,1:T(8,128)(2,1)S(1)} %copy-done.141, bf16[1024,512]{0,1:T(8,128)(2,1)S(1)} %copy-done.139), kind=kOutput, calls=%fused_computation.89 | convolution fusion | flops 4299161600 | bytes 14680064 | tf_op jit(solution)/shard_map/dot_general | solution.py:67
  590.1 8.6 add_convert_fusion.3
  627.9 8.4 add_convert_fusion.2
  685.7 12.5 %convolution_convert_fusion.6 = bf16[2048,768]{1,0:T(8,128)(2,1)} fusion(bf16[1024,128]{1,0:T(8,128)(2,1)S(1)} %convert_bitcast_fusion.4, bf16[1024,128]{1,0:T(8,128)(2,1)S(1)} %get-tuple-element.388, bf16[1024,128]{1,0:T(8,128)(2,1)S(1)} %get-tuple-element.387, bf16[1024,384]{1,0:T(8,128)(2,1)S(1)} %multiply_convert_fusion.6, ...), kind=kOutput, calls=%fused_computation.25 | convolution fusion | flops 6485966848 | bytes 14696448 | tf_op jit(solution)/shard_map/dot_general | solution.py:67
  702.0 9.2 %fusion.32 = f32[1024,2048]{1,0:T(8,128)} fusion(bf16[2048,768]{1,0:T(8,128)(2,1)} %get-tuple-element.169, bf16[1024,128]{1,0:T(8,128)(2,1)} %copy-done.90, bf16[1024,128]{1,0:T(8,128)(2,1)} %copy-done.92, bf16[1024,128]{1,0:T(8,128)(2,1)} %copy-done.91, bf16[1024,384]{1,0:T(8,128)(2,1)} %copy-done.75), kind=kOutput, calls=%fused_computation.73 | convolution fusion | flops 3227516928 | bytes 13107200 | tf_op jit(solution)/shard_map/dot_general | solution.py:73
  725.2 30.6 %core_back.3 = (bf16[1024,1024]{1,0:T(8,128)(2,1)S(1)}, f32[8,896]{1,0:T(8,128)S(1)}, f32[8,128]{1,0:T(8,128)S(1)}, f32[1,384,256]{2,1,0:T(8,128)}, f32[1,8,896]{2,1,0:T(8,128)}) custom-call(s32[1]{0:T(128)} %bitcast.2.turn_ref, f32[2048,1024]{1,0:T(8,128)} %fusion.82.x_ref.bc_ref.dt_ref, f32[2048,1024]{1,0:T(8,128)} %fusion.82.x_ref.bc_ref.dt_ref, ...), custom_call_target="tpu_custom_call" | custom-call | flops 30000001024 | bytes 9961472 | tf_op jit(solution)/shard_map/core_back/pallas_call | solution.py:690
  765.1 13.5 %add_convert_fusion.1 = bf16[2048,1024]{1,0:T(8,128)(2,1)S(1)} fusion(f32[2048,11]{1,0:T(8,128)S(1)} %reshape.328, bf16[1024,1024]{1,0:T(8,128)(2,1)} %copy-done.40, bf16[1024,1024]{1,0:T(8,128)(2,1)S(1)} %copy-done.39, bf16[2048,2048]{1,0:T(8,128)(2,1)} %bitcast.282, f32[2048]{0:T(1024)S(1)} %copy-done.106, f32[2048]{0:T(1024)S(1)} %copy-done.118), kind=kOutput, calls=%fused_computation.6 | convolution fusion | flops 8619294720 | bytes 16883712 | tf_op jit(solution)/shard_map/dot_general | solution.py:67
  782.6 8.4 add_convert_fusion
  810.5 17.9 %collective-permute-done.83 = bf16[512,1024]{1,0:T(8,128)(2,1)} collective-permute-done((bf16[512,1024]{1,0:T(8,128)(2,1)}, bf16[512,1024]{1,0:T(8,128)(2,1)}, u32[]{:S(2)}, u32[]{:S(2)}) %collective-permute-start.83) | collective-permute-done | bytes 1048608 | tf_op jit(solution)/shard_map/ppermute | solution.py:270
  828.3 20.6 %collective-permute-done.85 = bf16[512,1024]{1,0:T(8,128)(2,1)} collective-permute-done((bf16[512,1024]{1,0:T(8,128)(2,1)}, bf16[512,1024]{1,0:T(8,128)(2,1)}, u32[]{:S(2)}, u32[]{:S(2)}) %collective-permute-start.85) | collective-permute-done | bytes 1048608 | tf_op jit(solution)/shard_map/ppermute | solution.py:270
  (726 shorter events, 460.8 us)
Async XLA Ops:
  7.2 147.8 %all-gather.6.cloned.1.call-start = ((), (), s32[]{:S(2)}) async-start(), calls=%async_computation.11 | async-start | bytes 9437184 | tf_op jit(solution)/shard_map/all_gather | solution.py:835
  64.5 220.0 %all-gather.12.cloned.1.call-start = ((), (), s32[]{:S(2)}) async-start(), calls=%async_computation.20 | async-start | bytes 7864320 | tf_op jit(solution)/shard_map/all_gather | solution.py:867
  64.6 35.2 %collective-permute-start.18 = (bf16[512,1536]{1,0:T(8,128)(2,1)S(1)}, bf16[512,1536]{1,0:T(8,128)(2,1)}, u32[]{:S(2)}, u32[]{:S(2)}) collective-permute-start(bf16[512,1536]{1,0:T(8,128)(2,1)S(1)} %bitcast.253), channel_id=1, source_target_pairs={{0,8},{8,0},{16,24},{24,16},{1,9},{9,1},{17,25},{25,17},{2,10},{10... | collective-permute-start | bytes 4718600 | tf_op jit(solution)/shard_map/ppermute | solution.py:270
  66.4 36.3 %collective-permute-start.20 = (bf16[512,1536]{1,0:T(8,128)(2,1)S(1)}, bf16[512,1536]{1,0:T(8,128)(2,1)}, u32[]{:S(2)}, u32[]{:S(2)}) collective-permute-start(bf16[512,1536]{1,0:T(8,128)(2,1)S(1)} %bitcast.254), channel_id=1, source_target_pairs={{0,16},{8,24},{16,0},{24,8},{1,17},{9,25},{17,1},{25,9},{2,18},{10... | collective-permute-start | bytes 4718600 | tf_op jit(solution)/shard_map/ppermute | solution.py:270
  72.3 55.3 %collective-permute-start.17 = (bf16[512,640]{1,0:T(8,128)(2,1)}, bf16[512,640]{1,0:T(8,128)(2,1)S(1)}, u32[]{:S(2)}, u32[]{:S(2)}) collective-permute-start(bf16[512,640]{1,0:T(8,128)(2,1)} %slice.337), channel_id=1, source_target_pairs={{0,1},{1,0},{2,3},{3,2},{4,5},{5,4},{6,7},{7,6},{8,9},{9,8},{10,11... | collective-permute-start | bytes 1966088 | tf_op jit(solution)/shard_map/ppermute | solution.py:270
  160.9 32.6 %collective-permute-start.26 = (bf16[128,512]{1,0:T(8,128)(2,1)}, bf16[128,512]{1,0:T(8,128)(2,1)S(1)}, u32[]{:S(2)}, u32[]{:S(2)}) collective-permute-start(bf16[128,512]{1,0:T(8,128)(2,1)} %get-tuple-element.403), channel_id=1, source_target_pairs={{0,0},{1,2},{2,4},{3,6},{4,1},{5,3},{6,5},{7,7},{8,8},{9,10},{10,1... | collective-permute-start | bytes 393224 | tf_op jit(solution)/shard_map/ppermute | solution.py:875
  169.5 175.5 %reduce-scatter.9.cloned.1.call-start = ((), (), s32[]{:S(2)}) async-start(), calls=%async_computation.13 | async-start | bytes 4718592 | tf_op jit(solution)/shard_map/reduce_scatter | solution.py:944
  284.6 120.1 %reduce-scatter.7.cloned.1.call-start = ((), (), s32[]{:S(2)}) async-start(), calls=%async_computation.12 | async-start | bytes 4718592 | tf_op jit(solution)/shard_map/reduce_scatter | solution.py:944
  293.8 32.9 %collective-permute-start.33 = (bf16[128,2048]{1,0:T(8,128)(2,1)S(1)}, bf16[128,2048]{1,0:T(8,128)(2,1)S(1)}, u32[]{:S(2)}, u32[]{:S(2)}) collective-permute-start(bf16[128,2048]{1,0:T(8,128)(2,1)S(1)} %get-tuple-element.324), channel_id=1, source_target_pairs={{0,8},{8,0},{16,24},{24,16},{1,9},{9,1},{17,25},{25,17},{2,10},{10... | collective-permute-start | bytes 1572872 | tf_op jit(solution)/shard_map/ppermute | solution.py:270
  304.2 34.0 %collective-permute-start.34 = (bf16[128,2048]{1,0:T(8,128)(2,1)S(1)}, bf16[128,2048]{1,0:T(8,128)(2,1)S(1)}, u32[]{:S(2)}, u32[]{:S(2)}) collective-permute-start(bf16[128,2048]{1,0:T(8,128)(2,1)S(1)} %get-tuple-element.324), channel_id=1, source_target_pairs={{0,16},{8,24},{16,0},{24,8},{1,17},{9,25},{17,1},{25,9},{2,18},{10... | collective-permute-start | bytes 1572872 | tf_op jit(solution)/shard_map/ppermute | solution.py:270
  352.7 160.3 %all-gather.8.cloned.1.call-start = ((), (), s32[]{:S(2)}) async-start(), calls=%async_computation.14 | async-start | bytes 4718592 | tf_op jit(solution)/shard_map/all_gather | solution.py:957
  444.8 52.2 %collective-permute-start.66 = (bf16[512,2048]{1,0:T(8,128)(2,1)}, bf16[512,2048]{1,0:T(8,128)(2,1)}, u32[]{:S(2)}, u32[]{:S(2)}) collective-permute-start(bf16[512,2048]{1,0:T(8,128)(2,1)} %slice.362), channel_id=1, source_target_pairs={{0,1},{1,0},{2,3},{3,2},{4,5},{5,4},{6,7},{7,6},{8,9},{9,8},{10,11... | collective-permute-start | bytes 6291464 | tf_op jit(solution)/shard_map/ppermute | solution.py:270
  468.6 191.3 %all-gather.10.cloned.1.call-start = ((), (), s32[]{:S(2)}) async-start(), calls=%async_computation.15 | async-start | bytes 4718592 | tf_op jit(solution)/shard_map/all_gather | solution.py:1026
  544.4 153.8 %reduce-scatter.13.cloned.1.call-start = ((), (), s32[]{:S(2)}) async-start(), calls=%async_computation.17 | async-start | bytes 5242880 | tf_op jit(solution)/shard_map/reduce_scatter | solution.py:1088
  601.2 270.3 %reduce-scatter.17.cloned.1.call-start = ((), (), s32[]{:S(2)}) async-start(), calls=%async_computation.19 | async-start | bytes 2621440 | tf_op jit(solution)/shard_map/reduce_scatter | solution.py:1116
  604.0 37.2 %collective-permute-start.71 = (bf16[128,2048]{1,0:T(8,128)(2,1)}, bf16[128,2048]{1,0:T(8,128)(2,1)}, u32[]{:S(2)}, u32[]{:S(2)}) collective-permute-start(bf16[128,2048]{1,0:T(8,128)(2,1)} %get-tuple-element.344), channel_id=1, source_target_pairs={{0,8},{8,0},{16,24},{24,16},{1,9},{9,1},{17,25},{25,17},{2,10},{10... | collective-permute-start | bytes 1572872 | tf_op jit(solution)/shard_map/ppermute | solution.py:270
  605.2 43.7 %collective-permute-start.72 = (bf16[128,2048]{1,0:T(8,128)(2,1)}, bf16[128,2048]{1,0:T(8,128)(2,1)}, u32[]{:S(2)}, u32[]{:S(2)}) collective-permute-start(bf16[128,2048]{1,0:T(8,128)(2,1)} %get-tuple-element.346), channel_id=1, source_target_pairs={{0,16},{8,24},{16,0},{24,8},{1,17},{9,25},{17,1},{25,9},{2,18},{10... | collective-permute-start | bytes 1572872 | tf_op jit(solution)/shard_map/ppermute | solution.py:270
  605.9 43.0 %collective-permute-start.73 = (bf16[128,2048]{1,0:T(8,128)(2,1)}, bf16[128,2048]{1,0:T(8,128)(2,1)}, u32[]{:S(2)}, u32[]{:S(2)}) collective-permute-start(bf16[128,2048]{1,0:T(8,128)(2,1)} %get-tuple-element.345), channel_id=1, source_target_pairs={{0,24},{8,16},{16,8},{24,0},{1,25},{9,17},{17,9},{25,1},{2,26},{10... | collective-permute-start | bytes 1572872 | tf_op jit(solution)/shard_map/ppermute | solution.py:270
  610.1 38.8 %collective-permute-start.74 = (bf16[128,2048]{1,0:T(8,128)(2,1)}, bf16[128,2048]{1,0:T(8,128)(2,1)}, u32[]{:S(2)}, u32[]{:S(2)}) collective-permute-start(bf16[128,2048]{1,0:T(8,128)(2,1)} %get-tuple-element.347), channel_id=1, source_target_pairs={{0,8},{8,0},{16,24},{24,16},{1,9},{9,1},{17,25},{25,17},{2,10},{10... | collective-permute-start | bytes 1572872 | tf_op jit(solution)/shard_map/ppermute | solution.py:270
  611.2 37.7 %collective-permute-start.75 = (bf16[128,2048]{1,0:T(8,128)(2,1)}, bf16[128,2048]{1,0:T(8,128)(2,1)}, u32[]{:S(2)}, u32[]{:S(2)}) collective-permute-start(bf16[128,2048]{1,0:T(8,128)(2,1)} %get-tuple-element.349), channel_id=1, source_target_pairs={{0,16},{8,24},{16,0},{24,8},{1,17},{9,25},{17,1},{25,9},{2,18},{10... | collective-permute-start | bytes 1572872 | tf_op jit(solution)/shard_map/ppermute | solution.py:270
  659.9 237.6 %reduce-scatter.11.cloned.1.call-start = ((), (), s32[]{:S(2)}) async-start(), calls=%async_computation.16 | async-start | bytes 4718592 | tf_op jit(solution)/shard_map/reduce_scatter | solution.py:1110
  671.9 41.1 %collective-permute-start.77 = (bf16[512,512]{1,0:T(8,128)(2,1)}, bf16[512,512]{1,0:T(8,128)(2,1)}, u32[]{:S(2)}, u32[]{:S(2)}) collective-permute-start(bf16[512,512]{1,0:T(8,128)(2,1)} %get-tuple-element.341), channel_id=1, source_target_pairs={{0,8},{8,0},{16,24},{24,16},{1,9},{9,1},{17,25},{25,17},{2,10},{10... | collective-permute-start | bytes 1572872 | tf_op jit(solution)/shard_map/ppermute | solution.py:270
  673.1 39.9 %collective-permute-start.78 = (bf16[512,512]{1,0:T(8,128)(2,1)}, bf16[512,512]{1,0:T(8,128)(2,1)}, u32[]{:S(2)}, u32[]{:S(2)}) collective-permute-start(bf16[512,512]{1,0:T(8,128)(2,1)} %get-tuple-element.343), channel_id=1, source_target_pairs={{0,16},{8,24},{16,0},{24,8},{1,17},{9,25},{17,1},{25,9},{2,18},{10... | collective-permute-start | bytes 1572872 | tf_op jit(solution)/shard_map/ppermute | solution.py:270
  673.7 39.3 %collective-permute-start.79 = (bf16[512,512]{1,0:T(8,128)(2,1)}, bf16[512,512]{1,0:T(8,128)(2,1)}, u32[]{:S(2)}, u32[]{:S(2)}) collective-permute-start(bf16[512,512]{1,0:T(8,128)(2,1)} %get-tuple-element.342), channel_id=1, source_target_pairs={{0,24},{8,16},{16,8},{24,0},{1,25},{9,17},{17,9},{25,1},{2,26},{10... | collective-permute-start | bytes 1572872 | tf_op jit(solution)/shard_map/ppermute | solution.py:270
  717.3 41.3 %collective-permute-start.80 = (bf16[512,768]{1,0:T(8,128)(2,1)}, bf16[512,768]{1,0:T(8,128)(2,1)}, u32[]{:S(2)}, u32[]{:S(2)}) collective-permute-start(bf16[512,768]{1,0:T(8,128)(2,1)} %get-tuple-element.238), channel_id=1, source_target_pairs={{0,8},{8,0},{16,24},{24,16},{1,9},{9,1},{17,25},{25,17},{2,10},{10... | collective-permute-start | bytes 2359304 | tf_op jit(solution)/shard_map/ppermute | solution.py:270
  718.6 40.0 %collective-permute-start.81 = (bf16[512,768]{1,0:T(8,128)(2,1)}, bf16[512,768]{1,0:T(8,128)(2,1)}, u32[]{:S(2)}, u32[]{:S(2)}) collective-permute-start(bf16[512,768]{1,0:T(8,128)(2,1)} %get-tuple-element.239), channel_id=1, source_target_pairs={{0,16},{8,24},{16,0},{24,8},{1,17},{9,25},{17,1},{25,9},{2,18},{10... | collective-permute-start | bytes 2359304 | tf_op jit(solution)/shard_map/ppermute | solution.py:270
  720.1 38.6 %collective-permute-start.82 = (bf16[512,768]{1,0:T(8,128)(2,1)}, bf16[512,768]{1,0:T(8,128)(2,1)}, u32[]{:S(2)}, u32[]{:S(2)}) collective-permute-start(bf16[512,768]{1,0:T(8,128)(2,1)} %get-tuple-element.240), channel_id=1, source_target_pairs={{0,24},{8,16},{16,8},{24,0},{1,25},{9,17},{17,9},{25,1},{2,26},{10... | collective-permute-start | bytes 2359304 | tf_op jit(solution)/shard_map/ppermute | solution.py:270
  720.8 44.2 %all-to-all-start.1 = ((bf16[8,128,512]{2,1,0:T(8,128)(2,1)}), bf16[8,128,512]{2,1,0:T(8,128)(2,1)}, u32[]{:S(2)}, u32[]{:S(2)}) async-start(bf16[8,128,512]{2,1,0:T(8,128)(2,1)} %maximum_dynamic-update-slice_fusion), calls=%async_computation.5 | async-start | bytes 2097152 | tf_op jit(solution)/shard_map/all_to_all | solution.py:1060
  725.1 172.4 %reduce-scatter.15.cloned.1.call-start = ((), (), s32[]{:S(2)}) async-start(), calls=%async_computation.18 | async-start | bytes 4718592 | tf_op jit(solution)/shard_map/reduce_scatter | solution.py:1110
  799.8 49.1 %collective-permute-start.85 = (bf16[512,1024]{1,0:T(8,128)(2,1)}, bf16[512,1024]{1,0:T(8,128)(2,1)}, u32[]{:S(2)}, u32[]{:S(2)}) collective-permute-start(bf16[512,1024]{1,0:T(8,128)(2,1)} %get-tuple-element.251), channel_id=1, source_target_pairs={{0,24},{8,16},{16,8},{24,0},{1,25},{9,17},{17,9},{25,1},{2,26},{10... | collective-permute-start | bytes 3145736 | tf_op jit(solution)/shard_map/ppermute | solution.py:270
  805.8 46.9 %all-to-all-start.3 = ((bf16[8,64,768]{2,1,0:T(8,128)(2,1)}), bf16[8,64,768]{2,1,0:T(8,128)(2,1)}, u32[]{:S(2)}, u32[]{:S(2)}) async-start(bf16[8,64,768]{2,1,0:T(8,128)(2,1)} %bitcast.100), calls=%async_computation.8 | async-start | bytes 1572864 | tf_op jit(solution)/shard_map/all_to_all | solution.py:987
  855.1 32.9 %all-to-all-start.4 = ((bf16[8,64,1024]{2,1,0:T(8,128)(2,1)}), bf16[8,64,1024]{2,1,0:T(8,128)(2,1)}, u32[]{:S(2)}, u32[]{:S(2)}) async-start(bf16[8,64,1024]{2,1,0:T(8,128)(2,1)} %bitcast.102), calls=%async_computation.9 | async-start | bytes 2097152 | tf_op jit(solution)/shard_map/all_to_all | solution.py:987
  (212 other events, 3209.2 us)
Sparse Core Ops, SparseCore 0:
  64.6 90.3 all-gather.5
  169.6 114.8 all-gather.11
  286.8 48.2 reduce-scatter.8
  352.8 47.2 reduce-scatter.6
  468.7 44.3 all-gather.7
  544.5 44.9 all-gather.9
  601.3 74.3 reduce-scatter.12
  678.2 44.3 reduce-scatter.16
  724.9 61.8 reduce-scatter.10
  791.1 64.3 reduce-scatter.14

commit v4 on v3

--- a/solution.py
+++ b/solution.py
@@ -266,12 +266,24 @@
     return assemble(scalars, blocks, [shape], plan, 2 * peers * parts, "join_out")[0]
 
 
+def join_blocks(blocks):
+    rows, width = blocks[0].shape
+
+    def plan(scalar_ref, sources, outs, sems):
+        run_copies(
+            [(source, outs[0].at[pl.ds(i * rows, rows)]) for i, source in enumerate(sources)], sems
+        )
+
+    count = len(blocks)
+    return assemble([0], blocks, [(count * rows, width)], plan, count, "join_blocks")[0]
+
+
 def swap(block, axis, distance):
     return lax.ppermute(block, axis, [(i, i ^ distance) for i in range(lax.axis_size(axis))])
 
 
 def gather_core(near):
-    return jnp.concatenate(near + [swap(piece, "c", 1) for piece in near], axis=0)
+    return join_blocks(near + [swap(piece, "c", 1) for piece in near])
 
 
 def gather_plane(block):
@@ -948,10 +960,14 @@
 
     units = w_dn.shape[0]
     hidden, norm2, act, ffn, grad_gu, grad_hidden, grad_mix = [], [], [], [], [], [], []
+    def enter_ffn(s):
+        hidden.append(tokens[s].astype(f32) + valid[s] * mix[s].astype(f32))
+        norm2_f, pull = jax.vjp(lambda h: rms_norm(h, gain_all[1]), hidden[s])
+        return norm2_f.astype(bf16), pull
+
+    block, pull = enter_ffn(0)
     for s in range(seqs):
-        hidden.append(tokens[s].astype(f32) + valid[s] * mix[s].astype(f32))
-        norm2_f, norm2_pull = jax.vjp(lambda h: rms_norm(h, gain_all[1]), hidden[s])
-        near = from_dp(norm2_f.astype(bf16))
+        near = from_dp(block)
         if s > 0:
             near, local = lax.optimization_barrier((near, local))
             grad_mix.append(lax.all_gather(local, TEAM, axis=0, tiled=True))
@@ -965,14 +981,18 @@
         grad_upper = grad_act * gate * sig_gate
         grad_gu.append(jnp.concatenate([grad_gate, grad_upper], 1).astype(bf16))
         partial = dot_last(grad_gu[s], w_gu).astype(bf16)
+        ffn.append(dot(act[s], w_dn).astype(bf16))
+        near = scatter_core(partial)
         if s < seqs - 1:
             mix[s + 1] = after(mix[s + 1], partial)
-        ffn.append(dot(act[s], w_dn).astype(bf16))
-        near = scatter_core(partial)
-        if s == seqs - 1:
+            block, next_pull = enter_ffn(s + 1)
+            block, near = lax.optimization_barrier((block, near))
+        else:
             ffn = [scatter_core(part_ffn) for part_ffn in ffn]
             grad_mix[0], near, ffn = lax.optimization_barrier((grad_mix[0], near, ffn))
-        (grad_hidden_norm,) = norm2_pull(scatter_near(near))
+        (grad_hidden_norm,) = pull(scatter_near(near))
+        if s < seqs - 1:
+            pull = next_pull
         grad_hidden.append(cot[s] + grad_hidden_norm)
         local = (valid[s] * grad_hidden[s]).astype(bf16)
 

time: 919 us -> 910 us (level)
  local copies, waits for them, and re-layouts: 123 us -> 97.9 us
  Pallas kernels: 127 us -> 138 us
    unnamed x327 -> x350, local copies, waits for them, and re-layouts: 59 us -> 38.5 us
    pallas_call x4 -> x8, Pallas kernels: 17 us -> 28.7 us  [assemble(): pl.pallas_call(kernel, in_specs=[pl.BlockSpec(memory_space=pltpu.SMEM)] +...]
  transfers between devices with their start and end apart: 101 -> 101, of which waited for: 34 -> 33; matrix products, arithmetic and copies ran while one was open for 36% -> 34% of each run, Pallas kernels for 14% -> 15%
where the time goes in v4:
time: 910 us; the launch traced here: 901 us
  waiting for transfers between devices  287 us (32%)
  matrix products  169 us (19%)
  Pallas kernels  138 us (15%)
  starting transfers between devices  111 us (12%)
  local copies, waits for them, and re-layouts  97.9 us (11%)
  other arithmetic  80.2 us (9%)
  between operations  17.2 us (2%)
    ppermute x68, waiting for transfers between devices, swap(): lax.ppermute(block, axis, [(i, i ^ distance) for i in range(lax.axis_size...  197 us
    ppermute x68, starting transfers between devices, swap(): lax.ppermute(block, axis, [(i, i ^ distance) for i in range(lax.axis_size...  65.1 us
    pallas_call x2, Pallas kernels, core_back(): pl.pallas_call(functools.partial(core_back_kernel, heads=heads, span=span...  61.5 us
    dot_general x10, matrix products, dot_last(): lax.dot_general(left, right, (((1,), (1,)), ((), ())), preferred_element_...  58.5 us
    dot_general x8, matrix products, dot_first(): lax.dot_general(left, right, (((0,), (0,)), ((), ())), preferred_element_...  55.8 us
    dot_general x8, matrix products, dot(): return jnp.dot(left, right, preferred_element_type=f32, precision=precision)  54.9 us
    unnamed x350, local copies, waits for them, and re-layouts  38.5 us
    all_gather x1, waiting for transfers between devices, body(): lax.all_gather(w_ffn, LINE, axis=0, tiled=False).reshape(line, -1, columns)  30.3 us
  transfers between devices with their start and end apart: 101, of which 33 were waited for; matrix products, arithmetic and copies ran while one was open for 34% of the time, Pallas kernels for 15%

profile of v4, /device:TPU:0, one launch (start us, length us, event | category | flops | bytes accessed | tf_op | source)
XLA Modules:
  0.0 901.0 jit_solution(7145726643879426846)
XLA Ops:
  42.9 18.2 %collective-permute-done.3.refs_4_ = bf16[64,1536]{1,0:T(8,128)(2,1)S(1)} collective-permute-done((bf16[64,1536]{1,0:T(8,128)(2,1)}, bf16[64,1536]{1,0:T(8,128)(2,1)S(1)}, u32[]{:S(2)}, u32[]{:S(2)}) %collective-permute-start.3) | collective-permute-done | bytes 196640 | tf_op jit(solution)/shard_map/ppermute | solution.py:815
  76.5 22.3 %collective-permute-done.18.refs_1_ = bf16[512,1536]{1,0:T(8,128)(2,1)} collective-permute-done((bf16[512,1536]{1,0:T(8,128)(2,1)S(1)}, bf16[512,1536]{1,0:T(8,128)(2,1)}, u32[]{:S(2)}, u32[]{:S(2)}) %collective-permute-start.18) | collective-permute-done | bytes 1572896 | tf_op jit(solution)/shard_map/ppermute | solution.py:282
  135.6 18.9 %all-gather.6.cloned.1.call-done = bf16[2,1024,2048]{2,1,0:T(8,128)(2,1)} async-done(((bf16[2,128,2048]{2,1,0:T(8,128)(2,1)}), bf16[2,1024,2048]{2,1,0:T(8,128)(2,1)}) %all-gather.6.cloned.1.call-update) | async-done | bytes 8388624 | tf_op jit(solution)/shard_map/all_gather | solution.py:847
  169.3 14.7 %fusion.82.x_ref.bc_ref.dt_ref = f32[2048,1024]{1,0:T(8,128)} fusion(bf16[2048,1024]{1,0:T(8,128)(2,1)} %get-tuple-element.172, bf16[2048,2048]{1,0:T(8,128)(2,1)} %bitcast.278, f32[2048]{0:T(1024)S(1)} %get-tuple-element.312, f32[2048]{0:T(1024)S(1)} %add_rsqrt_fusion), kind=kOutput, calls=%fused_computation.274 | convolution fusion | flops 8606711808 | bytes 20987904 | tf_op jit(solution)/shard_map/dot_general | solution.py:63
  184.0 9.2 %fusion.84.z_ref = f32[2048,768]{1,0:T(8,128)S(1)} fusion(bf16[2048,768]{1,0:T(8,128)(2,1)S(1)} %copy-done.152, bf16[2048,2048]{1,0:T(8,128)(2,1)} %bitcast.279, f32[2048]{0:T(1024)S(1)} %get-tuple-element.312, f32[2048]{0:T(1024)S(1)} %add_rsqrt_fusion), kind=kOutput, calls=%fused_computation.275 | convolution fusion | flops 6459228160 | bytes 17842176 | tf_op jit(solution)/shard_map/dot_general | solution.py:63
  200.8 14.4 %core_fore.2 = (bf16[1024,384]{1,0:T(8,128)(2,1)S(1)}, f32[1024,384]{1,0:T(8,128)S(1)}, f32[1,4,384,256]{3,2,1,0:T(8,128)S(1)}, f32[1,384,256]{2,1,0:T(8,128)}, f32[1,8,128]{2,1,0:T(8,128)}) custom-call(s32[1]{0:T(128)} %bitcast.2.turn_ref, f32[2048,1024]{1,0:T(8,128)} %fusion.82.x_ref.bc_ref.dt_ref, f32[2048,1024]{1,0:T(8,128)} %fusion.82.x_ref.bc_ref.dt_ref, ...), custom_call_target="tpu_custom_call" | custom-call | flops 12999999488 | bytes 8781824 | tf_op jit(solution)/shard_map/core_fore/pallas_call | solution.py:531
  232.2 14.1 %core_fore.3 = (bf16[1024,384]{1,0:T(8,128)(2,1)S(1)}, f32[1024,384]{1,0:T(8,128)S(1)}, f32[1,4,384,256]{3,2,1,0:T(8,128)S(1)}, f32[1,384,256]{2,1,0:T(8,128)}, f32[1,8,128]{2,1,0:T(8,128)}) custom-call(s32[1]{0:T(128)} %bitcast.2.turn_ref, f32[2048,1024]{1,0:T(8,128)} %fusion.82.x_ref.bc_ref.dt_ref, f32[2048,1024]{1,0:T(8,128)} %fusion.82.x_ref.bc_ref.dt_ref, ...), custom_call_target="tpu_custom_call" | custom-call | flops 12999999488 | bytes 8781824 | tf_op jit(solution)/shard_map/core_fore/pallas_call | solution.py:531
  253.9 30.3 %all-gather.12.cloned.1.call-done = bf16[3072,1024]{1,0:T(8,128)(2,1)} async-done(((bf16[768,1024]{1,0:T(8,128)(2,1)}), bf16[3072,1024]{1,0:T(8,128)(2,1)}) %all-gather.12.cloned.1.call-update) | async-done | bytes 6291472 | tf_op jit(solution)/shard_map/all_gather | solution.py:879
  296.7 9.7 %collective-permute-done.40.refs_1_ = bf16[128,2048]{1,0:T(8,128)(2,1)S(1)} collective-permute-done((bf16[128,2048]{1,0:T(8,128)(2,1)S(1)}, bf16[128,2048]{1,0:T(8,128)(2,1)S(1)}, u32[]{:S(2)}, u32[]{:S(2)}) %collective-permute-start.40) | collective-permute-done | bytes 524320 | tf_op jit(solution)/shard_map/ppermute | solution.py:282
  307.8 9.8 %collective-permute-done.41.refs_2_ = bf16[128,2048]{1,0:T(8,128)(2,1)S(1)} collective-permute-done((bf16[128,2048]{1,0:T(8,128)(2,1)S(1)}, bf16[128,2048]{1,0:T(8,128)(2,1)S(1)}, u32[]{:S(2)}, u32[]{:S(2)}) %collective-permute-start.41) | collective-permute-done | bytes 524320 | tf_op jit(solution)/shard_map/ppermute | solution.py:282
  319.2 9.7 %collective-permute-done.33.refs_1_ = bf16[128,2048]{1,0:T(8,128)(2,1)S(1)} collective-permute-done((bf16[128,2048]{1,0:T(8,128)(2,1)S(1)}, bf16[128,2048]{1,0:T(8,128)(2,1)S(1)}, u32[]{:S(2)}, u32[]{:S(2)}) %collective-permute-start.33) | collective-permute-done | bytes 524320 | tf_op jit(solution)/shard_map/ppermute | solution.py:282
  328.9 11.3 %collective-permute-done.34.refs_2_ = bf16[128,2048]{1,0:T(8,128)(2,1)S(1)} collective-permute-done((bf16[128,2048]{1,0:T(8,128)(2,1)S(1)}, bf16[128,2048]{1,0:T(8,128)(2,1)S(1)}, u32[]{:S(2)}, u32[]{:S(2)}) %collective-permute-start.34) | collective-permute-done | bytes 524320 | tf_op jit(solution)/shard_map/ppermute | solution.py:282
  354.2 11.3 %collective-permute-done.47.refs_1_ = bf16[128,2048]{1,0:T(8,128)(2,1)S(1)} collective-permute-done((bf16[128,2048]{1,0:T(8,128)(2,1)S(1)}, bf16[128,2048]{1,0:T(8,128)(2,1)S(1)}, u32[]{:S(2)}, u32[]{:S(2)}) %collective-permute-start.47) | collective-permute-done | bytes 524320 | tf_op jit(solution)/shard_map/ppermute | solution.py:282
  366.0 11.1 %collective-permute-done.49.refs_3_ = bf16[128,2048]{1,0:T(8,128)(2,1)} collective-permute-done((bf16[128,2048]{1,0:T(8,128)(2,1)S(1)}, bf16[128,2048]{1,0:T(8,128)(2,1)}, u32[]{:S(2)}, u32[]{:S(2)}) %collective-permute-start.49) | collective-permute-done | bytes 524320 | tf_op jit(solution)/shard_map/ppermute | solution.py:282
  387.4 7.8 fusion.99
  422.0 8.6 collective-permute-done.58
  432.7 10.2 %collective-permute-done.59 = bf16[128,2048]{1,0:T(8,128)(2,1)S(1)} collective-permute-done((bf16[128,2048]{1,0:T(8,128)(2,1)S(1)}, bf16[128,2048]{1,0:T(8,128)(2,1)S(1)}, u32[]{:S(2)}, u32[]{:S(2)}) %collective-permute-start.59) | collective-permute-done | bytes 524320 | tf_op jit(solution)/shard_map/ppermute | solution.py:282
  453.1 11.2 %collective-permute-done.56.refs_2_ = bf16[128,2048]{1,0:T(8,128)(2,1)S(1)} collective-permute-done((bf16[128,2048]{1,0:T(8,128)(2,1)S(1)}, bf16[128,2048]{1,0:T(8,128)(2,1)S(1)}, u32[]{:S(2)}, u32[]{:S(2)}) %collective-permute-start.56) | collective-permute-done | bytes 524320 | tf_op jit(solution)/shard_map/ppermute | solution.py:282
  475.9 7.8 fusion.100
  489.9 7.6 convolution_convert_fusion.4
  526.9 11.7 %collective-permute-done.69 = bf16[128,2048]{1,0:T(8,128)(2,1)S(1)} collective-permute-done((bf16[128,2048]{1,0:T(8,128)(2,1)S(1)}, bf16[128,2048]{1,0:T(8,128)(2,1)S(1)}, u32[]{:S(2)}, u32[]{:S(2)}) %collective-permute-start.69) | collective-permute-done | bytes 524320 | tf_op jit(solution)/shard_map/ppermute | solution.py:282
  545.9 31.0 %core_back.2 = (bf16[1024,1024]{1,0:T(8,128)(2,1)S(1)}, f32[8,896]{1,0:T(8,128)S(1)}, f32[8,128]{1,0:T(8,128)S(1)}, f32[1,384,256]{2,1,0:T(8,128)}, f32[1,8,896]{2,1,0:T(8,128)}) custom-call(s32[1]{0:T(128)} %bitcast.2.turn_ref, f32[2048,1024]{1,0:T(8,128)} %fusion.82.x_ref.bc_ref.dt_ref, f32[2048,1024]{1,0:T(8,128)} %fusion.82.x_ref.bc_ref.dt_ref, ...), custom_call_target="tpu_custom_call" | custom-call | flops 30000001024 | bytes 9961472 | tf_op jit(solution)/shard_map/core_back/pallas_call | solution.py:702
  577.0 7.8 fusion.40
  584.8 8.5 add_convert_fusion.3
  622.2 8.4 add_convert_fusion.2
  681.5 9.4 %convolution_convert_fusion.6 = bf16[2048,768]{1,0:T(8,128)(2,1)} fusion(bf16[1024,128]{1,0:T(8,128)(2,1)S(1)} %convert_bitcast_fusion.4, bf16[1024,128]{1,0:T(8,128)(2,1)S(1)} %get-tuple-element.383, bf16[1024,128]{1,0:T(8,128)(2,1)S(1)} %get-tuple-element.382, bf16[1024,384]{1,0:T(8,128)(2,1)S(1)} %copy-done.90, bf16[1024,128]{1,0:T(8,128)(2,1)S(1)} %copy-done.100, ...), kind=kOutput, calls=%fused_computation.25 | convolution fusion | flops 6485966848 | bytes 14696448 | tf_op jit(solution)/shard_map/dot_general | solution.py:67
  695.0 7.7 fusion.32
  718.1 30.5 %core_back.3 = (bf16[1024,1024]{1,0:T(8,128)(2,1)S(1)}, f32[8,896]{1,0:T(8,128)S(1)}, f32[8,128]{1,0:T(8,128)S(1)}, f32[1,384,256]{2,1,0:T(8,128)}, f32[1,8,896]{2,1,0:T(8,128)}) custom-call(s32[1]{0:T(128)} %bitcast.2.turn_ref, f32[2048,1024]{1,0:T(8,128)} %fusion.82.x_ref.bc_ref.dt_ref, f32[2048,1024]{1,0:T(8,128)} %fusion.82.x_ref.bc_ref.dt_ref, ...), custom_call_target="tpu_custom_call" | custom-call | flops 30000001024 | bytes 9961472 | tf_op jit(solution)/shard_map/core_back/pallas_call | solution.py:702
  757.0 13.8 %add_convert_fusion.1 = bf16[2048,1024]{1,0:T(8,128)(2,1)S(1)} fusion(f32[2048,11]{1,0:T(8,128)} %reshape.328, bf16[1024,1024]{1,0:T(8,128)(2,1)} %copy-done.45, bf16[1024,1024]{1,0:T(8,128)(2,1)S(1)} %copy-done.44, bf16[2048,2048]{1,0:T(8,128)(2,1)} %bitcast.280, f32[2048]{0:T(1024)S(1)} %copy-done.127, f32[2048]{0:T(1024)S(1)} %copy-done.134), kind=kOutput, calls=%fused_computation.6 | convolution fusion | flops 8619294720 | bytes 16883712 | tf_op jit(solution)/shard_map/dot_general | solution.py:67
  774.9 8.4 add_convert_fusion
  802.8 17.9 %collective-permute-done.83 = bf16[512,1024]{1,0:T(8,128)(2,1)} collective-permute-done((bf16[512,1024]{1,0:T(8,128)(2,1)}, bf16[512,1024]{1,0:T(8,128)(2,1)}, u32[]{:S(2)}, u32[]{:S(2)}) %collective-permute-start.83) | collective-permute-done | bytes 1048608 | tf_op jit(solution)/shard_map/ppermute | solution.py:282
  820.7 21.5 %collective-permute-done.85 = bf16[512,1024]{1,0:T(8,128)(2,1)} collective-permute-done((bf16[512,1024]{1,0:T(8,128)(2,1)}, bf16[512,1024]{1,0:T(8,128)(2,1)}, u32[]{:S(2)}, u32[]{:S(2)}) %collective-permute-start.85) | collective-permute-done | bytes 1048608 | tf_op jit(solution)/shard_map/ppermute | solution.py:282
  (753 shorter events, 449.0 us)
Async XLA Ops:
  7.2 147.3 %all-gather.6.cloned.1.call-start = ((), (), s32[]{:S(2)}) async-start(), calls=%async_computation.11 | async-start | bytes 9437184 | tf_op jit(solution)/shard_map/all_gather | solution.py:847
  64.0 220.2 %all-gather.12.cloned.1.call-start = ((), (), s32[]{:S(2)}) async-start(), calls=%async_computation.20 | async-start | bytes 7864320 | tf_op jit(solution)/shard_map/all_gather | solution.py:879
  64.1 34.7 %collective-permute-start.18 = (bf16[512,1536]{1,0:T(8,128)(2,1)S(1)}, bf16[512,1536]{1,0:T(8,128)(2,1)}, u32[]{:S(2)}, u32[]{:S(2)}) collective-permute-start(bf16[512,1536]{1,0:T(8,128)(2,1)S(1)} %bitcast.252), channel_id=1, source_target_pairs={{0,8},{8,0},{16,24},{24,16},{1,9},{9,1},{17,25},{25,17},{2,10},{10... | collective-permute-start | bytes 4718600 | tf_op jit(solution)/shard_map/ppermute | solution.py:282
  65.7 36.1 %collective-permute-start.20 = (bf16[512,1536]{1,0:T(8,128)(2,1)S(1)}, bf16[512,1536]{1,0:T(8,128)(2,1)}, u32[]{:S(2)}, u32[]{:S(2)}) collective-permute-start(bf16[512,1536]{1,0:T(8,128)(2,1)S(1)} %bitcast.253), channel_id=1, source_target_pairs={{0,16},{8,24},{16,0},{24,8},{1,17},{9,25},{17,1},{25,9},{2,18},{10... | collective-permute-start | bytes 4718600 | tf_op jit(solution)/shard_map/ppermute | solution.py:282
  71.7 54.3 %collective-permute-start.17 = (bf16[512,640]{1,0:T(8,128)(2,1)}, bf16[512,640]{1,0:T(8,128)(2,1)S(1)}, u32[]{:S(2)}, u32[]{:S(2)}) collective-permute-start(bf16[512,640]{1,0:T(8,128)(2,1)} %slice.337), channel_id=1, source_target_pairs={{0,1},{1,0},{2,3},{3,2},{4,5},{5,4},{6,7},{7,6},{8,9},{9,8},{10,11... | collective-permute-start | bytes 1966088 | tf_op jit(solution)/shard_map/ppermute | solution.py:282
  169.2 178.3 %reduce-scatter.9.cloned.1.call-start = ((), (), s32[]{:S(2)}) async-start(), calls=%async_computation.13 | async-start | bytes 4718592 | tf_op jit(solution)/shard_map/reduce_scatter | solution.py:956
  284.3 124.2 %reduce-scatter.7.cloned.1.call-start = ((), (), s32[]{:S(2)}) async-start(), calls=%async_computation.12 | async-start | bytes 4718592 | tf_op jit(solution)/shard_map/reduce_scatter | solution.py:956
  289.9 220.7 %all-gather.8.cloned.1.call-start = ((), (), s32[]{:S(2)}) async-start(), calls=%async_computation.14 | async-start | bytes 4718592 | tf_op jit(solution)/shard_map/all_gather | solution.py:973
  295.2 33.7 %collective-permute-start.33 = (bf16[128,2048]{1,0:T(8,128)(2,1)S(1)}, bf16[128,2048]{1,0:T(8,128)(2,1)S(1)}, u32[]{:S(2)}, u32[]{:S(2)}) collective-permute-start(bf16[128,2048]{1,0:T(8,128)(2,1)S(1)} %multiply_convert_fusion.13.refs_0_), channel_id=1, source_target_pairs={{0,8},{8,0},{16,24},{24,16},{1,9},{9,1},{17,25},{25,17},{2,10},{10... | collective-permute-start | bytes 1572872 | tf_op jit(solution)/shard_map/ppermute | solution.py:282
  306.4 33.9 %collective-permute-start.34 = (bf16[128,2048]{1,0:T(8,128)(2,1)S(1)}, bf16[128,2048]{1,0:T(8,128)(2,1)S(1)}, u32[]{:S(2)}, u32[]{:S(2)}) collective-permute-start(bf16[128,2048]{1,0:T(8,128)(2,1)S(1)} %multiply_convert_fusion.13.refs_0_), channel_id=1, source_target_pairs={{0,16},{8,24},{16,0},{24,8},{1,17},{9,25},{17,1},{25,9},{2,18},{10... | collective-permute-start | bytes 1572872 | tf_op jit(solution)/shard_map/ppermute | solution.py:282
  419.4 33.8 %collective-permute-start.55 = (bf16[128,2048]{1,0:T(8,128)(2,1)S(1)}, bf16[128,2048]{1,0:T(8,128)(2,1)S(1)}, u32[]{:S(2)}, u32[]{:S(2)}) collective-permute-start(bf16[128,2048]{1,0:T(8,128)(2,1)S(1)} %multiply_convert_fusion.10.refs_0_), channel_id=1, source_target_pairs={{0,8},{8,0},{16,24},{24,16},{1,9},{9,1},{17,25},{25,17},{2,10},{10... | collective-permute-start | bytes 1572872 | tf_op jit(solution)/shard_map/ppermute | solution.py:282
  420.4 43.9 %collective-permute-start.56 = (bf16[128,2048]{1,0:T(8,128)(2,1)S(1)}, bf16[128,2048]{1,0:T(8,128)(2,1)S(1)}, u32[]{:S(2)}, u32[]{:S(2)}) collective-permute-start(bf16[128,2048]{1,0:T(8,128)(2,1)S(1)} %multiply_convert_fusion.10.refs_0_), channel_id=1, source_target_pairs={{0,16},{8,24},{16,0},{24,8},{1,17},{9,25},{17,1},{25,9},{2,18},{10... | collective-permute-start | bytes 1572872 | tf_op jit(solution)/shard_map/ppermute | solution.py:282
  430.6 33.7 %collective-permute-start.57 = (bf16[128,2048]{1,0:T(8,128)(2,1)S(1)}, bf16[128,2048]{1,0:T(8,128)(2,1)S(1)}, u32[]{:S(2)}, u32[]{:S(2)}) collective-permute-start(bf16[128,2048]{1,0:T(8,128)(2,1)S(1)} %multiply_convert_fusion.10.refs_0_), channel_id=1, source_target_pairs={{0,24},{8,16},{16,8},{24,0},{1,25},{9,17},{17,9},{25,1},{2,26},{10... | collective-permute-start | bytes 1572872 | tf_op jit(solution)/shard_map/ppermute | solution.py:282
  465.9 187.8 %all-gather.10.cloned.1.call-start = ((), (), s32[]{:S(2)}) async-start(), calls=%async_computation.15 | async-start | bytes 4718592 | tf_op jit(solution)/shard_map/all_gather | solution.py:1046
  542.0 149.1 %reduce-scatter.13.cloned.1.call-start = ((), (), s32[]{:S(2)}) async-start(), calls=%async_computation.17 | async-start | bytes 5242880 | tf_op jit(solution)/shard_map/reduce_scatter | solution.py:1108
  595.9 267.7 %reduce-scatter.17.cloned.1.call-start = ((), (), s32[]{:S(2)}) async-start(), calls=%async_computation.19 | async-start | bytes 2621440 | tf_op jit(solution)/shard_map/reduce_scatter | solution.py:1136
  598.7 36.9 %collective-permute-start.71 = (bf16[128,2048]{1,0:T(8,128)(2,1)}, bf16[128,2048]{1,0:T(8,128)(2,1)}, u32[]{:S(2)}, u32[]{:S(2)}) collective-permute-start(bf16[128,2048]{1,0:T(8,128)(2,1)} %get-tuple-element.340), channel_id=1, source_target_pairs={{0,8},{8,0},{16,24},{24,16},{1,9},{9,1},{17,25},{25,17},{2,10},{10... | collective-permute-start | bytes 1572872 | tf_op jit(solution)/shard_map/ppermute | solution.py:282
  600.0 41.0 %collective-permute-start.72 = (bf16[128,2048]{1,0:T(8,128)(2,1)}, bf16[128,2048]{1,0:T(8,128)(2,1)}, u32[]{:S(2)}, u32[]{:S(2)}) collective-permute-start(bf16[128,2048]{1,0:T(8,128)(2,1)} %get-tuple-element.342), channel_id=1, source_target_pairs={{0,16},{8,24},{16,0},{24,8},{1,17},{9,25},{17,1},{25,9},{2,18},{10... | collective-permute-start | bytes 1572872 | tf_op jit(solution)/shard_map/ppermute | solution.py:282
  600.8 40.2 %collective-permute-start.73 = (bf16[128,2048]{1,0:T(8,128)(2,1)}, bf16[128,2048]{1,0:T(8,128)(2,1)}, u32[]{:S(2)}, u32[]{:S(2)}) collective-permute-start(bf16[128,2048]{1,0:T(8,128)(2,1)} %get-tuple-element.341), channel_id=1, source_target_pairs={{0,24},{8,16},{16,8},{24,0},{1,25},{9,17},{17,9},{25,1},{2,26},{10... | collective-permute-start | bytes 1572872 | tf_op jit(solution)/shard_map/ppermute | solution.py:282
  603.5 37.4 %collective-permute-start.74 = (bf16[128,2048]{1,0:T(8,128)(2,1)}, bf16[128,2048]{1,0:T(8,128)(2,1)}, u32[]{:S(2)}, u32[]{:S(2)}) collective-permute-start(bf16[128,2048]{1,0:T(8,128)(2,1)} %get-tuple-element.343), channel_id=1, source_target_pairs={{0,8},{8,0},{16,24},{24,16},{1,9},{9,1},{17,25},{25,17},{2,10},{10... | collective-permute-start | bytes 1572872 | tf_op jit(solution)/shard_map/ppermute | solution.py:282
  604.7 36.3 %collective-permute-start.75 = (bf16[128,2048]{1,0:T(8,128)(2,1)}, bf16[128,2048]{1,0:T(8,128)(2,1)}, u32[]{:S(2)}, u32[]{:S(2)}) collective-permute-start(bf16[128,2048]{1,0:T(8,128)(2,1)} %get-tuple-element.345), channel_id=1, source_target_pairs={{0,16},{8,24},{16,0},{24,8},{1,17},{9,25},{17,1},{25,9},{2,18},{10... | collective-permute-start | bytes 1572872 | tf_op jit(solution)/shard_map/ppermute | solution.py:282
  653.8 235.6 %reduce-scatter.11.cloned.1.call-start = ((), (), s32[]{:S(2)}) async-start(), calls=%async_computation.16 | async-start | bytes 4718592 | tf_op jit(solution)/shard_map/reduce_scatter | solution.py:1130
  665.9 38.5 %collective-permute-start.77 = (bf16[512,512]{1,0:T(8,128)(2,1)}, bf16[512,512]{1,0:T(8,128)(2,1)}, u32[]{:S(2)}, u32[]{:S(2)}) collective-permute-start(bf16[512,512]{1,0:T(8,128)(2,1)} %get-tuple-element.337), channel_id=1, source_target_pairs={{0,8},{8,0},{16,24},{24,16},{1,9},{9,1},{17,25},{25,17},{2,10},{10... | collective-permute-start | bytes 1572872 | tf_op jit(solution)/shard_map/ppermute | solution.py:282
  667.4 37.0 %collective-permute-start.78 = (bf16[512,512]{1,0:T(8,128)(2,1)}, bf16[512,512]{1,0:T(8,128)(2,1)}, u32[]{:S(2)}, u32[]{:S(2)}) collective-permute-start(bf16[512,512]{1,0:T(8,128)(2,1)} %get-tuple-element.339), channel_id=1, source_target_pairs={{0,16},{8,24},{16,0},{24,8},{1,17},{9,25},{17,1},{25,9},{2,18},{10... | collective-permute-start | bytes 1572872 | tf_op jit(solution)/shard_map/ppermute | solution.py:282
  668.2 36.2 %collective-permute-start.79 = (bf16[512,512]{1,0:T(8,128)(2,1)}, bf16[512,512]{1,0:T(8,128)(2,1)}, u32[]{:S(2)}, u32[]{:S(2)}) collective-permute-start(bf16[512,512]{1,0:T(8,128)(2,1)} %get-tuple-element.338), channel_id=1, source_target_pairs={{0,24},{8,16},{16,8},{24,0},{1,25},{9,17},{17,9},{25,1},{2,26},{10... | collective-permute-start | bytes 1572872 | tf_op jit(solution)/shard_map/ppermute | solution.py:282
  710.3 42.4 %collective-permute-start.80 = (bf16[512,768]{1,0:T(8,128)(2,1)}, bf16[512,768]{1,0:T(8,128)(2,1)}, u32[]{:S(2)}, u32[]{:S(2)}) collective-permute-start(bf16[512,768]{1,0:T(8,128)(2,1)} %get-tuple-element.242), channel_id=1, source_target_pairs={{0,8},{8,0},{16,24},{24,16},{1,9},{9,1},{17,25},{25,17},{2,10},{10... | collective-permute-start | bytes 2359304 | tf_op jit(solution)/shard_map/ppermute | solution.py:282
  710.8 41.9 %collective-permute-start.81 = (bf16[512,768]{1,0:T(8,128)(2,1)}, bf16[512,768]{1,0:T(8,128)(2,1)}, u32[]{:S(2)}, u32[]{:S(2)}) collective-permute-start(bf16[512,768]{1,0:T(8,128)(2,1)} %get-tuple-element.243), channel_id=1, source_target_pairs={{0,16},{8,24},{16,0},{24,8},{1,17},{9,25},{17,1},{25,9},{2,18},{10... | collective-permute-start | bytes 2359304 | tf_op jit(solution)/shard_map/ppermute | solution.py:282
  711.7 40.9 %collective-permute-start.82 = (bf16[512,768]{1,0:T(8,128)(2,1)}, bf16[512,768]{1,0:T(8,128)(2,1)}, u32[]{:S(2)}, u32[]{:S(2)}) collective-permute-start(bf16[512,768]{1,0:T(8,128)(2,1)} %get-tuple-element.244), channel_id=1, source_target_pairs={{0,24},{8,16},{16,8},{24,0},{1,25},{9,17},{17,9},{25,1},{2,26},{10... | collective-permute-start | bytes 2359304 | tf_op jit(solution)/shard_map/ppermute | solution.py:282
  713.8 43.2 %all-to-all-start.1 = ((bf16[8,128,512]{2,1,0:T(8,128)(2,1)}), bf16[8,128,512]{2,1,0:T(8,128)(2,1)}, u32[]{:S(2)}, u32[]{:S(2)}) async-start(bf16[8,128,512]{2,1,0:T(8,128)(2,1)} %maximum_dynamic-update-slice_fusion), calls=%async_computation.5 | async-start | bytes 2097152 | tf_op jit(solution)/shard_map/all_to_all | solution.py:1080
  718.0 171.3 %reduce-scatter.15.cloned.1.call-start = ((), (), s32[]{:S(2)}) async-start(), calls=%async_computation.18 | async-start | bytes 4718592 | tf_op jit(solution)/shard_map/reduce_scatter | solution.py:1130
  792.1 50.1 %collective-permute-start.85 = (bf16[512,1024]{1,0:T(8,128)(2,1)}, bf16[512,1024]{1,0:T(8,128)(2,1)}, u32[]{:S(2)}, u32[]{:S(2)}) collective-permute-start(bf16[512,1024]{1,0:T(8,128)(2,1)} %get-tuple-element.255), channel_id=1, source_target_pairs={{0,24},{8,16},{16,8},{24,0},{1,25},{9,17},{17,9},{25,1},{2,26},{10... | collective-permute-start | bytes 3145736 | tf_op jit(solution)/shard_map/ppermute | solution.py:282
  798.1 47.9 %all-to-all-start.3 = ((bf16[8,64,768]{2,1,0:T(8,128)(2,1)}), bf16[8,64,768]{2,1,0:T(8,128)(2,1)}, u32[]{:S(2)}, u32[]{:S(2)}) async-start(bf16[8,64,768]{2,1,0:T(8,128)(2,1)} %bitcast.100), calls=%async_computation.8 | async-start | bytes 1572864 | tf_op jit(solution)/shard_map/all_to_all | solution.py:1007
  (237 other events, 3122.2 us)
Sparse Core Ops, SparseCore 0:
  64.2 90.2 all-gather.5
  169.4 114.8 all-gather.11
  286.6 48.2 reduce-scatter.8
  337.0 48.1 reduce-scatter.6
  466.1 44.5 all-gather.7
  542.1 45.0 all-gather.9
  596.0 74.5 reduce-scatter.12
  673.0 44.3 reduce-scatter.16
  719.7 60.1 reduce-scatter.10
  783.4 63.5 reduce-scatter.14

commit v5 on v4

--- a/solution.py
+++ b/solution.py
@@ -878,7 +878,6 @@
     )
     w_ffn = lax.all_gather(w_ffn, LINE, axis=0, tiled=False).reshape(line, -1, columns)
     my_seq = lax.axis_index(SEQ)
-    w_out = after(w_out, block_tokens)
     if part == dp and groups == 1:
         parts = []
         for k in range(part):
@@ -1110,6 +1109,9 @@
             dlate_s, grad_early, grad_w_out = lax.optimization_barrier(
                 (dlate_s, grad_early, grad_w_out)
             )
+            grad_w_out = grad_w_out.reshape(groups, dp, ratio, out_rows, cut)[0]
+            grad_w_out = lax.dynamic_index_in_dim(grad_w_out, my_seq // part, 1, keepdims=False)
+            grad_w_out = lax.all_to_all(grad_w_out, "dp", 0, 0, tiled=True)
             grad_late = dot_first(norm1, jnp.concatenate([*dlate, dlate_s], axis=0))
             rest_at = inner + MH
             grad_late = grad_late + jnp.pad(
@@ -1117,14 +1119,13 @@
                 ((0, 0), (rest_at, grad_late.shape[1] - rest_at - rest_cols)),
             )
             late_cuts = cuts_dp(grad_late.astype(bf16), 0)
-            dlate_s, late_cuts = lax.optimization_barrier((dlate_s, late_cuts))
+            dlate_s, late_cuts, grad_w_out = lax.optimization_barrier(
+                (dlate_s, late_cuts, grad_w_out)
+            )
             grad_late = sum_cuts(late_cuts)
         dlate.append(dlate_s)
         partial = (dot_last(dearly[s], w_early) + dot_last(dlate_s, w_late)).astype(bf16)
         if s == seqs - 1:
-            grad_w_out = grad_w_out.reshape(groups, dp, ratio, out_rows, cut)[0]
-            grad_w_out = lax.dynamic_index_in_dim(grad_w_out, my_seq // part, 1, keepdims=False)
-            grad_w_out = lax.all_to_all(after(grad_w_out, partial), "dp", 0, 0, tiled=True)
             grad_w_out = grad_w_out.transpose(1, 0, 2).reshape(out_rows, width).astype(f32)
             grad_early = to_owners(grad_early)
         grad_norm1.append(lax.psum_scatter(partial, TEAM, scatter_dimension=0, tiled=True))

time: 910 us -> 910 us (level)
  waiting for transfers between devices: 287 us -> 276 us
  starting transfers between devices: 111 us -> 121 us
    all_to_all x2, waiting for transfers between devices: 6.27 us -> 33.3 us  [to_owners(): lax.all_to_all(partial, TEAM, 0, 0, tiled=True).transpose(1, 0, 2)]
    ppermute x68, waiting for transfers between devices: 197 us -> 173 us  [swap(): lax.ppermute(block, axis, [(i, i ^ distance) for i in range(lax.axis_size...]
    all_gather x1, waiting for transfers between devices: 18.9 us -> 0.02 us  [body(): lax.all_gather(after(tokens, w_big), TEAM, axis=1, tiled=True)]
    ppermute x4, starting transfers between devices: 7.62 us -> 17.5 us  [body(): parts.append(lax.ppermute(block, TEAM, route))]
    unnamed x350 -> x352, local copies, waits for them, and re-layouts: 38.5 us -> 37.3 us
where the time goes in v5:
time: 910 us; the launch traced here: 900 us
  waiting for transfers between devices  276 us (30%)
  matrix products  171 us (19%)
  Pallas kernels  138 us (15%)
  starting transfers between devices  121 us (13%)
  local copies, waits for them, and re-layouts  95.9 us (11%)
  other arithmetic  81.2 us (9%)
  between operations  17.3 us (2%)
    ppermute x68, waiting for transfers between devices, swap(): lax.ppermute(block, axis, [(i, i ^ distance) for i in range(lax.axis_size...  173 us
    ppermute x68, starting transfers between devices, swap(): lax.ppermute(block, axis, [(i, i ^ distance) for i in range(lax.axis_size...  64.9 us
    pallas_call x2, Pallas kernels, core_back(): pl.pallas_call(functools.partial(core_back_kernel, heads=heads, span=span...  61.5 us
    dot_general x10, matrix products, dot_last(): lax.dot_general(left, right, (((1,), (1,)), ((), ())), preferred_element_...  59.5 us
    dot_general x8, matrix products, dot(): return jnp.dot(left, right, preferred_element_type=f32, precision=precision)  57.1 us
    dot_general x8, matrix products, dot_first(): lax.dot_general(left, right, (((0,), (0,)), ((), ())), preferred_element_...  53.9 us
    unnamed x352, local copies, waits for them, and re-layouts  37.3 us
    all_to_all x2, waiting for transfers between devices, to_owners(): lax.all_to_all(partial, TEAM, 0, 0, tiled=True).transpose(1, 0, 2)  33.3 us
  transfers between devices with their start and end apart: 101, of which 33 were waited for; matrix products, arithmetic and copies ran while one was open for 34% of the time, Pallas kernels for 15%

profile of v5, /device:TPU:0, one launch (start us, length us, event | category | flops | bytes accessed | tf_op | source)
XLA Modules:
  0.0 900.2 jit_solution(14996767032438178527)
XLA Ops:
  42.9 18.3 %collective-permute-done.3.refs_4_ = bf16[64,1536]{1,0:T(8,128)(2,1)S(1)} collective-permute-done((bf16[64,1536]{1,0:T(8,128)(2,1)}, bf16[64,1536]{1,0:T(8,128)(2,1)S(1)}, u32[]{:S(2)}, u32[]{:S(2)}) %collective-permute-start.3) | collective-permute-done | bytes 196640 | tf_op jit(solution)/shard_map/ppermute | solution.py:815
  76.5 22.3 %collective-permute-done.18.refs_1_ = bf16[512,1536]{1,0:T(8,128)(2,1)} collective-permute-done((bf16[512,1536]{1,0:T(8,128)(2,1)S(1)}, bf16[512,1536]{1,0:T(8,128)(2,1)}, u32[]{:S(2)}, u32[]{:S(2)}) %collective-permute-start.18) | collective-permute-done | bytes 1572896 | tf_op jit(solution)/shard_map/ppermute | solution.py:282
  136.1 13.2 %collective-permute-start.27 = (bf16[128,512]{1,0:T(8,128)(2,1)S(1)}, bf16[128,512]{1,0:T(8,128)(2,1)S(1)}, u32[]{:S(2)}, u32[]{:S(2)}) collective-permute-start(bf16[128,512]{1,0:T(8,128)(2,1)S(1)} %get-tuple-element.399), channel_id=1, source_target_pairs={{0,2},{1,0},{2,6},{3,4},{4,3},{5,1},{6,7},{7,5},{8,10},{9,8},{10,1... | collective-permute-start | bytes 393224 | tf_op jit(solution)/shard_map/ppermute | solution.py:886
  166.4 10.3 %fusion.84.z_ref = f32[2048,768]{1,0:T(8,128)S(1)} fusion(bf16[2048,768]{1,0:T(8,128)(2,1)} %get-tuple-element.170, bf16[2048,2048]{1,0:T(8,128)(2,1)} %bitcast.278, f32[2048]{0:T(1024)S(1)} %get-tuple-element.310, f32[2048]{0:T(1024)S(1)} %add_rsqrt_fusion), kind=kOutput, calls=%fused_computation.275 | convolution fusion | flops 6459228160 | bytes 17842176 | tf_op jit(solution)/shard_map/dot_general | solution.py:63
  176.7 15.8 %fusion.82.x_ref.bc_ref.dt_ref = f32[2048,1024]{1,0:T(8,128)} fusion(bf16[2048,1024]{1,0:T(8,128)(2,1)S(1)} %copy-done.150, bf16[2048,2048]{1,0:T(8,128)(2,1)} %bitcast.279, f32[2048]{0:T(1024)S(1)} %get-tuple-element.310, f32[2048]{0:T(1024)S(1)} %add_rsqrt_fusion), kind=kOutput, calls=%fused_computation.274 | convolution fusion | flops 8606711808 | bytes 20987904 | tf_op jit(solution)/shard_map/dot_general | solution.py:63
  198.6 14.4 %core_fore.2 = (bf16[1024,384]{1,0:T(8,128)(2,1)S(1)}, f32[1024,384]{1,0:T(8,128)S(1)}, f32[1,4,384,256]{3,2,1,0:T(8,128)S(1)}, f32[1,384,256]{2,1,0:T(8,128)}, f32[1,8,128]{2,1,0:T(8,128)}) custom-call(s32[1]{0:T(128)} %bitcast.2.turn_ref, f32[2048,1024]{1,0:T(8,128)} %fusion.82.x_ref.bc_ref.dt_ref, f32[2048,1024]{1,0:T(8,128)} %fusion.82.x_ref.bc_ref.dt_ref, ...), custom_call_target="tpu_custom_call" | custom-call | flops 12999999488 | bytes 8781824 | tf_op jit(solution)/shard_map/core_fore/pallas_call | solution.py:531
  230.1 14.1 %core_fore.3 = (bf16[1024,384]{1,0:T(8,128)(2,1)S(1)}, f32[1024,384]{1,0:T(8,128)S(1)}, f32[1,4,384,256]{3,2,1,0:T(8,128)S(1)}, f32[1,384,256]{2,1,0:T(8,128)}, f32[1,8,128]{2,1,0:T(8,128)}) custom-call(s32[1]{0:T(128)} %bitcast.2.turn_ref, f32[2048,1024]{1,0:T(8,128)} %fusion.82.x_ref.bc_ref.dt_ref, f32[2048,1024]{1,0:T(8,128)} %fusion.82.x_ref.bc_ref.dt_ref, ...), custom_call_target="tpu_custom_call" | custom-call | flops 12999999488 | bytes 8781824 | tf_op jit(solution)/shard_map/core_fore/pallas_call | solution.py:531
  251.7 32.8 %all-gather.12.cloned.1.call-done = bf16[3072,1024]{1,0:T(8,128)(2,1)} async-done(((bf16[768,1024]{1,0:T(8,128)(2,1)}), bf16[3072,1024]{1,0:T(8,128)(2,1)}) %all-gather.12.cloned.1.call-update) | async-done | bytes 6291472 | tf_op jit(solution)/shard_map/all_gather | solution.py:879
  296.9 9.7 %collective-permute-done.40.refs_1_ = bf16[128,2048]{1,0:T(8,128)(2,1)S(1)} collective-permute-done((bf16[128,2048]{1,0:T(8,128)(2,1)S(1)}, bf16[128,2048]{1,0:T(8,128)(2,1)S(1)}, u32[]{:S(2)}, u32[]{:S(2)}) %collective-permute-start.40) | collective-permute-done | bytes 524320 | tf_op jit(solution)/shard_map/ppermute | solution.py:282
  308.0 9.8 %collective-permute-done.41.refs_2_ = bf16[128,2048]{1,0:T(8,128)(2,1)S(1)} collective-permute-done((bf16[128,2048]{1,0:T(8,128)(2,1)S(1)}, bf16[128,2048]{1,0:T(8,128)(2,1)S(1)}, u32[]{:S(2)}, u32[]{:S(2)}) %collective-permute-start.41) | collective-permute-done | bytes 524320 | tf_op jit(solution)/shard_map/ppermute | solution.py:282
  319.4 9.7 %collective-permute-done.33.refs_1_ = bf16[128,2048]{1,0:T(8,128)(2,1)S(1)} collective-permute-done((bf16[128,2048]{1,0:T(8,128)(2,1)S(1)}, bf16[128,2048]{1,0:T(8,128)(2,1)S(1)}, u32[]{:S(2)}, u32[]{:S(2)}) %collective-permute-start.33) | collective-permute-done | bytes 524320 | tf_op jit(solution)/shard_map/ppermute | solution.py:282
  329.1 11.3 %collective-permute-done.34.refs_2_ = bf16[128,2048]{1,0:T(8,128)(2,1)S(1)} collective-permute-done((bf16[128,2048]{1,0:T(8,128)(2,1)S(1)}, bf16[128,2048]{1,0:T(8,128)(2,1)S(1)}, u32[]{:S(2)}, u32[]{:S(2)}) %collective-permute-start.34) | collective-permute-done | bytes 524320 | tf_op jit(solution)/shard_map/ppermute | solution.py:282
  354.4 11.3 %collective-permute-done.47.refs_1_ = bf16[128,2048]{1,0:T(8,128)(2,1)S(1)} collective-permute-done((bf16[128,2048]{1,0:T(8,128)(2,1)S(1)}, bf16[128,2048]{1,0:T(8,128)(2,1)S(1)}, u32[]{:S(2)}, u32[]{:S(2)}) %collective-permute-start.47) | collective-permute-done | bytes 524320 | tf_op jit(solution)/shard_map/ppermute | solution.py:282
  366.2 11.1 %collective-permute-done.49.refs_3_ = bf16[128,2048]{1,0:T(8,128)(2,1)} collective-permute-done((bf16[128,2048]{1,0:T(8,128)(2,1)S(1)}, bf16[128,2048]{1,0:T(8,128)(2,1)}, u32[]{:S(2)}, u32[]{:S(2)}) %collective-permute-start.49) | collective-permute-done | bytes 524320 | tf_op jit(solution)/shard_map/ppermute | solution.py:282
  387.7 7.8 fusion.99
  422.2 8.6 collective-permute-done.58
  432.9 10.2 %collective-permute-done.59 = bf16[128,2048]{1,0:T(8,128)(2,1)S(1)} collective-permute-done((bf16[128,2048]{1,0:T(8,128)(2,1)S(1)}, bf16[128,2048]{1,0:T(8,128)(2,1)S(1)}, u32[]{:S(2)}, u32[]{:S(2)}) %collective-permute-start.59) | collective-permute-done | bytes 524320 | tf_op jit(solution)/shard_map/ppermute | solution.py:282
  453.3 11.2 %collective-permute-done.56.refs_2_ = bf16[128,2048]{1,0:T(8,128)(2,1)S(1)} collective-permute-done((bf16[128,2048]{1,0:T(8,128)(2,1)S(1)}, bf16[128,2048]{1,0:T(8,128)(2,1)S(1)}, u32[]{:S(2)}, u32[]{:S(2)}) %collective-permute-start.56) | collective-permute-done | bytes 524320 | tf_op jit(solution)/shard_map/ppermute | solution.py:282
  476.0 7.8 fusion.100
  490.0 7.6 convolution_convert_fusion.4
  527.1 11.7 %collective-permute-done.69 = bf16[128,2048]{1,0:T(8,128)(2,1)S(1)} collective-permute-done((bf16[128,2048]{1,0:T(8,128)(2,1)S(1)}, bf16[128,2048]{1,0:T(8,128)(2,1)S(1)}, u32[]{:S(2)}, u32[]{:S(2)}) %collective-permute-start.69) | collective-permute-done | bytes 524320 | tf_op jit(solution)/shard_map/ppermute | solution.py:282
  546.3 31.0 %core_back.2 = (bf16[1024,1024]{1,0:T(8,128)(2,1)S(1)}, f32[8,896]{1,0:T(8,128)S(1)}, f32[8,128]{1,0:T(8,128)S(1)}, f32[1,384,256]{2,1,0:T(8,128)}, f32[1,8,896]{2,1,0:T(8,128)}) custom-call(s32[1]{0:T(128)} %bitcast.2.turn_ref, f32[2048,1024]{1,0:T(8,128)} %fusion.82.x_ref.bc_ref.dt_ref, f32[2048,1024]{1,0:T(8,128)} %fusion.82.x_ref.bc_ref.dt_ref, ...), custom_call_target="tpu_custom_call" | custom-call | flops 30000001024 | bytes 9961472 | tf_op jit(solution)/shard_map/core_back/pallas_call | solution.py:702
  577.4 7.7 fusion.40
  585.1 8.5 add_convert_fusion.3
  622.5 8.4 add_convert_fusion.2
  681.9 7.7 convolution_convert_fusion.6
  695.3 7.6 fusion.32
  718.4 30.5 %core_back.3 = (bf16[1024,1024]{1,0:T(8,128)(2,1)S(1)}, f32[8,896]{1,0:T(8,128)S(1)}, f32[8,128]{1,0:T(8,128)S(1)}, f32[1,384,256]{2,1,0:T(8,128)}, f32[1,8,896]{2,1,0:T(8,128)}) custom-call(s32[1]{0:T(128)} %bitcast.2.turn_ref, f32[2048,1024]{1,0:T(8,128)} %fusion.82.x_ref.bc_ref.dt_ref, f32[2048,1024]{1,0:T(8,128)} %fusion.82.x_ref.bc_ref.dt_ref, ...), custom_call_target="tpu_custom_call" | custom-call | flops 30000001024 | bytes 9961472 | tf_op jit(solution)/shard_map/core_back/pallas_call | solution.py:702
  763.6 13.7 %add_convert_fusion.1 = bf16[2048,1024]{1,0:T(8,128)(2,1)S(1)} fusion(f32[2048,11]{1,0:T(8,128)S(1)} %copy-done.88, bf16[1024,1024]{1,0:T(8,128)(2,1)} %copy-done.45, bf16[1024,1024]{1,0:T(8,128)(2,1)S(1)} %copy-done.44, bf16[2048,2048]{1,0:T(8,128)(2,1)} %bitcast.280, f32[2048]{0:T(1024)S(1)} %copy-done.129, f32[2048]{0:T(1024)S(1)} %copy-done.136), kind=kOutput, calls=%fused_computation.6 | convolution fusion | flops 8619294720 | bytes 16883712 | tf_op jit(solution)/shard_map/dot_general | solution.py:67
  780.0 9.6 %add_convert_fusion = bf16[1024,2048]{1,0:T(8,128)(2,1)} fusion(f32[1024,2048]{1,0:T(8,128)} %fusion.32, bf16[1024,1024]{1,0:T(8,128)(2,1)S(1)} %copy-done.46, bf16[2048,1024]{1,0:T(8,128)(2,1)} %get-tuple-element.171), kind=kOutput, calls=%fused_computation.5 | convolution fusion | flops 4299161600 | bytes 18874368 | tf_op jit(solution)/shard_map/dot_general | solution.py:73
  798.9 27.0 %all-to-all-done.3 = bf16[8,64,768]{2,1,0:T(8,128)(2,1)} async-done(((bf16[8,64,768]{2,1,0:T(8,128)(2,1)}), bf16[8,64,768]{2,1,0:T(8,128)(2,1)}, u32[]{:S(2)}, u32[]{:S(2)}) %all-to-all-start.3) | async-done | bytes 786464 | tf_op jit(solution)/shard_map/all_to_all | solution.py:1006
  828.3 15.4 %collective-permute-done.84 = bf16[512,1024]{1,0:T(8,128)(2,1)} collective-permute-done((bf16[512,1024]{1,0:T(8,128)(2,1)}, bf16[512,1024]{1,0:T(8,128)(2,1)}, u32[]{:S(2)}, u32[]{:S(2)}) %collective-permute-start.84) | collective-permute-done | bytes 1048608 | tf_op jit(solution)/shard_map/ppermute | solution.py:282
  (755 shorter events, 447.0 us)
Async XLA Ops:
  7.2 152.8 %all-gather.6.cloned.1.call-start = ((), (), s32[]{:S(2)}) async-start(), calls=%async_computation.11 | async-start | bytes 9437184 | tf_op jit(solution)/shard_map/all_gather | solution.py:847
  64.1 220.4 %all-gather.12.cloned.1.call-start = ((), (), s32[]{:S(2)}) async-start(), calls=%async_computation.20 | async-start | bytes 7864320 | tf_op jit(solution)/shard_map/all_gather | solution.py:879
  64.1 34.7 %collective-permute-start.18 = (bf16[512,1536]{1,0:T(8,128)(2,1)S(1)}, bf16[512,1536]{1,0:T(8,128)(2,1)}, u32[]{:S(2)}, u32[]{:S(2)}) collective-permute-start(bf16[512,1536]{1,0:T(8,128)(2,1)S(1)} %bitcast.252), channel_id=1, source_target_pairs={{0,8},{8,0},{16,24},{24,16},{1,9},{9,1},{17,25},{25,17},{2,10},{10... | collective-permute-start | bytes 4718600 | tf_op jit(solution)/shard_map/ppermute | solution.py:282
  65.7 36.1 %collective-permute-start.20 = (bf16[512,1536]{1,0:T(8,128)(2,1)S(1)}, bf16[512,1536]{1,0:T(8,128)(2,1)}, u32[]{:S(2)}, u32[]{:S(2)}) collective-permute-start(bf16[512,1536]{1,0:T(8,128)(2,1)S(1)} %bitcast.253), channel_id=1, source_target_pairs={{0,16},{8,24},{16,0},{24,8},{1,17},{9,25},{17,1},{25,9},{2,18},{10... | collective-permute-start | bytes 4718600 | tf_op jit(solution)/shard_map/ppermute | solution.py:282
  71.7 54.3 %collective-permute-start.17 = (bf16[512,640]{1,0:T(8,128)(2,1)}, bf16[512,640]{1,0:T(8,128)(2,1)S(1)}, u32[]{:S(2)}, u32[]{:S(2)}) collective-permute-start(bf16[512,640]{1,0:T(8,128)(2,1)} %slice.337), channel_id=1, source_target_pairs={{0,1},{1,0},{2,3},{3,2},{4,5},{5,4},{6,7},{7,6},{8,9},{9,8},{10,11... | collective-permute-start | bytes 1966088 | tf_op jit(solution)/shard_map/ppermute | solution.py:282
  166.3 181.4 %reduce-scatter.9.cloned.1.call-start = ((), (), s32[]{:S(2)}) async-start(), calls=%async_computation.13 | async-start | bytes 4718592 | tf_op jit(solution)/shard_map/reduce_scatter | solution.py:955
  284.5 124.2 %reduce-scatter.7.cloned.1.call-start = ((), (), s32[]{:S(2)}) async-start(), calls=%async_computation.12 | async-start | bytes 4718592 | tf_op jit(solution)/shard_map/reduce_scatter | solution.py:955
  290.1 220.7 %all-gather.8.cloned.1.call-start = ((), (), s32[]{:S(2)}) async-start(), calls=%async_computation.14 | async-start | bytes 4718592 | tf_op jit(solution)/shard_map/all_gather | solution.py:972
  306.6 33.9 %collective-permute-start.34 = (bf16[128,2048]{1,0:T(8,128)(2,1)S(1)}, bf16[128,2048]{1,0:T(8,128)(2,1)S(1)}, u32[]{:S(2)}, u32[]{:S(2)}) collective-permute-start(bf16[128,2048]{1,0:T(8,128)(2,1)S(1)} %multiply_convert_fusion.13.refs_0_), channel_id=1, source_target_pairs={{0,16},{8,24},{16,0},{24,8},{1,17},{9,25},{17,1},{25,9},{2,18},{10... | collective-permute-start | bytes 1572872 | tf_op jit(solution)/shard_map/ppermute | solution.py:282
  419.6 33.8 %collective-permute-start.55 = (bf16[128,2048]{1,0:T(8,128)(2,1)S(1)}, bf16[128,2048]{1,0:T(8,128)(2,1)S(1)}, u32[]{:S(2)}, u32[]{:S(2)}) collective-permute-start(bf16[128,2048]{1,0:T(8,128)(2,1)S(1)} %multiply_convert_fusion.10.refs_0_), channel_id=1, source_target_pairs={{0,8},{8,0},{16,24},{24,16},{1,9},{9,1},{17,25},{25,17},{2,10},{10... | collective-permute-start | bytes 1572872 | tf_op jit(solution)/shard_map/ppermute | solution.py:282
  420.6 43.9 %collective-permute-start.56 = (bf16[128,2048]{1,0:T(8,128)(2,1)S(1)}, bf16[128,2048]{1,0:T(8,128)(2,1)S(1)}, u32[]{:S(2)}, u32[]{:S(2)}) collective-permute-start(bf16[128,2048]{1,0:T(8,128)(2,1)S(1)} %multiply_convert_fusion.10.refs_0_), channel_id=1, source_target_pairs={{0,16},{8,24},{16,0},{24,8},{1,17},{9,25},{17,1},{25,9},{2,18},{10... | collective-permute-start | bytes 1572872 | tf_op jit(solution)/shard_map/ppermute | solution.py:282
  466.2 187.9 %all-gather.10.cloned.1.call-start = ((), (), s32[]{:S(2)}) async-start(), calls=%async_computation.15 | async-start | bytes 4718592 | tf_op jit(solution)/shard_map/all_gather | solution.py:1045
  542.3 149.1 %reduce-scatter.13.cloned.1.call-start = ((), (), s32[]{:S(2)}) async-start(), calls=%async_computation.17 | async-start | bytes 5242880 | tf_op jit(solution)/shard_map/reduce_scatter | solution.py:1107
  596.1 266.6 %reduce-scatter.17.cloned.1.call-start = ((), (), s32[]{:S(2)}) async-start(), calls=%async_computation.19 | async-start | bytes 2621440 | tf_op jit(solution)/shard_map/reduce_scatter | solution.py:1137
  598.9 36.9 %collective-permute-start.71 = (bf16[128,2048]{1,0:T(8,128)(2,1)}, bf16[128,2048]{1,0:T(8,128)(2,1)}, u32[]{:S(2)}, u32[]{:S(2)}) collective-permute-start(bf16[128,2048]{1,0:T(8,128)(2,1)} %get-tuple-element.338), channel_id=1, source_target_pairs={{0,8},{8,0},{16,24},{24,16},{1,9},{9,1},{17,25},{25,17},{2,10},{10... | collective-permute-start | bytes 1572872 | tf_op jit(solution)/shard_map/ppermute | solution.py:282
  600.1 41.1 %collective-permute-start.72 = (bf16[128,2048]{1,0:T(8,128)(2,1)}, bf16[128,2048]{1,0:T(8,128)(2,1)}, u32[]{:S(2)}, u32[]{:S(2)}) collective-permute-start(bf16[128,2048]{1,0:T(8,128)(2,1)} %get-tuple-element.340), channel_id=1, source_target_pairs={{0,16},{8,24},{16,0},{24,8},{1,17},{9,25},{17,1},{25,9},{2,18},{10... | collective-permute-start | bytes 1572872 | tf_op jit(solution)/shard_map/ppermute | solution.py:282
  600.9 40.4 %collective-permute-start.73 = (bf16[128,2048]{1,0:T(8,128)(2,1)}, bf16[128,2048]{1,0:T(8,128)(2,1)}, u32[]{:S(2)}, u32[]{:S(2)}) collective-permute-start(bf16[128,2048]{1,0:T(8,128)(2,1)} %get-tuple-element.339), channel_id=1, source_target_pairs={{0,24},{8,16},{16,8},{24,0},{1,25},{9,17},{17,9},{25,1},{2,26},{10... | collective-permute-start | bytes 1572872 | tf_op jit(solution)/shard_map/ppermute | solution.py:282
  603.7 37.6 %collective-permute-start.74 = (bf16[128,2048]{1,0:T(8,128)(2,1)}, bf16[128,2048]{1,0:T(8,128)(2,1)}, u32[]{:S(2)}, u32[]{:S(2)}) collective-permute-start(bf16[128,2048]{1,0:T(8,128)(2,1)} %get-tuple-element.341), channel_id=1, source_target_pairs={{0,8},{8,0},{16,24},{24,16},{1,9},{9,1},{17,25},{25,17},{2,10},{10... | collective-permute-start | bytes 1572872 | tf_op jit(solution)/shard_map/ppermute | solution.py:282
  604.8 36.5 %collective-permute-start.75 = (bf16[128,2048]{1,0:T(8,128)(2,1)}, bf16[128,2048]{1,0:T(8,128)(2,1)}, u32[]{:S(2)}, u32[]{:S(2)}) collective-permute-start(bf16[128,2048]{1,0:T(8,128)(2,1)} %get-tuple-element.343), channel_id=1, source_target_pairs={{0,16},{8,24},{16,0},{24,8},{1,17},{9,25},{17,1},{25,9},{2,18},{10... | collective-permute-start | bytes 1572872 | tf_op jit(solution)/shard_map/ppermute | solution.py:282
  654.1 234.4 %reduce-scatter.11.cloned.1.call-start = ((), (), s32[]{:S(2)}) async-start(), calls=%async_computation.16 | async-start | bytes 4718592 | tf_op jit(solution)/shard_map/reduce_scatter | solution.py:1131
  666.2 36.6 %collective-permute-start.77 = (bf16[512,512]{1,0:T(8,128)(2,1)}, bf16[512,512]{1,0:T(8,128)(2,1)}, u32[]{:S(2)}, u32[]{:S(2)}) collective-permute-start(bf16[512,512]{1,0:T(8,128)(2,1)} %get-tuple-element.335), channel_id=1, source_target_pairs={{0,8},{8,0},{16,24},{24,16},{1,9},{9,1},{17,25},{25,17},{2,10},{10... | collective-permute-start | bytes 1572872 | tf_op jit(solution)/shard_map/ppermute | solution.py:282
  667.7 35.2 %collective-permute-start.78 = (bf16[512,512]{1,0:T(8,128)(2,1)}, bf16[512,512]{1,0:T(8,128)(2,1)}, u32[]{:S(2)}, u32[]{:S(2)}) collective-permute-start(bf16[512,512]{1,0:T(8,128)(2,1)} %get-tuple-element.337), channel_id=1, source_target_pairs={{0,16},{8,24},{16,0},{24,8},{1,17},{9,25},{17,1},{25,9},{2,18},{10... | collective-permute-start | bytes 1572872 | tf_op jit(solution)/shard_map/ppermute | solution.py:282
  668.5 34.4 %collective-permute-start.79 = (bf16[512,512]{1,0:T(8,128)(2,1)}, bf16[512,512]{1,0:T(8,128)(2,1)}, u32[]{:S(2)}, u32[]{:S(2)}) collective-permute-start(bf16[512,512]{1,0:T(8,128)(2,1)} %get-tuple-element.336), channel_id=1, source_target_pairs={{0,24},{8,16},{16,8},{24,0},{1,25},{9,17},{17,9},{25,1},{2,26},{10... | collective-permute-start | bytes 1572872 | tf_op jit(solution)/shard_map/ppermute | solution.py:282
  710.6 42.4 %collective-permute-start.80 = (bf16[512,768]{1,0:T(8,128)(2,1)}, bf16[512,768]{1,0:T(8,128)(2,1)}, u32[]{:S(2)}, u32[]{:S(2)}) collective-permute-start(bf16[512,768]{1,0:T(8,128)(2,1)} %get-tuple-element.240), channel_id=1, source_target_pairs={{0,8},{8,0},{16,24},{24,16},{1,9},{9,1},{17,25},{25,17},{2,10},{10... | collective-permute-start | bytes 2359304 | tf_op jit(solution)/shard_map/ppermute | solution.py:282
  711.1 41.9 %collective-permute-start.81 = (bf16[512,768]{1,0:T(8,128)(2,1)}, bf16[512,768]{1,0:T(8,128)(2,1)}, u32[]{:S(2)}, u32[]{:S(2)}) collective-permute-start(bf16[512,768]{1,0:T(8,128)(2,1)} %get-tuple-element.241), channel_id=1, source_target_pairs={{0,16},{8,24},{16,0},{24,8},{1,17},{9,25},{17,1},{25,9},{2,18},{10... | collective-permute-start | bytes 2359304 | tf_op jit(solution)/shard_map/ppermute | solution.py:282
  711.8 41.2 %collective-permute-start.82 = (bf16[512,768]{1,0:T(8,128)(2,1)}, bf16[512,768]{1,0:T(8,128)(2,1)}, u32[]{:S(2)}, u32[]{:S(2)}) collective-permute-start(bf16[512,768]{1,0:T(8,128)(2,1)} %get-tuple-element.242), channel_id=1, source_target_pairs={{0,24},{8,16},{16,8},{24,0},{1,25},{9,17},{17,9},{25,1},{2,26},{10... | collective-permute-start | bytes 2359304 | tf_op jit(solution)/shard_map/ppermute | solution.py:282
  714.1 43.3 %all-to-all-start.1 = ((bf16[8,128,512]{2,1,0:T(8,128)(2,1)}), bf16[8,128,512]{2,1,0:T(8,128)(2,1)}, u32[]{:S(2)}, u32[]{:S(2)}) async-start(bf16[8,128,512]{2,1,0:T(8,128)(2,1)} %maximum_dynamic-update-slice_fusion), calls=%async_computation.5 | async-start | bytes 2097152 | tf_op jit(solution)/shard_map/all_to_all | solution.py:1079
  763.5 125.0 %reduce-scatter.15.cloned.1.call-start = ((), (), s32[]{:S(2)}) async-start(), calls=%async_computation.18 | async-start | bytes 4718592 | tf_op jit(solution)/shard_map/reduce_scatter | solution.py:1131
  789.6 36.3 %all-to-all-start.3 = ((bf16[8,64,768]{2,1,0:T(8,128)(2,1)}), bf16[8,64,768]{2,1,0:T(8,128)(2,1)}, u32[]{:S(2)}, u32[]{:S(2)}) async-start(bf16[8,64,768]{2,1,0:T(8,128)(2,1)} %bitcast.100), calls=%async_computation.8 | async-start | bytes 1572864 | tf_op jit(solution)/shard_map/all_to_all | solution.py:1006
  793.9 34.5 %collective-permute-start.83 = (bf16[512,1024]{1,0:T(8,128)(2,1)}, bf16[512,1024]{1,0:T(8,128)(2,1)}, u32[]{:S(2)}, u32[]{:S(2)}) collective-permute-start(bf16[512,1024]{1,0:T(8,128)(2,1)} %get-tuple-element.252), channel_id=1, source_target_pairs={{0,8},{8,0},{16,24},{24,16},{1,9},{9,1},{17,25},{25,17},{2,10},{10... | collective-permute-start | bytes 3145736 | tf_op jit(solution)/shard_map/ppermute | solution.py:282
  795.9 47.9 %collective-permute-start.84 = (bf16[512,1024]{1,0:T(8,128)(2,1)}, bf16[512,1024]{1,0:T(8,128)(2,1)}, u32[]{:S(2)}, u32[]{:S(2)}) collective-permute-start(bf16[512,1024]{1,0:T(8,128)(2,1)} %get-tuple-element.253), channel_id=1, source_target_pairs={{0,16},{8,24},{16,0},{24,8},{1,17},{9,25},{17,1},{25,9},{2,18},{10... | collective-permute-start | bytes 3145736 | tf_op jit(solution)/shard_map/ppermute | solution.py:282
  797.3 46.5 %collective-permute-start.85 = (bf16[512,1024]{1,0:T(8,128)(2,1)}, bf16[512,1024]{1,0:T(8,128)(2,1)}, u32[]{:S(2)}, u32[]{:S(2)}) collective-permute-start(bf16[512,1024]{1,0:T(8,128)(2,1)} %get-tuple-element.254), channel_id=1, source_target_pairs={{0,24},{8,16},{16,8},{24,0},{1,25},{9,17},{17,9},{25,1},{2,26},{10... | collective-permute-start | bytes 3145736 | tf_op jit(solution)/shard_map/ppermute | solution.py:282
  (238 other events, 3099.4 us)
Sparse Core Ops, SparseCore 0:
  64.2 92.9 all-gather.5
  166.5 117.9 all-gather.11
  286.8 48.2 reduce-scatter.8
  337.2 48.1 reduce-scatter.6
  466.3 44.5 all-gather.7
  542.4 44.9 all-gather.9
  596.3 74.4 reduce-scatter.12
  673.2 44.3 reduce-scatter.16
  719.9 60.4 reduce-scatter.10
  789.7 62.0 reduce-scatter.14
